TPU v7x, 32 devices: a whole 2x2x4 slice. The times are simulated.
32 devices in a mesh: groups: 2 (over y), dp: 4 (over z), tensor: 4 (over x, core).
Axes of the slice: x: 2, y: 2, z: 4, core: 2. Of those that a mesh axis runs over, the one named last changes fastest.
Arguments:
- activations: bfloat16 [16, 128, 28672], P(('groups', 'dp'), None, 'tensor'), parts along dimension 0, may hold values from -6 to 6
- out_grads: bfloat16 [16, 128, 8192], P(('groups', 'dp'), None, 'tensor'), parts along dimension 0, may hold values from -6 to 6
- proj_in: bfloat16 [28672, 64], P('tensor'), may hold values from -0.03125 to 0.03125
- proj_out: bfloat16 [8192, 64], P('tensor'), may hold values from -0.0625 to 0.0625
- lengths: int32 [16], P(('groups', 'dp')), parts along dimension 0, may hold values from 64 to 128, as said below
- query_ids: int32 [128], P('groups'), parts along dimension 0, may hold values from 0 to 7
Outputs:
- scores: float32 [64, 16], P(None, ('groups', 'dp')), parts along dimension 1
There are 2 independent parts, one for each index of `groups`. A program takes and returns all parts, laid end to end along the dimension named above; an argument that names none is the same for every part. Nothing has to cross between parts.
Inputs may be any that keep to these rules, and one draw needn't show every extreme that they name: `lengths`: some example has exactly 128 live tokens.
All inputs are finite; a program needn't handle non-finite values.
Results may differ from a plain program's by a relative error of at most 0.0003.
Values sent between devices are 32-bit elements; how exact they have to be, the bound alone decides.
No kernel may reach another device: no remote copies, remote signals or barrier semaphores. Data moves between devices by JAX's collectives and lax.ppermute only.
A program may use at most 64 MiB of HBM per device.

v0:
```python
import jax
import jax.numpy as jnp
from jax import lax
from jax.sharding import PartitionSpec as P


def damped_inverse(cov, sketch_rank):
    eye_mat = jnp.eye(sketch_rank, dtype=jnp.float32)
    damped = cov + 0.1 * jnp.trace(cov) / sketch_rank * eye_mat
    factor = jnp.linalg.cholesky(damped)
    return jax.scipy.linalg.cho_solve((factor, True), eye_mat)


def per_device(activations, out_grads, proj_in, proj_out, lengths, query_ids):
    count_ex = activations.shape[0]
    seq_len = activations.shape[1]
    sketch_rank = proj_in.shape[1]
    num_queries = query_ids.shape[0]
    high = lax.Precision.HIGHEST
    in_part = jnp.einsum("elf,fr->elr", activations, proj_in, preferred_element_type=jnp.float32)
    out_part = jnp.einsum("elf,fr->elr", out_grads, proj_out, preferred_element_type=jnp.float32)
    joined = jnp.concatenate([out_part, in_part], axis=2)
    summed = lax.psum(joined, "tensor")
    live_mask = jnp.arange(seq_len, dtype=jnp.int32)[None, :] < lengths[:, None]
    summed = jnp.where(live_mask[:, :, None], summed, 0.0)
    out_sk = summed[:, :, :sketch_rank]
    in_sk = summed[:, :, sketch_rank:]
    cov_out_loc = jnp.einsum("elr,els->rs", out_sk, out_sk, precision=high)
    cov_in_loc = jnp.einsum("elr,els->rs", in_sk, in_sk, precision=high)
    tokens_loc = jnp.sum(lengths).astype(jnp.float32)
    cov_out, cov_in, count = lax.psum((cov_out_loc, cov_in_loc, tokens_loc), "dp")
    sketch = jnp.einsum("ela,elb->eab", out_sk, in_sk, precision=high)
    inv_out = damped_inverse(cov_out / count, sketch_rank)
    inv_in = damped_inverse(cov_in / count, sketch_rank)
    flat_sketch = sketch.reshape(count_ex, sketch_rank * sketch_rank)
    every_sketch = lax.all_gather(flat_sketch, "dp", axis=0, tiled=True)
    query_flat = every_sketch[query_ids]
    query = query_flat.reshape(num_queries, sketch_rank, sketch_rank)
    conditioned = jnp.einsum("ab,jbc,cd->jad", inv_out, query, inv_in, precision=high)
    scores = jnp.einsum("jab,eab->je", conditioned, sketch, precision=high)
    return scores / (sketch_rank * seq_len)


def solution(mesh):
    placed = (
        P(("groups", "dp"), None, "tensor"),
        P(("groups", "dp"), None, "tensor"),
        P("tensor", None),
        P("tensor", None),
        P(("groups", "dp")),
        P("groups"),
    )
    return jax.shard_map(
        per_device, mesh=mesh, in_specs=placed, out_specs=P(None, ("groups", "dp")), check_vma=False
    )
```

profile of v0, /device:TPU:0, one launch (start us, length us, event | category | flops | bytes accessed | tf_op | source)
XLA Modules:
  0.0 133.8 jit_solution(584143998656220383)
XLA Ops:
  6.5 0.0 copy-start
  6.5 0.0 copy-start.1
  6.5 0.0 copy-start.2
  6.5 0.0 copy-start.3
  6.5 0.0 all-reduce.3.cloned.1.call-start
  6.6 3.6 %fusion.1 = f32[2,128,64]{1,2,0:T(8,128)S(1)} fusion(bf16[2,128,7168]{2,1,0:T(8,128)(2,1)} %param.9, bf16[7168,64]{0,1:T(8,128)(2,1)} %param.11), kind=kOutput, calls=%fused_computation.7 | convolution fusion | flops 234881024 | bytes 4653056 | tf_op jit(solution)/shard_map/elf,fr->elr/dot_general | solution.py:20
  10.2 0.0 copy-done
  10.2 0.0 copy-done.1
  10.2 0.4 fusion.3
  10.7 0.7 pad_maximum_fusion
  11.3 0.0 all-reduce.3.cloned.1.call-update
  11.4 0.0 copy-done.2
  11.4 0.1 iota_compare_fusion.5
  11.4 0.6 reduce_sum.25
  12.7 0.0 copy-done.3
  12.8 32.8 %all-reduce.3.cloned.1.call-done = f32[2,128,128]{1,2,0:T(8,128)} async-done(((f32[2,128,128]{1,2,0:T(8,128)}), f32[2,128,128]{1,2,0:T(8,128)}) %all-reduce.3.cloned.1.call-update) | async-done | bytes 131088 | tf_op jit(solution)/shard_map/psum | solution.py:23
  45.6 0.9 broadcast_select_fusion
  46.5 0.2 convolution_bitcast_fusion.1
  46.7 0.2 convolution_bitcast_fusion.3
  46.9 0.2 fusion.7
  47.2 20.4 %all-reduce = (f32[64,64]{0,1:T(8,128)S(1)}, f32[]{:T(128)}, f32[64,64]{0,1:T(8,128)S(1)}) all-reduce(f32[64,64]{0,1:T(8,128)S(1)} %convolution_bitcast_fusion.3, f32[]{:T(128)S(6)} %convert_element_type.9, f32[64,64]{0,1:T(8,128)S(1)} %convolution_bitcast_fusion.1), channel_id=1, replica_groups=mesh['groups'=2,'dp'=4,'tensor'=4] {'dp'}, use_global_device_ids=true, to_apply=%region_1.2 | all-reduce | flops 8193 | bytes 65544 | tf_op jit(solution)/shard_map/psum | solution.py:31
  67.6 1.3 select_reduce_fusion.2
  68.9 1.2 select_reduce_fusion.3
  71.4 0.7 select_add_fusion
  72.1 0.1 copy.15
  72.2 5.8 %cholesky.55 = f32[64,64]{1,0:T(8,128)S(1)} custom-call(f32[64,64]{1,0:T(8,128)S(1)} %fusion.19), custom_call_target="Cholesky" | custom-call | tf_op jit(solution)/shard_map/jit(cholesky)/cholesky | solution.py:10
  78.1 0.6 compare_reduce_fusion
  78.7 0.7 fusion.16
  79.4 4.9 %custom-call.9 = f32[1,64,64]{1,2,0:T(8,128)S(1)} custom-call(f32[1,64,64]{2,1,0:T(8,128)S(1)} %fusion.16), custom_call_target="InvertDiagBlocksLowerTriangular" | custom-call | tf_op jit(solution)/shard_map/jit(_cho_solve)/triangular_solve | solution.py:11
  84.3 0.3 fusion.11
  84.5 0.2 convolution_bitcast_fusion
  84.7 0.1 copy.13
  84.8 5.8 %cholesky.44 = f32[64,64]{1,0:T(8,128)S(1)} custom-call(f32[64,64]{1,0:T(8,128)S(1)} %fusion.22), custom_call_target="Cholesky" | custom-call | tf_op jit(solution)/shard_map/jit(cholesky)/cholesky | solution.py:10
  90.7 0.6 compare_reduce_fusion.1
  91.3 0.7 fusion.15
  92.0 4.9 %custom-call.8 = f32[1,64,64]{1,2,0:T(8,128)S(1)} custom-call(f32[1,64,64]{2,1,0:T(8,128)S(1)} %fusion.15), custom_call_target="InvertDiagBlocksLowerTriangular" | custom-call | tf_op jit(solution)/shard_map/jit(_cho_solve)/triangular_solve | solution.py:11
  96.9 0.3 fusion.13
  97.1 0.2 convolution_bitcast_fusion.2
  97.3 0.1 reshape.48
  97.4 13.5 %all-gather = f32[4,2,4096]{2,1,0:T(2,128)S(1)} all-gather(f32[1,2,4096]{2,1,0:T(2,128)S(1)} %reshape.48), channel_id=1, replica_groups=mesh['groups'=2,'dp'=4,'tensor'=4] {'dp'}, dimensions={0}, use_global_device_ids=true | all-gather | bytes 163840 | tf_op jit(solution)/shard_map/all_gather | solution.py:36
  111.0 0.1 reshape.49
  111.0 1.9 %gather_fusion = f32[64,4096]{1,0:T(8,128)} fusion(f32[8,4096]{1,0:T(8,128)S(1)} %reshape.49, s32[1024]{0:T(1024)S(1)} %pad_clamp_fusion), kind=kCustom, calls=%fused_computation | custom fusion | bytes 2097408 | tf_op jit(solution)/shard_map/gather | solution.py:37
  112.9 2.0 %reshape.38 = f32[64,64,64]{2,1,0:T(8,128)S(1)} reshape(f32[64,4096]{1,0:T(8,128)} %gather_fusion) | data formatting | bytes 2097152 | tf_op jit(solution)/shard_map/reshape | solution.py:38
  114.9 4.8 %fusion.23 = f32[64,64,64]{2,1,0:T(8,128)} fusion(f32[64,64,64]{2,1,0:T(8,128)S(1)} %reshape.38, f32[64,64,1]{1,0,2:T(8,128)S(1)} %convolution_bitcast_fusion.2), kind=kOutput, calls=%fused_computation.51 | convolution fusion | flops 201326592 | bytes 2113536 | tf_op jit(solution)/shard_map/ab,jbc,cd->jad/dot_general | solution.py:39
  119.7 3.1 %copy.19 = f32[64,64,64]{1,0,2:T(8,128)S(1)} copy(f32[64,64,64]{2,1,0:T(8,128)} %fusion.23) | data formatting | bytes 2097152 | tf_op jit(solution)/shard_map/ab,jbc,cd->jad/dot_general | solution.py:39
  122.8 1.8 %fusion.24 = f32[64,64,64]{2,0,1:T(8,128)S(1)} fusion(f32[64,64,64]{1,0,2:T(8,128)S(1)} %copy.19, f32[64,64,1]{1,0,2:T(8,128)S(1)} %convolution_bitcast_fusion), kind=kOutput, calls=%fused_computation.52 | convolution fusion | flops 201326592 | bytes 2113536 | tf_op jit(solution)/shard_map/ab,jbc,cd->jad/dot_general | solution.py:39
  124.7 2.3 %fusion = f32[64,2]{0,1:T(2,128)} fusion(f32[64,64,64]{2,0,1:T(8,128)S(1)} %fusion.24, f32[2,64,64]{2,1,0:T(8,128)S(1)} %fusion.7), kind=kOutput, calls=%fused_computation.6 | convolution fusion | flops 6291584 | bytes 1081856 | tf_op jit(solution)/shard_map/jab,eab->je/dot_general | solution.py:40
  (6 shorter events, 0.1 us)
Async XLA Ops:
  6.5 3.7 %copy-start = (bf16[2,128,2048]{2,1,0:T(8,128)(2,1)S(1)}, bf16[2,128,2048]{2,1,0:T(8,128)(2,1)}, u32[]{:S(2)}) copy-start(bf16[2,128,2048]{2,1,0:T(8,128)(2,1)} %param.10) | copy-start | bytes 3145732
  6.5 3.7 %copy-start.1 = (bf16[2048,64]{0,1:T(8,128)(2,1)S(1)}, bf16[2048,64]{0,1:T(8,128)(2,1)}, u32[]{:S(2)}) copy-start(bf16[2048,64]{0,1:T(8,128)(2,1)} %param.12) | copy-start | bytes 786436
  6.5 4.8 %copy-start.2 = (s32[2]{0:T(128)S(1)}, s32[2]{0:T(128)}, u32[]{:S(2)}) copy-start(s32[2]{0:T(128)} %param.13) | copy-start | bytes 28
  6.5 6.2 %copy-start.3 = (s32[64]{0:T(128)S(1)}, s32[64]{0:T(128)}, u32[]{:S(2)}) copy-start(s32[64]{0:T(128)} %param.14) | copy-start | bytes 772
  6.5 39.1 %all-reduce.3.cloned.1.call-start = ((), (), s32[]{:S(2)}) async-start(), calls=%async_computation | async-start | bytes 262144 | tf_op jit(solution)/shard_map/psum | solution.py:23
Sparse Core Ops, SparseCore 0:
  11.5 34.0 all-reduce.2
where the time goes:
time: 134 us
  blocking collectives  34 us (25%)
  waiting for transfers between devices  32.9 us (25%)
  other arithmetic  29.7 us (22%)
  between operations  15.5 us (12%)
  matrix products  14.4 us (11%)
  local copies, waits for them, and re-layouts  7.31 us (5%)
    psum x1, waiting for transfers between devices, per_device(): summed = lax.psum(joined, 'tensor')  32.8 us
    psum x1, blocking collectives, per_device(): lax.psum((cov_out_loc, cov_in_loc, tokens_loc), 'dp')  20.4 us
    all_gather x1, blocking collectives, per_device(): every_sketch = lax.all_gather(flat_sketch, 'dp', axis=0, tiled=True)  13.5 us
    another operation x6, other arithmetic, damped_inverse(): factor = jnp.linalg.cholesky(damped)  13 us
    another operation x4, other arithmetic, damped_inverse(): return jax.scipy.linalg.cho_solve((factor, True), eye_mat)  11.1 us
    dot_general x2, matrix products, per_device(): jnp.einsum('ab,jbc,cd->jad', inv_out, query, inv_in, precision=high)  6.63 us
    dot_general x1, matrix products, per_device(): jnp.einsum('elf,fr->elr', activations, proj_in, preferred_element_type=jn...  3.61 us
    dot_general x1, local copies, waits for them, and re-layouts, per_device(): jnp.einsum('ab,jbc,cd->jad', inv_out, query, inv_in, precision=high)  3.1 us
  transfers between devices with their start and end apart: 1, of which 1 were waited for; matrix products, arithmetic and copies ran while one was open for 1% of the time, Pallas kernels for 0%

commit v1 on v0

v1 whole, which is shorter than its diff:
```python
import functools

import jax
import jax.numpy as jnp
from jax import lax
from jax.experimental import pallas as pl
from jax.experimental.pallas import tpu as pltpu
from jax.sharding import PartitionSpec as P

HIGH = lax.Precision.HIGHEST
VMEM = pl.BlockSpec(memory_space=pltpu.VMEM)
SMEM = pl.BlockSpec(memory_space=pltpu.SMEM)
ANY = pl.BlockSpec(memory_space=pl.ANY)
DAMP = 0.1


def dot_nt(a, b):
    return lax.dot_general(a, b, (((1,), (1,)), ((), ())), preferred_element_type=jnp.float32)


def dot_hi(a, b):
    return jnp.dot(a, b, precision=HIGH, preferred_element_type=jnp.float32)


def project_kernel(place, lengths, act, grad, proj_in, proj_out, keep, send, act_v, grad_v, pin_v, pout_v, sems):
    chunks = sems.shape[0] - 1
    width = act.shape[2] // chunks
    copies = []

    def begin(src, dst, slot):
        copy = pltpu.make_async_copy(src, dst, sems.at[slot, len(copies) % 2])
        copy.start()
        copies.append(copy)

    begin(proj_out, pout_v, 0)
    begin(grad, grad_v, 0)
    for n in range(chunks):
        span = pl.ds(n * width, width)
        begin(proj_in.at[:, span], pin_v.at[:, span], n + 1)
        begin(act.at[:, :, span], act_v.at[:, :, span], n + 1)
    examples, seq_len, _ = act.shape
    rank = proj_in.shape[0]
    copies[0].wait()
    copies[1].wait()
    out_part = dot_nt(grad_v[...].reshape(examples * seq_len, -1), pout_v[...])
    in_part = jnp.zeros((examples * seq_len, rank), jnp.float32)
    for n in range(chunks):
        copies[2 * n + 2].wait()
        copies[2 * n + 3].wait()
        span = pl.ds(n * width, width)
        in_part += dot_nt(act_v[:, :, span].reshape(examples * seq_len, width), pin_v[:, span])
    both = jnp.concatenate([out_part, in_part], axis=1)
    token = lax.broadcasted_iota(jnp.int32, (seq_len, 2 * rank), 0)
    first = jnp.where(token < lengths[0], both[:seq_len], 0.0)
    second = jnp.where(token < lengths[1], both[seq_len:], 0.0)
    own = place[0] == 0
    keep[...] = jnp.where(own, first, second)
    send[...] = jnp.where(own, second, first)


def gram_kernel(place, lengths, mine, theirs, packed):
    tokens = mine[...] + theirs[...]
    rank = tokens.shape[1] // 2
    gram = lax.dot_general(
        tokens, tokens, (((0,), (0,)), ((), ())), precision=HIGH, preferred_element_type=jnp.float32
    )
    top = pltpu.roll(gram[:rank], rank, 1)
    low = gram[rank:]
    row = lax.broadcasted_iota(jnp.int32, (rank, 2 * rank), 0)
    lane = lax.broadcasted_iota(jnp.int32, (rank, 2 * rank), 1)
    packed[:rank] = jnp.where(lane <= rank + row, top, low)
    diag = jnp.sum(jnp.where(lane == rank + row, low, 0.0), axis=0, keepdims=True)
    live = lengths[place[0]].astype(jnp.float32)
    tail = jnp.broadcast_to(diag, (8, 2 * rank))
    packed[rank:] = jnp.where(lax.broadcasted_iota(jnp.int32, (8, 2 * rank), 1) < rank, live, tail)


def collect_kernel(*refs):
    packs, total, sketches = refs[:-2], refs[-2], refs[-1]
    rank = packs[0].shape[1] // 2
    parts = [ref[...] for ref in packs]
    lane = lax.broadcasted_iota(jnp.int32, (rank, 2 * rank), 1)
    for n in range(len(parts) // 2):
        sketches[n] = jnp.where(lane < rank, parts[2 * n][:rank], pltpu.roll(parts[2 * n + 1][:rank], rank, 1))
    while len(parts) > 1:
        parts = [parts[n] + parts[n + 1] for n in range(0, len(parts), 2)]
    total[...] = parts[0]


def inverse_steps(rank):
    least = 2.0 * (DAMP / rank) / (1.0 + 2.0 * DAMP / rank)
    scales = []
    while (1.0 - least) ** 2 > 1e-7:
        image = least * (2.0 - least)
        scales.append(2.0 / (1.0 + image))
        least = scales[-1] * image
    return scales + [1.0]


def inverse_kernel(mine, theirs, inv_out, inv_in, scale_out, scale_in):
    total = mine[...] + theirs[...]
    rank = total.shape[1] // 2
    mixed = total[:rank, rank:]
    turned = mixed.T
    diag = total[rank : rank + 1, rank:]
    count = total[rank : rank + 1, :1]
    row = lax.broadcasted_iota(jnp.int32, (rank, rank), 0)
    lane = lax.broadcasted_iota(jnp.int32, (rank, rank), 1)
    eye = row == lane
    sum_out = jnp.where(lane <= row, mixed, turned)
    sum_in = jnp.where(lane > row, mixed, jnp.where(eye, diag, turned))
    factor = 2.0 / (1.0 + 2.0 * DAMP / rank)

    def start(sums):
        trace = jnp.sum(jnp.sum(jnp.where(eye, sums, 0.0), axis=0, keepdims=True), axis=1, keepdims=True)
        return sums * (factor / trace) + jnp.where(eye, factor * DAMP / rank, 0.0), factor * count / trace

    t_out, c_out = start(sum_out)
    t_in, c_in = start(sum_in)
    steps = inverse_steps(rank)
    two_eye = jnp.where(eye, 2.0, 0.0)
    x_out = steps[0] * (two_eye - t_out)
    x_in = steps[0] * (two_eye - t_in)
    t_out = steps[0] * (2.0 * t_out - dot_hi(t_out, t_out))
    t_in = steps[0] * (2.0 * t_in - dot_hi(t_in, t_in))
    for n, scale in enumerate(steps[1:]):
        x_out, x_in, p_out, p_in = (
            scale * (2.0 * x_out - dot_hi(x_out, t_out)),
            scale * (2.0 * x_in - dot_hi(x_in, t_in)),
            t_out,
            t_in,
        )
        if n < len(steps) - 2:
            t_out = scale * (2.0 * p_out - dot_hi(p_out, p_out))
            t_in = scale * (2.0 * p_in - dot_hi(p_in, p_in))
    inv_out[...] = x_out
    inv_in[...] = x_in
    scale_out[...] = jnp.broadcast_to(c_out, scale_out.shape)
    scale_in[...] = jnp.broadcast_to(c_in, scale_in.shape)


def score_kernel(place, queries, mine, theirs, inv_out, inv_in, scale_out, scale_in, scores):
    pairs = mine.shape[0]
    rank = mine.shape[1]
    right = jnp.concatenate([inv_in[...], inv_in[...]], axis=1)
    left = inv_out[...]
    blocks = [mine[n] for n in range(pairs)] + [theirs[n] for n in range(pairs)]
    rows = []
    for own in (mine[0][:, :rank], theirs[0][:, :rank]):
        half = dot_hi(left, own) * scale_out[:1, :1]
        whole = dot_hi(half, right) * scale_in[:1, :1]
        for block in blocks:
            rows.append(jnp.sum(block * whole, axis=0, keepdims=True))
    sums = jnp.concatenate(rows, axis=0)
    height = len(rows)
    num = queries.shape[1]
    index = lax.broadcasted_iota(jnp.int32, (height, num), 0) % (2 * pairs)
    core = place[0] ^ (index // pairs)
    chosen = queries[...]
    terms = jnp.zeros((height, num), jnp.float32)
    for half in range(2):
        value = jnp.sum(sums[:, half * rank : (half + 1) * rank], axis=1, keepdims=True)
        example = (place[1] ^ (2 * (index % pairs) + half)) * 2 + core
        terms += jnp.where(chosen == example, value, 0.0)
    terms = terms * (1.0 / place[2].astype(jnp.float32))
    here = jnp.sum(terms[: height // 2], axis=0, keepdims=True)
    there = jnp.sum(terms[height // 2 :], axis=0, keepdims=True)
    own = place[0] == 0
    scores[0:1, :] = jnp.where(own, here, there)
    scores[1:2, :] = jnp.where(own, there, here)


def shape(*dims):
    return jax.ShapeDtypeStruct(dims, jnp.float32)


def mirror(size, step):
    return [(n, n ^ step) for n in range(size)]


def per_device(dp, tensor, activations, out_grads, proj_in, proj_out, lengths, query_ids):
    examples, seq_len, hidden = activations.shape
    rank = proj_in.shape[1]
    num = query_ids.shape[0]
    chunks = 7 if hidden % (7 * 128) == 0 else 1
    side = lax.axis_index("tensor") % 2
    depth = lax.axis_index("dp")
    place = jnp.stack([side, depth, jnp.int32(rank * seq_len)]).astype(jnp.int32)
    pin_t, pout_t = proj_in.T, proj_out.T
    keep, send = pl.pallas_call(
        project_kernel,
        out_shape=[shape(seq_len, 2 * rank)] * 2,
        in_specs=[SMEM, SMEM, ANY, ANY, ANY, ANY],
        out_specs=[VMEM, VMEM],
        scratch_shapes=[
            pltpu.VMEM(activations.shape, jnp.bfloat16),
            pltpu.VMEM(out_grads.shape, jnp.bfloat16),
            pltpu.VMEM(pin_t.shape, jnp.bfloat16),
            pltpu.VMEM(pout_t.shape, jnp.bfloat16),
            pltpu.SemaphoreType.DMA((chunks + 1, 2)),
        ],
        compiler_params=pltpu.CompilerParams(vmem_limit_bytes=24 * 2**20),
        name="project",
    )(place, lengths, activations, out_grads, pin_t, pout_t)
    total = keep + lax.ppermute(send, "tensor", mirror(tensor, 1))
    step = 2
    while 2 * step < tensor:
        total = total + lax.ppermute(total, "tensor", mirror(tensor, step))
        step *= 2
    other = lax.ppermute(total, "tensor", mirror(tensor, step)) if step < tensor else jnp.zeros_like(total)
    packed = pl.pallas_call(
        gram_kernel,
        out_shape=shape(rank + 8, 2 * rank),
        in_specs=[SMEM, SMEM, VMEM, VMEM],
        out_specs=VMEM,
        name="gram",
    )(place, lengths, total, other)
    if dp <= 4:
        packs = [packed] + [lax.ppermute(packed, "dp", mirror(dp, step)) for step in range(1, dp)]
    else:
        gathered = lax.all_gather(packed, "dp", axis=0)[depth ^ jnp.arange(dp, dtype=jnp.int32)]
        packs = [gathered[n] for n in range(dp)]
    summed, sketches = pl.pallas_call(
        collect_kernel,
        out_shape=[shape(rank + 8, 2 * rank), shape(dp // 2, rank, 2 * rank)],
        in_specs=[VMEM] * dp,
        out_specs=[VMEM, VMEM],
        name="collect",
    )(*packs)
    summed_other = lax.ppermute(summed, "tensor", mirror(tensor, 1))
    sketches_other = lax.ppermute(sketches, "tensor", mirror(tensor, 1))
    inverses = pl.pallas_call(
        inverse_kernel,
        out_shape=[shape(rank, rank), shape(rank, rank), shape(8, 128), shape(8, 128)],
        in_specs=[VMEM, VMEM],
        out_specs=[VMEM] * 4,
        name="inverse",
    )(summed, summed_other)
    scores = pl.pallas_call(
        score_kernel,
        out_shape=shape(examples, num),
        in_specs=[SMEM] + [VMEM] * 7,
        out_specs=VMEM,
        name="scores",
    )(place, query_ids.reshape(1, num), sketches, sketches_other, *inverses)
    return scores.T


def solution(mesh):
    placed = (
        P(("groups", "dp"), None, "tensor"),
        P(("groups", "dp"), None, "tensor"),
        P("tensor", None),
        P("tensor", None),
        P(("groups", "dp")),
        P("groups"),
    )
    return jax.shard_map(
        functools.partial(per_device, mesh.shape["dp"], mesh.shape["tensor"]),
        mesh=mesh,
        in_specs=placed,
        out_specs=P(None, ("groups", "dp")),
        check_vma=False,
    )
```

time: 134 us -> 40.1 us (0.30)
  blocking collectives: 34 us -> 0 us
  other arithmetic: 29.7 us -> 0.09 us
  waiting for transfers between devices: 32.9 us -> 8.9 us
  between operations: 15.5 us -> 0.05 us
  matrix products: 14.4 us -> 0 us
  Pallas kernels: 0 us -> 13 us
  starting transfers between devices: 0.03 us -> 8.46 us
  local copies, waits for them, and re-layouts: 7.31 us -> 9.15 us
    psum x1 -> x0, waiting for transfers between devices: 32.8 us -> none  [per_device(): summed = lax.psum(joined, 'tensor')]
    another operation x10 -> x1, other arithmetic: 24.1 us -> 0.08 us  [per_device(): jnp.stack([side, depth, jnp.int32(rank * seq_len)]).astype(jnp.int32)]
    psum x1 -> x0, blocking collectives: 20.4 us -> none  [per_device(): lax.psum((cov_out_loc, cov_in_loc, tokens_loc), 'dp')]
    dot_general x8 -> x0, matrix products: 13.6 us -> none  [the longest x2 6.63 us: per_device(): jnp.einsum('ab,jbc,cd->jad', inv_out, query, inv_in, precision=high)]
    all_gather x1 -> x0, blocking collectives: 13.5 us -> none  [per_device(): every_sketch = lax.all_gather(flat_sketch, 'dp', axis=0, tiled=True)]
    pallas_call x0 -> x5, Pallas kernels: none -> 13 us  [the longest x1 4.07 us: per_device(): pl.pallas_call(project_kernel, out_shape=[shape(seq_len, 2 * rank)] * 2,...]
    unnamed x10 -> x26, local copies, waits for them, and re-layouts: 0.2 us -> 9.15 us
    ppermute x0 -> x7, waiting for transfers between devices: none -> 8.9 us  [the longest x3 4.5 us: per_device(): lax.ppermute(packed, 'dp', mirror(dp, step))]
  transfers between devices with their start and end apart: 1 -> 7, of which waited for: 1 -> 5; matrix products, arithmetic and copies ran while one was open for 1% -> 0% of each run, Pallas kernels for 0% -> 9%
where the time goes in v1:
time: 40.1 us; the launch traced here: 39.7 us
  Pallas kernels  13 us (32%)
  local copies, waits for them, and re-layouts  9.15 us (23%)
  waiting for transfers between devices  8.9 us (22%)
  starting transfers between devices  8.46 us (21%)
    unnamed x26, local copies, waits for them, and re-layouts  9.15 us
    ppermute x3, starting transfers between devices, per_device(): lax.ppermute(packed, 'dp', mirror(dp, step))  4.53 us
    ppermute x3, waiting for transfers between devices, per_device(): lax.ppermute(packed, 'dp', mirror(dp, step))  4.5 us
    pallas_call x1, Pallas kernels, per_device(): pl.pallas_call(project_kernel, out_shape=[shape(seq_len, 2 * rank)] * 2,...  4.07 us
    pallas_call x1, Pallas kernels, per_device(): pl.pallas_call(inverse_kernel, out_shape=[shape(rank, rank), shape(rank,...  3.55 us
    ppermute x1, starting transfers between devices, per_device(): lax.ppermute(total, 'tensor', mirror(tensor, step))  2.9 us
    ppermute x1, waiting for transfers between devices, per_device(): lax.ppermute(total, 'tensor', mirror(tensor, step))  2.41 us
    pallas_call x1, Pallas kernels, per_device(): pl.pallas_call(score_kernel, out_shape=shape(examples, num), in_specs=[SM...  2.05 us
  transfers between devices with their start and end apart: 7, of which 5 were waited for; matrix products, arithmetic and copies ran while one was open for 0% of the time, Pallas kernels for 9%

profile of v1, /device:TPU:0, one launch (start us, length us, event | category | flops | bytes accessed | tf_op | source)
XLA Modules:
  0.0 39.7 jit_solution(5982651779238616055)
XLA Ops:
  0.0 0.1 pad_add_fusion.place
  0.1 0.0 copy-start.4
  0.1 0.0 copy-start
  0.1 2.0 %copy-done = bf16[2,128,7168]{2,1,0:T(8,128)(2,1)S(1)} copy-done((bf16[2,128,7168]{2,1,0:T(8,128)(2,1)S(1)}, bf16[2,128,7168]{2,1,0:T(8,128)(2,1)}, u32[]{:S(2)}) %copy-start) | copy-done | bytes 3670040
  2.1 0.0 copy-start.1
  2.1 1.2 %copy-done.1 = bf16[2,128,2048]{2,1,0:T(8,128)(2,1)S(1)} copy-done((bf16[2,128,2048]{2,1,0:T(8,128)(2,1)S(1)}, bf16[2,128,2048]{2,1,0:T(8,128)(2,1)}, u32[]{:S(2)}) %copy-start.1) | copy-done | bytes 1048600
  3.3 0.0 copy-start.2
  3.3 1.2 %copy-done.2 = bf16[7168,64]{0,1:T(8,128)(2,1)S(1)} copy-done((bf16[7168,64]{0,1:T(8,128)(2,1)S(1)}, bf16[7168,64]{0,1:T(8,128)(2,1)}, u32[]{:S(2)}) %copy-start.2) | copy-done | bytes 917528
  4.5 0.0 copy-start.3
  4.5 0.9 %copy-done.3 = bf16[2048,64]{0,1:T(8,128)(2,1)S(1)} copy-done((bf16[2048,64]{0,1:T(8,128)(2,1)S(1)}, bf16[2048,64]{0,1:T(8,128)(2,1)}, u32[]{:S(2)}) %copy-start.3) | copy-done | bytes 262168
  5.5 0.0 copy-start.5
  5.5 0.7 %copy-done.5 = s32[2]{0:T(128)S(1)} copy-done((s32[2]{0:T(128)S(1)}, s32[2]{0:T(128)}, u32[]{:S(2)}) %copy-start.5) | copy-done | bytes 32
  6.1 4.1 %project.1 = (f32[128,128]{1,0:T(8,128)S(1)}, f32[128,128]{1,0:T(8,128)S(1)}) custom-call(s32[3]{0:T(128)S(1)} %pad_add_fusion.place, s32[2]{0:T(128)S(1)} %copy-done.5, bf16[2,128,7168]{2,1,0:T(8,128)(2,1)S(1)} %copy-done, bf16[2,128,2048]{2,1,0:T(8,128)(2,1)S(1)} %copy-done.1, bf16[64,7168]{1,0:T(8,128)(2,1)S(1)} %bitcast.6, bf16[64,2048]{1,0:T(8,128)(2,1)S(1)} %bitcast.7), custom_call_target="tpu_custom_call" | custom-call | tf_op jit(solution)/shard_map/project/pallas_call | solution.py:190
  10.2 0.5 %collective-permute-start = (f32[128,128]{1,0:T(8,128)S(1)}, f32[128,128]{1,0:T(8,128)S(1)}, u32[]{:S(2)}, u32[]{:S(2)}) collective-permute-start(f32[128,128]{1,0:T(8,128)S(1)} %get-tuple-element.14), channel_id=1, source_target_pairs={{0,1},{1,0},{2,3},{3,2},{4,5},{5,4},{6,7},{7,6},{8,9},{9,8},{10,11... | collective-permute-start | bytes 196616 | tf_op jit(solution)/shard_map/ppermute | solution.py:205
  10.7 0.9 %collective-permute-done = f32[128,128]{1,0:T(8,128)S(1)} collective-permute-done((f32[128,128]{1,0:T(8,128)S(1)}, f32[128,128]{1,0:T(8,128)S(1)}, u32[]{:S(2)}, u32[]{:S(2)}) %collective-permute-start) | collective-permute-done | bytes 65568 | tf_op jit(solution)/shard_map/ppermute | solution.py:205
  11.6 0.0 copy-start.6
  11.7 2.9 %collective-permute-start.1 = (f32[128,128]{1,0:T(8,128)S(1)}, f32[128,128]{1,0:T(8,128)S(1)}, u32[]{:S(2)}, u32[]{:S(2)}) collective-permute-start(f32[128,128]{1,0:T(8,128)S(1)} %add.8.mine), channel_id=1, source_target_pairs={{0,2},{1,3},{2,0},{3,1},{4,6},{5,7},{6,4},{7,5},{8,10},{9,11},{10,... | collective-permute-start | bytes 196616 | tf_op jit(solution)/shard_map/ppermute | solution.py:210
  14.6 2.4 %collective-permute-done.1.theirs = f32[128,128]{1,0:T(8,128)S(1)} collective-permute-done((f32[128,128]{1,0:T(8,128)S(1)}, f32[128,128]{1,0:T(8,128)S(1)}, u32[]{:S(2)}, u32[]{:S(2)}) %collective-permute-start.1) | collective-permute-done | bytes 65568 | tf_op jit(solution)/shard_map/ppermute | solution.py:210
  17.0 0.0 copy-done.4
  17.0 0.0 copy-done.6
  17.0 0.0 copy-start.8
  17.0 0.6 %copy-done.8 = f32[128,128]{1,0:T(8,128)} copy-done((f32[128,128]{1,0:T(8,128)}, f32[128,128]{1,0:T(8,128)S(1)}, u32[]{:S(2)}) %copy-start.8) | copy-done | bytes 65560
  17.6 1.8 %gram.1.refs_0_ = f32[72,128]{1,0:T(8,128)} custom-call(s32[3]{0:T(128)} %copy-done.4, s32[2]{0:T(128)} %lengths.3, f32[128,128]{1,0:T(8,128)} %copy-done.6, f32[128,128]{1,0:T(8,128)} %copy-done.8), custom_call_target="tpu_custom_call" | custom-call | tf_op jit(solution)/shard_map/gram/pallas_call | solution.py:211
  19.4 4.0 %collective-permute-start.4 = (f32[72,128]{1,0:T(8,128)}, f32[72,128]{1,0:T(8,128)S(1)}, u32[]{:S(2)}, u32[]{:S(2)}) collective-permute-start(f32[72,128]{1,0:T(8,128)} %gram.1.refs_0_), channel_id=1, source_target_pairs={{0,12},{4,8},{8,4},{12,0},{1,13},{5,9},{9,5},{13,1},{2,14},{6,10},... | collective-permute-start | bytes 110600 | tf_op jit(solution)/shard_map/ppermute | solution.py:219
  23.4 0.0 collective-permute-start.3
  23.4 0.6 %collective-permute-start.2 = (f32[72,128]{1,0:T(8,128)}, f32[72,128]{1,0:T(8,128)S(1)}, u32[]{:S(2)}, u32[]{:S(2)}) collective-permute-start(f32[72,128]{1,0:T(8,128)} %gram.1.refs_0_), channel_id=1, source_target_pairs={{0,4},{4,0},{8,12},{12,8},{1,5},{5,1},{9,13},{13,9},{2,6},{6,2},{1... | collective-permute-start | bytes 110600 | tf_op jit(solution)/shard_map/ppermute | solution.py:219
  24.0 1.8 %collective-permute-done.4.refs_3_ = f32[72,128]{1,0:T(8,128)S(1)} collective-permute-done((f32[72,128]{1,0:T(8,128)}, f32[72,128]{1,0:T(8,128)S(1)}, u32[]{:S(2)}, u32[]{:S(2)}) %collective-permute-start.4) | collective-permute-done | bytes 36896 | tf_op jit(solution)/shard_map/ppermute | solution.py:219
  25.7 0.0 copy-start.10
  25.7 2.7 %collective-permute-done.3.refs_2_ = f32[72,128]{1,0:T(8,128)S(1)} collective-permute-done((f32[72,128]{1,0:T(8,128)}, f32[72,128]{1,0:T(8,128)S(1)}, u32[]{:S(2)}, u32[]{:S(2)}) %collective-permute-start.3) | collective-permute-done | bytes 36896 | tf_op jit(solution)/shard_map/ppermute | solution.py:219
  28.5 0.0 copy-start.11
  28.5 0.0 collective-permute-done.2.refs_1_
  28.5 0.0 copy-done.10
  28.5 0.6 %copy-done.11 = f32[72,128]{1,0:T(8,128)} copy-done((f32[72,128]{1,0:T(8,128)}, f32[72,128]{1,0:T(8,128)S(1)}, u32[]{:S(2)}) %copy-start.11) | copy-done | bytes 36888
  29.1 0.0 copy-start.12
  29.1 0.6 %copy-done.12 = f32[72,128]{1,0:T(8,128)} copy-done((f32[72,128]{1,0:T(8,128)}, f32[72,128]{1,0:T(8,128)S(1)}, u32[]{:S(2)}) %copy-start.12) | copy-done | bytes 36888
  29.7 1.5 %collect.1 = (f32[72,128]{1,0:T(8,128)}, f32[2,64,128]{2,1,0:T(8,128)}) custom-call(f32[72,128]{1,0:T(8,128)} %gram.1.refs_0_, f32[72,128]{1,0:T(8,128)} %copy-done.12, f32[72,128]{1,0:T(8,128)} %copy-done.11, f32[72,128]{1,0:T(8,128)} %copy-done.10), custom_call_target="tpu_custom_call" | custom-call | tf_op jit(solution)/shard_map/collect/pallas_call | solution.py:223
  31.2 0.0 collective-permute-start.5
  31.2 0.5 %collective-permute-start.6 = (f32[72,128]{1,0:T(8,128)}, f32[72,128]{1,0:T(8,128)S(1)}, u32[]{:S(2)}, u32[]{:S(2)}) collective-permute-start(f32[72,128]{1,0:T(8,128)} %get-tuple-element.16.mine), channel_id=1, source_target_pairs={{0,1},{1,0},{2,3},{3,2},{4,5},{5,4},{6,7},{7,6},{8,9},{9,8},{10,11... | collective-permute-start | bytes 110600 | tf_op jit(solution)/shard_map/ppermute | solution.py:230
  31.7 1.1 %collective-permute-done.6.theirs = f32[72,128]{1,0:T(8,128)S(1)} collective-permute-done((f32[72,128]{1,0:T(8,128)}, f32[72,128]{1,0:T(8,128)S(1)}, u32[]{:S(2)}, u32[]{:S(2)}) %collective-permute-start.6) | collective-permute-done | bytes 36896 | tf_op jit(solution)/shard_map/ppermute | solution.py:230
  32.8 0.0 copy-start.9
  32.8 0.6 %copy-done.9 = f32[72,128]{1,0:T(8,128)} copy-done((f32[72,128]{1,0:T(8,128)}, f32[72,128]{1,0:T(8,128)S(1)}, u32[]{:S(2)}) %copy-start.9) | copy-done | bytes 36888
  33.4 3.5 %inverse.1 = (f32[64,64]{1,0:T(8,128)}, f32[64,64]{1,0:T(8,128)}, f32[8,128]{1,0:T(8,128)}, f32[8,128]{1,0:T(8,128)}) custom-call(f32[72,128]{1,0:T(8,128)} %get-tuple-element.16.mine, f32[72,128]{1,0:T(8,128)} %copy-done.9), custom_call_target="tpu_custom_call" | custom-call | tf_op jit(solution)/shard_map/inverse/pallas_call | solution.py:232
  37.0 0.0 collective-permute-done.5.theirs
  37.0 0.0 copy-start.7
  37.0 0.6 %copy-done.7 = f32[2,64,128]{2,1,0:T(8,128)} copy-done((f32[2,64,128]{2,1,0:T(8,128)}, f32[2,64,128]{2,1,0:T(8,128)S(1)}, u32[]{:S(2)}) %copy-start.7) | copy-done | bytes 65560
  37.6 2.1 %scores.1 = f32[2,64]{1,0:T(2,128)} custom-call(s32[3]{0:T(128)} %copy-done.4, s32[1,64]{1,0:T(1,128)} %bitcast.8, f32[2,64,128]{2,1,0:T(8,128)} %get-tuple-element.15.mine, f32[2,64,128]{2,1,0:T(8,128)} %copy-done.7, f32[64,64]{1,0:T(8,128)} %get-tuple-element.17.inv_out, f32[64,64]{1,0:T(8,128)} %get-tuple-element.18.inv_in, ...), custom_call_target="tpu_custom_call" | custom-call | tf_op jit(solution)/shard_map/scores/pallas_call | solution.py:239
  (1 shorter events, 0.0 us)
Async XLA Ops:
  0.1 16.9 %copy-start.4 = (s32[3]{0:T(128)}, s32[3]{0:T(128)S(1)}, u32[]{:S(2)}) copy-start(s32[3]{0:T(128)S(1)} %pad_add_fusion.place) | copy-start | bytes 40
  0.1 2.0 %copy-start = (bf16[2,128,7168]{2,1,0:T(8,128)(2,1)S(1)}, bf16[2,128,7168]{2,1,0:T(8,128)(2,1)}, u32[]{:S(2)}) copy-start(bf16[2,128,7168]{2,1,0:T(8,128)(2,1)} %act.1) | copy-start | bytes 11010052
  2.1 1.2 %copy-start.1 = (bf16[2,128,2048]{2,1,0:T(8,128)(2,1)S(1)}, bf16[2,128,2048]{2,1,0:T(8,128)(2,1)}, u32[]{:S(2)}) copy-start(bf16[2,128,2048]{2,1,0:T(8,128)(2,1)} %grad.1) | copy-start | bytes 3145732
  3.3 1.2 %copy-start.2 = (bf16[7168,64]{0,1:T(8,128)(2,1)S(1)}, bf16[7168,64]{0,1:T(8,128)(2,1)}, u32[]{:S(2)}) copy-start(bf16[7168,64]{0,1:T(8,128)(2,1)} %param.8) | copy-start | bytes 2752516
  4.5 0.9 %copy-start.3 = (bf16[2048,64]{0,1:T(8,128)(2,1)S(1)}, bf16[2048,64]{0,1:T(8,128)(2,1)}, u32[]{:S(2)}) copy-start(bf16[2048,64]{0,1:T(8,128)(2,1)} %param.9) | copy-start | bytes 786436
  5.5 0.7 %copy-start.5 = (s32[2]{0:T(128)S(1)}, s32[2]{0:T(128)}, u32[]{:S(2)}) copy-start(s32[2]{0:T(128)} %lengths.3) | copy-start | bytes 28
  10.2 1.4 %collective-permute-start = (f32[128,128]{1,0:T(8,128)S(1)}, f32[128,128]{1,0:T(8,128)S(1)}, u32[]{:S(2)}, u32[]{:S(2)}) collective-permute-start(f32[128,128]{1,0:T(8,128)S(1)} %get-tuple-element.14), channel_id=1, source_target_pairs={{0,1},{1,0},{2,3},{3,2},{4,5},{5,4},{6,7},{7,6},{8,9},{9,8},{10,11... | collective-permute-start | bytes 196616 | tf_op jit(solution)/shard_map/ppermute | solution.py:205
  11.6 5.3 %copy-start.6 = (f32[128,128]{1,0:T(8,128)}, f32[128,128]{1,0:T(8,128)S(1)}, u32[]{:S(2)}) copy-start(f32[128,128]{1,0:T(8,128)S(1)} %add.8.mine) | copy-start | bytes 196612
  11.7 5.3 %collective-permute-start.1 = (f32[128,128]{1,0:T(8,128)S(1)}, f32[128,128]{1,0:T(8,128)S(1)}, u32[]{:S(2)}, u32[]{:S(2)}) collective-permute-start(f32[128,128]{1,0:T(8,128)S(1)} %add.8.mine), channel_id=1, source_target_pairs={{0,2},{1,3},{2,0},{3,1},{4,6},{5,7},{6,4},{7,5},{8,10},{9,11},{10,... | collective-permute-start | bytes 196616 | tf_op jit(solution)/shard_map/ppermute | solution.py:210
  17.0 0.6 %copy-start.8 = (f32[128,128]{1,0:T(8,128)}, f32[128,128]{1,0:T(8,128)S(1)}, u32[]{:S(2)}) copy-start(f32[128,128]{1,0:T(8,128)S(1)} %collective-permute-done.1.theirs) | copy-start | bytes 196612
  19.4 6.3 %collective-permute-start.4 = (f32[72,128]{1,0:T(8,128)}, f32[72,128]{1,0:T(8,128)S(1)}, u32[]{:S(2)}, u32[]{:S(2)}) collective-permute-start(f32[72,128]{1,0:T(8,128)} %gram.1.refs_0_), channel_id=1, source_target_pairs={{0,12},{4,8},{8,4},{12,0},{1,13},{5,9},{9,5},{13,1},{2,14},{6,10},... | collective-permute-start | bytes 110600 | tf_op jit(solution)/shard_map/ppermute | solution.py:219
  23.4 5.1 %collective-permute-start.3 = (f32[72,128]{1,0:T(8,128)}, f32[72,128]{1,0:T(8,128)S(1)}, u32[]{:S(2)}, u32[]{:S(2)}) collective-permute-start(f32[72,128]{1,0:T(8,128)} %gram.1.refs_0_), channel_id=1, source_target_pairs={{0,8},{4,12},{8,0},{12,4},{1,9},{5,13},{9,1},{13,5},{2,10},{6,14},... | collective-permute-start | bytes 110600 | tf_op jit(solution)/shard_map/ppermute | solution.py:219
  23.4 5.1 %collective-permute-start.2 = (f32[72,128]{1,0:T(8,128)}, f32[72,128]{1,0:T(8,128)S(1)}, u32[]{:S(2)}, u32[]{:S(2)}) collective-permute-start(f32[72,128]{1,0:T(8,128)} %gram.1.refs_0_), channel_id=1, source_target_pairs={{0,4},{4,0},{8,12},{12,8},{1,5},{5,1},{9,13},{13,9},{2,6},{6,2},{1... | collective-permute-start | bytes 110600 | tf_op jit(solution)/shard_map/ppermute | solution.py:219
  25.7 2.7 %copy-start.10 = (f32[72,128]{1,0:T(8,128)}, f32[72,128]{1,0:T(8,128)S(1)}, u32[]{:S(2)}) copy-start(f32[72,128]{1,0:T(8,128)S(1)} %collective-permute-done.4.refs_3_) | copy-start | bytes 110596
  28.5 0.6 %copy-start.11 = (f32[72,128]{1,0:T(8,128)}, f32[72,128]{1,0:T(8,128)S(1)}, u32[]{:S(2)}) copy-start(f32[72,128]{1,0:T(8,128)S(1)} %collective-permute-done.3.refs_2_) | copy-start | bytes 110596
  29.1 0.6 %copy-start.12 = (f32[72,128]{1,0:T(8,128)}, f32[72,128]{1,0:T(8,128)S(1)}, u32[]{:S(2)}) copy-start(f32[72,128]{1,0:T(8,128)S(1)} %collective-permute-done.2.refs_1_) | copy-start | bytes 110596
  31.2 5.8 %collective-permute-start.5 = (f32[2,64,128]{2,1,0:T(8,128)}, f32[2,64,128]{2,1,0:T(8,128)S(1)}, u32[]{:S(2)}, u32[]{:S(2)}) collective-permute-start(f32[2,64,128]{2,1,0:T(8,128)} %get-tuple-element.15.mine), channel_id=1, source_target_pairs={{0,1},{1,0},{2,3},{3,2},{4,5},{5,4},{6,7},{7,6},{8,9},{9,8},{10,11... | collective-permute-start | bytes 196616 | tf_op jit(solution)/shard_map/ppermute | solution.py:231
  31.2 1.6 %collective-permute-start.6 = (f32[72,128]{1,0:T(8,128)}, f32[72,128]{1,0:T(8,128)S(1)}, u32[]{:S(2)}, u32[]{:S(2)}) collective-permute-start(f32[72,128]{1,0:T(8,128)} %get-tuple-element.16.mine), channel_id=1, source_target_pairs={{0,1},{1,0},{2,3},{3,2},{4,5},{5,4},{6,7},{7,6},{8,9},{9,8},{10,11... | collective-permute-start | bytes 110600 | tf_op jit(solution)/shard_map/ppermute | solution.py:230
  32.8 0.6 %copy-start.9 = (f32[72,128]{1,0:T(8,128)}, f32[72,128]{1,0:T(8,128)S(1)}, u32[]{:S(2)}) copy-start(f32[72,128]{1,0:T(8,128)S(1)} %collective-permute-done.6.theirs) | copy-start | bytes 110596
  37.0 0.6 %copy-start.7 = (f32[2,64,128]{2,1,0:T(8,128)}, f32[2,64,128]{2,1,0:T(8,128)S(1)}, u32[]{:S(2)}) copy-start(f32[2,64,128]{2,1,0:T(8,128)S(1)} %collective-permute-done.5.theirs) | copy-start | bytes 196612

commit v2 on v1

--- a/solution.py
+++ b/solution.py
@@ -9,8 +9,7 @@
 
 HIGH = lax.Precision.HIGHEST
 VMEM = pl.BlockSpec(memory_space=pltpu.VMEM)
-SMEM = pl.BlockSpec(memory_space=pltpu.SMEM)
-ANY = pl.BlockSpec(memory_space=pl.ANY)
+HBM = pl.BlockSpec(memory_space=pltpu.HBM)
 DAMP = 0.1
 
 
@@ -22,8 +21,8 @@
     return jnp.dot(a, b, precision=HIGH, preferred_element_type=jnp.float32)
 
 
-def project_kernel(place, lengths, act, grad, proj_in, proj_out, keep, send, act_v, grad_v, pin_v, pout_v, sems):
-    chunks = sems.shape[0] - 1
+def project_kernel(lengths, act, grad, proj_in, proj_out, keep, send, live, len_s, act_v, grad_v, pin_v, pout_v, sems):
+    chunks = sems.shape[0] - 2
     width = act.shape[2] // chunks
     copies = []
 
@@ -34,6 +33,7 @@
 
     begin(proj_out, pout_v, 0)
     begin(grad, grad_v, 0)
+    begin(lengths, len_s, chunks + 1)
     for n in range(chunks):
         span = pl.ds(n * width, width)
         begin(proj_in.at[:, span], pin_v.at[:, span], n + 1)
@@ -45,20 +45,22 @@
     out_part = dot_nt(grad_v[...].reshape(examples * seq_len, -1), pout_v[...])
     in_part = jnp.zeros((examples * seq_len, rank), jnp.float32)
     for n in range(chunks):
-        copies[2 * n + 2].wait()
         copies[2 * n + 3].wait()
+        copies[2 * n + 4].wait()
         span = pl.ds(n * width, width)
         in_part += dot_nt(act_v[:, :, span].reshape(examples * seq_len, width), pin_v[:, span])
     both = jnp.concatenate([out_part, in_part], axis=1)
     token = lax.broadcasted_iota(jnp.int32, (seq_len, 2 * rank), 0)
-    first = jnp.where(token < lengths[0], both[:seq_len], 0.0)
-    second = jnp.where(token < lengths[1], both[seq_len:], 0.0)
-    own = place[0] == 0
-    keep[...] = jnp.where(own, first, second)
-    send[...] = jnp.where(own, second, first)
-
-
-def gram_kernel(place, lengths, mine, theirs, packed):
+    copies[2].wait()
+    first = jnp.where(token < len_s[0], both[:seq_len], 0.0)
+    second = jnp.where(token < len_s[1], both[seq_len:], 0.0)
+    side = lax.rem(lax.axis_index("tensor"), 2)
+    keep[...] = jnp.where(side == 0, first, second)
+    send[...] = jnp.where(side == 0, second, first)
+    live[...] = jnp.full(live.shape, len_s[side].astype(jnp.float32))
+
+
+def gram_kernel(live, mine, theirs, packed):
     tokens = mine[...] + theirs[...]
     rank = tokens.shape[1] // 2
     gram = lax.dot_general(
@@ -70,9 +72,7 @@
     lane = lax.broadcasted_iota(jnp.int32, (rank, 2 * rank), 1)
     packed[:rank] = jnp.where(lane <= rank + row, top, low)
     diag = jnp.sum(jnp.where(lane == rank + row, low, 0.0), axis=0, keepdims=True)
-    live = lengths[place[0]].astype(jnp.float32)
-    tail = jnp.broadcast_to(diag, (8, 2 * rank))
-    packed[rank:] = jnp.where(lax.broadcasted_iota(jnp.int32, (8, 2 * rank), 1) < rank, live, tail)
+    packed[rank:] = jnp.where(lax.broadcasted_iota(jnp.int32, (8, 2 * rank), 1) < rank, live[...], diag)
 
 
 def collect_kernel(*refs):
@@ -139,7 +139,7 @@
     scale_in[...] = jnp.broadcast_to(c_in, scale_in.shape)
 
 
-def score_kernel(place, queries, mine, theirs, inv_out, inv_in, scale_out, scale_in, scores):
+def score_kernel(seq_len, queries, mine, theirs, inv_out, inv_in, scale_out, scale_in, scores):
     pairs = mine.shape[0]
     rank = mine.shape[1]
     right = jnp.concatenate([inv_in[...], inv_in[...]], axis=1)
@@ -155,94 +155,93 @@
     height = len(rows)
     num = queries.shape[1]
     index = lax.broadcasted_iota(jnp.int32, (height, num), 0) % (2 * pairs)
-    core = place[0] ^ (index // pairs)
+    side = lax.rem(lax.axis_index("tensor"), 2)
+    depth = lax.axis_index("dp")
+    core = side ^ (index // pairs)
     chosen = queries[...]
     terms = jnp.zeros((height, num), jnp.float32)
     for half in range(2):
         value = jnp.sum(sums[:, half * rank : (half + 1) * rank], axis=1, keepdims=True)
-        example = (place[1] ^ (2 * (index % pairs) + half)) * 2 + core
+        example = (depth ^ (2 * (index % pairs) + half)) * 2 + core
         terms += jnp.where(chosen == example, value, 0.0)
-    terms = terms * (1.0 / place[2].astype(jnp.float32))
+    terms = terms * (1.0 / (rank * seq_len))
     here = jnp.sum(terms[: height // 2], axis=0, keepdims=True)
     there = jnp.sum(terms[height // 2 :], axis=0, keepdims=True)
-    own = place[0] == 0
-    scores[0:1, :] = jnp.where(own, here, there)
-    scores[1:2, :] = jnp.where(own, there, here)
+    scores[0:1, :] = jnp.where(side == 0, here, there)
+    scores[1:2, :] = jnp.where(side == 0, there, here)
 
 
 def shape(*dims):
-    return jax.ShapeDtypeStruct(dims, jnp.float32)
+    return pltpu.VMEM(dims, jnp.float32)
+
+
+def call(kernel, name, out_shape, *operands):
+    many = isinstance(out_shape, list)
+    return pl.pallas_call(
+        kernel,
+        out_shape=out_shape,
+        in_specs=[VMEM] * len(operands),
+        out_specs=[VMEM] * len(out_shape) if many else VMEM,
+        compiler_params=pltpu.CompilerParams(vmem_limit_bytes=4 * 2**20),
+        name=name,
+    )(*[pltpu.with_memory_space_constraint(operand, pltpu.VMEM) for operand in operands])
 
 
 def mirror(size, step):
     return [(n, n ^ step) for n in range(size)]
 
 
+def project(activations, out_grads, proj_in, proj_out, lengths):
+    seq_len, hidden = activations.shape[1:]
+    chunks = 7 if hidden % (7 * 128) == 0 else 1
+    block = shape(seq_len, 2 * proj_in.shape[0])
+    operands = [lengths, activations, out_grads, proj_in, proj_out]
+    return pl.pallas_call(
+        project_kernel,
+        out_shape=[block, block, shape(8, 2 * proj_in.shape[0])],
+        in_specs=[HBM] * 5,
+        out_specs=[VMEM] * 3,
+        scratch_shapes=[pltpu.SMEM(lengths.shape, jnp.int32)]
+        + [pltpu.VMEM(operand.shape, jnp.bfloat16) for operand in operands[1:]]
+        + [pltpu.SemaphoreType.DMA((chunks + 2, 2))],
+        compiler_params=pltpu.CompilerParams(vmem_limit_bytes=24 * 2**20),
+        name="project",
+    )(*[pltpu.with_memory_space_constraint(operand, pltpu.HBM) for operand in operands])
+
+
 def per_device(dp, tensor, activations, out_grads, proj_in, proj_out, lengths, query_ids):
-    examples, seq_len, hidden = activations.shape
+    examples, seq_len, _ = activations.shape
     rank = proj_in.shape[1]
     num = query_ids.shape[0]
-    chunks = 7 if hidden % (7 * 128) == 0 else 1
-    side = lax.axis_index("tensor") % 2
-    depth = lax.axis_index("dp")
-    place = jnp.stack([side, depth, jnp.int32(rank * seq_len)]).astype(jnp.int32)
-    pin_t, pout_t = proj_in.T, proj_out.T
-    keep, send = pl.pallas_call(
-        project_kernel,
-        out_shape=[shape(seq_len, 2 * rank)] * 2,
-        in_specs=[SMEM, SMEM, ANY, ANY, ANY, ANY],
-        out_specs=[VMEM, VMEM],
-        scratch_shapes=[
-            pltpu.VMEM(activations.shape, jnp.bfloat16),
-            pltpu.VMEM(out_grads.shape, jnp.bfloat16),
-            pltpu.VMEM(pin_t.shape, jnp.bfloat16),
-            pltpu.VMEM(pout_t.shape, jnp.bfloat16),
-            pltpu.SemaphoreType.DMA((chunks + 1, 2)),
-        ],
-        compiler_params=pltpu.CompilerParams(vmem_limit_bytes=24 * 2**20),
-        name="project",
-    )(place, lengths, activations, out_grads, pin_t, pout_t)
+    keep, send, live = project(activations, out_grads, proj_in.T, proj_out.T, lengths)
     total = keep + lax.ppermute(send, "tensor", mirror(tensor, 1))
     step = 2
     while 2 * step < tensor:
         total = total + lax.ppermute(total, "tensor", mirror(tensor, step))
         step *= 2
     other = lax.ppermute(total, "tensor", mirror(tensor, step)) if step < tensor else jnp.zeros_like(total)
-    packed = pl.pallas_call(
-        gram_kernel,
-        out_shape=shape(rank + 8, 2 * rank),
-        in_specs=[SMEM, SMEM, VMEM, VMEM],
-        out_specs=VMEM,
-        name="gram",
-    )(place, lengths, total, other)
+    packed = call(gram_kernel, "gram", shape(rank + 8, 2 * rank), live, total, other)
     if dp <= 4:
         packs = [packed] + [lax.ppermute(packed, "dp", mirror(dp, step)) for step in range(1, dp)]
     else:
-        gathered = lax.all_gather(packed, "dp", axis=0)[depth ^ jnp.arange(dp, dtype=jnp.int32)]
+        order = lax.axis_index("dp") ^ jnp.arange(dp, dtype=jnp.int32)
+        gathered = lax.all_gather(packed, "dp", axis=0)[order]
         packs = [gathered[n] for n in range(dp)]
-    summed, sketches = pl.pallas_call(
-        collect_kernel,
-        out_shape=[shape(rank + 8, 2 * rank), shape(dp // 2, rank, 2 * rank)],
-        in_specs=[VMEM] * dp,
-        out_specs=[VMEM, VMEM],
-        name="collect",
-    )(*packs)
+    results = [shape(rank + 8, 2 * rank), shape(dp // 2, rank, 2 * rank)]
+    summed, sketches = call(collect_kernel, "collect", results, *packs)
     summed_other = lax.ppermute(summed, "tensor", mirror(tensor, 1))
     sketches_other = lax.ppermute(sketches, "tensor", mirror(tensor, 1))
-    inverses = pl.pallas_call(
-        inverse_kernel,
-        out_shape=[shape(rank, rank), shape(rank, rank), shape(8, 128), shape(8, 128)],
-        in_specs=[VMEM, VMEM],
-        out_specs=[VMEM] * 4,
-        name="inverse",
-    )(summed, summed_other)
-    scores = pl.pallas_call(
-        score_kernel,
-        out_shape=shape(examples, num),
-        in_specs=[SMEM] + [VMEM] * 7,
-        out_specs=VMEM,
-        name="scores",
-    )(place, query_ids.reshape(1, num), sketches, sketches_other, *inverses)
+    results = [shape(rank, rank), shape(rank, rank), shape(8, 128), shape(8, 128)]
+    inverses = call(inverse_kernel, "inverse", results, summed, summed_other)
+    scores = call(
+        functools.partial(score_kernel, seq_len),
+        "scores",
+        shape(examples, num),
+        query_ids.reshape(1, num),
+        sketches,
+        sketches_other,
+        *inverses,
+    )
     return scores.T
 
 

time: 40.1 us -> 25.4 us (0.63)
  local copies, waits for them, and re-layouts: 9.15 us -> 0.57 us
  Pallas kernels: 13 us -> 7.54 us
  waiting for transfers between devices: 8.9 us -> 8.4 us
    unnamed x26 -> x3, local copies, waits for them, and re-layouts: 9.15 us -> 0.57 us
    pallas_call x5, Pallas kernels: 13 us -> 7.54 us  [the longest x1 4.4 us: project(): pl.pallas_call(project_kernel, out_shape=[block, block, shape(8, 2 * proj...]
where the time goes in v2:
time: 25.4 us; the launch traced here: 25.2 us
  starting transfers between devices  8.66 us (34%)
  waiting for transfers between devices  8.4 us (33%)
  Pallas kernels  7.54 us (30%)
  local copies, waits for them, and re-layouts  0.57 us (2%)
    ppermute x3, starting transfers between devices, per_device(): lax.ppermute(packed, 'dp', mirror(dp, step))  4.67 us
    pallas_call x1, Pallas kernels, project(): pl.pallas_call(project_kernel, out_shape=[block, block, shape(8, 2 * proj...  4.4 us
    ppermute x3, waiting for transfers between devices, per_device(): lax.ppermute(packed, 'dp', mirror(dp, step))  4.22 us
    pallas_call x4, Pallas kernels, call(): pl.pallas_call(kernel, out_shape=out_shape, in_specs=[VMEM] * len(operand...  3.14 us
    ppermute x1, starting transfers between devices, per_device(): lax.ppermute(total, 'tensor', mirror(tensor, step))  2.9 us
    ppermute x1, waiting for transfers between devices, per_device(): lax.ppermute(total, 'tensor', mirror(tensor, step))  2.41 us
    ppermute x1, waiting for transfers between devices, per_device(): total = keep + lax.ppermute(send, 'tensor', mirror(tensor, 1))  0.9 us
    ppermute x1, waiting for transfers between devices, per_device(): summed_other = lax.ppermute(summed, 'tensor', mirror(tensor, 1))  0.87 us
  transfers between devices with their start and end apart: 7, of which 5 were waited for; matrix products, arithmetic and copies ran while one was open for 0% of the time, Pallas kernels for 9%

profile of v2, /device:TPU:0, one launch (start us, length us, event | category | flops | bytes accessed | tf_op | source)
XLA Modules:
  0.0 25.2 jit_solution(1917376108334310719)
XLA Ops:
  0.0 0.0 copy-start
  0.0 4.4 %project.1 = (f32[128,128]{1,0:T(8,128)S(1)}, f32[128,128]{1,0:T(8,128)S(1)}, f32[8,128]{1,0:T(8,128)S(1)}) custom-call(s32[2]{0:T(128)} %lengths.1, bf16[2,128,7168]{2,1,0:T(8,128)(2,1)} %act.1, bf16[2,128,2048]{2,1,0:T(8,128)(2,1)} %grad.1, bf16[64,7168]{1,0:T(8,128)(2,1)} %bitcast.6, bf16[64,2048]{1,0:T(8,128)(2,1)} %bitcast.7), custom_call_target="tpu_custom_call" | custom-call | tf_op jit(solution)/shard_map/project/pallas_call | solution.py:199
  4.4 0.5 %collective-permute-start = (f32[128,128]{1,0:T(8,128)S(1)}, f32[128,128]{1,0:T(8,128)S(1)}, u32[]{:S(2)}, u32[]{:S(2)}) collective-permute-start(f32[128,128]{1,0:T(8,128)S(1)} %get-tuple-element.16), channel_id=1, source_target_pairs={{0,1},{1,0},{2,3},{3,2},{4,5},{5,4},{6,7},{7,6},{8,9},{9,8},{10,11... | collective-permute-start | bytes 196616 | tf_op jit(solution)/shard_map/ppermute | solution.py:217
  4.9 0.9 %collective-permute-done = f32[128,128]{1,0:T(8,128)S(1)} collective-permute-done((f32[128,128]{1,0:T(8,128)S(1)}, f32[128,128]{1,0:T(8,128)S(1)}, u32[]{:S(2)}, u32[]{:S(2)}) %collective-permute-start) | collective-permute-done | bytes 65568 | tf_op jit(solution)/shard_map/ppermute | solution.py:217
  5.8 2.9 %collective-permute-start.1 = (f32[128,128]{1,0:T(8,128)S(1)}, f32[128,128]{1,0:T(8,128)S(1)}, u32[]{:S(2)}, u32[]{:S(2)}) collective-permute-start(f32[128,128]{1,0:T(8,128)S(1)} %add.3.mine), channel_id=1, source_target_pairs={{0,2},{1,3},{2,0},{3,1},{4,6},{5,7},{6,4},{7,5},{8,10},{9,11},{10,... | collective-permute-start | bytes 196616 | tf_op jit(solution)/shard_map/ppermute | solution.py:222
  8.7 2.4 %collective-permute-done.1.theirs = f32[128,128]{1,0:T(8,128)S(1)} collective-permute-done((f32[128,128]{1,0:T(8,128)S(1)}, f32[128,128]{1,0:T(8,128)S(1)}, u32[]{:S(2)}, u32[]{:S(2)}) %collective-permute-start.1) | collective-permute-done | bytes 65568 | tf_op jit(solution)/shard_map/ppermute | solution.py:222
  11.2 0.3 %gram.1.refs_0_ = f32[72,128]{1,0:T(8,128)S(1)} custom-call(f32[8,128]{1,0:T(8,128)S(1)} %get-tuple-element.14.live, f32[128,128]{1,0:T(8,128)S(1)} %add.3.mine, f32[128,128]{1,0:T(8,128)S(1)} %collective-permute-done.1.theirs), custom_call_target="tpu_custom_call" | custom-call | tf_op jit(solution)/shard_map/gram/pallas_call | solution.py:180
  11.5 4.0 %collective-permute-start.4 = (f32[72,128]{1,0:T(8,128)S(1)}, f32[72,128]{1,0:T(8,128)S(1)}, u32[]{:S(2)}, u32[]{:S(2)}) collective-permute-start(f32[72,128]{1,0:T(8,128)S(1)} %gram.1.refs_0_), channel_id=1, source_target_pairs={{0,12},{4,8},{8,4},{12,0},{1,13},{5,9},{9,5},{13,1},{2,14},{6,10},... | collective-permute-start | bytes 110600 | tf_op jit(solution)/shard_map/ppermute | solution.py:225
  15.5 0.0 collective-permute-start.3
  15.5 0.6 %collective-permute-start.2 = (f32[72,128]{1,0:T(8,128)S(1)}, f32[72,128]{1,0:T(8,128)S(1)}, u32[]{:S(2)}, u32[]{:S(2)}) collective-permute-start(f32[72,128]{1,0:T(8,128)S(1)} %gram.1.refs_0_), channel_id=1, source_target_pairs={{0,4},{4,0},{8,12},{12,8},{1,5},{5,1},{9,13},{13,9},{2,6},{6,2},{1... | collective-permute-start | bytes 110600 | tf_op jit(solution)/shard_map/ppermute | solution.py:225
  16.2 1.5 %collective-permute-done.4.refs_3_ = f32[72,128]{1,0:T(8,128)S(1)} collective-permute-done((f32[72,128]{1,0:T(8,128)S(1)}, f32[72,128]{1,0:T(8,128)S(1)}, u32[]{:S(2)}, u32[]{:S(2)}) %collective-permute-start.4) | collective-permute-done | bytes 36896 | tf_op jit(solution)/shard_map/ppermute | solution.py:225
  17.6 2.7 %collective-permute-done.3.refs_2_ = f32[72,128]{1,0:T(8,128)S(1)} collective-permute-done((f32[72,128]{1,0:T(8,128)S(1)}, f32[72,128]{1,0:T(8,128)S(1)}, u32[]{:S(2)}, u32[]{:S(2)}) %collective-permute-start.3) | collective-permute-done | bytes 36896 | tf_op jit(solution)/shard_map/ppermute | solution.py:225
  20.4 0.0 collective-permute-done.2.refs_1_
  20.4 0.1 collect.1
  20.5 0.1 collective-permute-start.5
  20.5 0.5 %collective-permute-start.6 = (f32[72,128]{1,0:T(8,128)S(1)}, f32[72,128]{1,0:T(8,128)S(1)}, u32[]{:S(2)}, u32[]{:S(2)}) collective-permute-start(f32[72,128]{1,0:T(8,128)S(1)} %get-tuple-element.18.mine), channel_id=1, source_target_pairs={{0,1},{1,0},{2,3},{3,2},{4,5},{5,4},{6,7},{7,6},{8,9},{9,8},{10,11... | collective-permute-start | bytes 110600 | tf_op jit(solution)/shard_map/ppermute | solution.py:232
  21.0 0.9 %collective-permute-done.6.theirs = f32[72,128]{1,0:T(8,128)S(1)} collective-permute-done((f32[72,128]{1,0:T(8,128)S(1)}, f32[72,128]{1,0:T(8,128)S(1)}, u32[]{:S(2)}, u32[]{:S(2)}) %collective-permute-start.6) | collective-permute-done | bytes 36896 | tf_op jit(solution)/shard_map/ppermute | solution.py:232
  21.9 2.2 %inverse.1 = (f32[64,64]{1,0:T(8,128)S(1)}, f32[64,64]{1,0:T(8,128)S(1)}, f32[8,128]{1,0:T(8,128)S(1)}, f32[8,128]{1,0:T(8,128)S(1)}) custom-call(f32[72,128]{1,0:T(8,128)S(1)} %get-tuple-element.18.mine, f32[72,128]{1,0:T(8,128)S(1)} %collective-permute-done.6.theirs), custom_call_target="tpu_custom_call" | custom-call | tf_op jit(solution)/shard_map/inverse/pallas_call | solution.py:180
  24.1 0.0 collective-permute-done.5.theirs
  24.1 0.0 copy-done
  24.1 0.6 %scores.1 = f32[2,64]{1,0:T(2,128)S(1)} custom-call(s32[1,64]{1,0:T(1,128)S(1)} %bitcast.5, f32[2,64,128]{2,1,0:T(8,128)S(1)} %get-tuple-element.17.mine, f32[2,64,128]{2,1,0:T(8,128)S(1)} %collective-permute-done.5.theirs, f32[64,64]{1,0:T(8,128)S(1)} %get-tuple-element.19.inv_out, f32[64,64]{1,0:T(8,128)S(1)} %get-tuple-element.20.inv_in, ...), custom_call_target="tpu_custom_call" | custom-call | tf_op jit(solution)/shard_map/scores/pallas_call | solution.py:180
  24.7 0.6 %copy.7 = f32[64,2]{0,1:T(2,128)} copy(f32[64,2]{0,1:T(2,128)S(1)} %bitcast.4) | data formatting | bytes 1024
  (1 shorter events, 0.0 us)
Async XLA Ops:
  0.0 24.1 %copy-start = (s32[64]{0:T(128)S(1)}, s32[64]{0:T(128)}, u32[]{:S(2)}) copy-start(s32[64]{0:T(128)} %param.11) | copy-start | bytes 772
  4.4 1.4 %collective-permute-start = (f32[128,128]{1,0:T(8,128)S(1)}, f32[128,128]{1,0:T(8,128)S(1)}, u32[]{:S(2)}, u32[]{:S(2)}) collective-permute-start(f32[128,128]{1,0:T(8,128)S(1)} %get-tuple-element.16), channel_id=1, source_target_pairs={{0,1},{1,0},{2,3},{3,2},{4,5},{5,4},{6,7},{7,6},{8,9},{9,8},{10,11... | collective-permute-start | bytes 196616 | tf_op jit(solution)/shard_map/ppermute | solution.py:217
  5.8 5.3 %collective-permute-start.1 = (f32[128,128]{1,0:T(8,128)S(1)}, f32[128,128]{1,0:T(8,128)S(1)}, u32[]{:S(2)}, u32[]{:S(2)}) collective-permute-start(f32[128,128]{1,0:T(8,128)S(1)} %add.3.mine), channel_id=1, source_target_pairs={{0,2},{1,3},{2,0},{3,1},{4,6},{5,7},{6,4},{7,5},{8,10},{9,11},{10,... | collective-permute-start | bytes 196616 | tf_op jit(solution)/shard_map/ppermute | solution.py:222
  11.5 6.1 %collective-permute-start.4 = (f32[72,128]{1,0:T(8,128)S(1)}, f32[72,128]{1,0:T(8,128)S(1)}, u32[]{:S(2)}, u32[]{:S(2)}) collective-permute-start(f32[72,128]{1,0:T(8,128)S(1)} %gram.1.refs_0_), channel_id=1, source_target_pairs={{0,12},{4,8},{8,4},{12,0},{1,13},{5,9},{9,5},{13,1},{2,14},{6,10},... | collective-permute-start | bytes 110600 | tf_op jit(solution)/shard_map/ppermute | solution.py:225
  15.5 4.9 %collective-permute-start.3 = (f32[72,128]{1,0:T(8,128)S(1)}, f32[72,128]{1,0:T(8,128)S(1)}, u32[]{:S(2)}, u32[]{:S(2)}) collective-permute-start(f32[72,128]{1,0:T(8,128)S(1)} %gram.1.refs_0_), channel_id=1, source_target_pairs={{0,8},{4,12},{8,0},{12,4},{1,9},{5,13},{9,1},{13,5},{2,10},{6,14},... | collective-permute-start | bytes 110600 | tf_op jit(solution)/shard_map/ppermute | solution.py:225
  15.5 4.9 %collective-permute-start.2 = (f32[72,128]{1,0:T(8,128)S(1)}, f32[72,128]{1,0:T(8,128)S(1)}, u32[]{:S(2)}, u32[]{:S(2)}) collective-permute-start(f32[72,128]{1,0:T(8,128)S(1)} %gram.1.refs_0_), channel_id=1, source_target_pairs={{0,4},{4,0},{8,12},{12,8},{1,5},{5,1},{9,13},{13,9},{2,6},{6,2},{1... | collective-permute-start | bytes 110600 | tf_op jit(solution)/shard_map/ppermute | solution.py:225
  20.5 3.6 %collective-permute-start.5 = (f32[2,64,128]{2,1,0:T(8,128)S(1)}, f32[2,64,128]{2,1,0:T(8,128)S(1)}, u32[]{:S(2)}, u32[]{:S(2)}) collective-permute-start(f32[2,64,128]{2,1,0:T(8,128)S(1)} %get-tuple-element.17.mine), channel_id=1, source_target_pairs={{0,1},{1,0},{2,3},{3,2},{4,5},{5,4},{6,7},{7,6},{8,9},{9,8},{10,11... | collective-permute-start | bytes 196616 | tf_op jit(solution)/shard_map/ppermute | solution.py:233
  20.5 1.4 %collective-permute-start.6 = (f32[72,128]{1,0:T(8,128)S(1)}, f32[72,128]{1,0:T(8,128)S(1)}, u32[]{:S(2)}, u32[]{:S(2)}) collective-permute-start(f32[72,128]{1,0:T(8,128)S(1)} %get-tuple-element.18.mine), channel_id=1, source_target_pairs={{0,1},{1,0},{2,3},{3,2},{4,5},{5,4},{6,7},{7,6},{8,9},{9,8},{10,11... | collective-permute-start | bytes 110600 | tf_op jit(solution)/shard_map/ppermute | solution.py:232

commit v3 on v2

v3 whole, which is shorter than its diff:
```python
import functools

import jax
import jax.numpy as jnp
from jax import lax
from jax.experimental import pallas as pl
from jax.experimental.pallas import tpu as pltpu
from jax.sharding import PartitionSpec as P

HIGH = lax.Precision.HIGHEST
VMEM = pl.BlockSpec(memory_space=pltpu.VMEM)
HBM = pl.BlockSpec(memory_space=pltpu.HBM)
DAMP = 0.1


def dot_nt(a, b):
    return lax.dot_general(a, b, (((1,), (1,)), ((), ())), preferred_element_type=jnp.float32)


def dot_hi(a, b):
    return jnp.dot(a, b, precision=HIGH, preferred_element_type=jnp.float32)


def project_kernel(lengths, act, grad, proj_in, proj_out, sketch, live, len_s, act_v, grad_v, pin_v, pout_v, sems):
    chunks = sems.shape[0] - 2
    width = act.shape[2] // chunks
    copies = []

    def begin(src, dst, slot):
        copy = pltpu.make_async_copy(src, dst, sems.at[slot, len(copies) % 2])
        copy.start()
        copies.append(copy)

    begin(proj_out, pout_v, 0)
    begin(grad, grad_v, 0)
    begin(lengths, len_s, chunks + 1)
    for n in range(chunks):
        span = pl.ds(n * width, width)
        begin(proj_in.at[:, span], pin_v.at[:, span], n + 1)
        begin(act.at[:, :, span], act_v.at[:, :, span], n + 1)
    examples, seq_len, _ = act.shape
    rank = proj_in.shape[0]
    copies[0].wait()
    copies[1].wait()
    out_part = dot_nt(grad_v[...].reshape(examples * seq_len, -1), pout_v[...])
    in_part = jnp.zeros((examples * seq_len, rank), jnp.float32)
    for n in range(chunks):
        copies[2 * n + 3].wait()
        copies[2 * n + 4].wait()
        span = pl.ds(n * width, width)
        in_part += dot_nt(act_v[:, :, span].reshape(examples * seq_len, width), pin_v[:, span])
    both = jnp.concatenate([out_part, in_part], axis=1)
    token = lax.broadcasted_iota(jnp.int32, (seq_len, 2 * rank), 0)
    copies[2].wait()
    count = jnp.int32(0)
    for e in range(examples):
        rows = pl.ds(e * seq_len, seq_len)
        sketch[rows] = jnp.where(token < len_s[e], both[e * seq_len : (e + 1) * seq_len], 0.0)
        count += len_s[e]
    live[...] = jnp.full(live.shape, count.astype(jnp.float32))


def gram_kernel(seq_len, leads, live, mine, theirs, packed):
    rank = mine.shape[1] // 2

    @pl.when(leads())
    def _():
        tokens = mine[...] + theirs[...]
        grams = []
        for e in range(2):
            block = tokens[e * seq_len : (e + 1) * seq_len]
            grams.append(
                lax.dot_general(
                    block, block, (((0,), (0,)), ((), ())), precision=HIGH, preferred_element_type=jnp.float32
                )
            )
        total = grams[0] + grams[1]
        low = total[rank:]
        row = lax.broadcasted_iota(jnp.int32, (rank, 2 * rank), 0)
        lane = lax.broadcasted_iota(jnp.int32, (rank, 2 * rank), 1)
        mixed = jnp.where(lane <= row, total[:rank], pltpu.roll(low, rank, 1))
        packed[:rank] = jnp.where(lane < rank, mixed, grams[0][:rank])
        half = rank // 2
        folded = pltpu.roll(grams[1][half:rank], rank, 1)
        packed[rank : rank + half] = jnp.where(lane[:half] < rank, folded, grams[1][:half])
        diag = jnp.sum(jnp.where(lane == rank + row, low, 0.0), axis=0, keepdims=True)
        diag = pltpu.roll(jnp.broadcast_to(diag, (8, 2 * rank)), rank, 1)
        packed[rank + half :] = jnp.where(lane[:8] < rank, diag, live[...])


def unfold(top, folded):
    rank = top.shape[0]
    lane = lax.broadcasted_iota(jnp.int32, top.shape, 1)
    return jnp.where(lane < rank, jnp.concatenate([pltpu.roll(folded, rank, 1), folded], axis=0), top)


def merge_kernel(leads, mine, theirs, merged):
    rank = mine.shape[1] // 2
    half = rank // 2

    @pl.when(leads())
    def _():
        top, other = mine[:rank], theirs[:rank]
        lane = lax.broadcasted_iota(jnp.int32, top.shape, 1)
        merged[:rank] = jnp.where(lane < rank, top + other, top)
        merged[rank : rank + half] = mine[rank : rank + half]
        merged[rank + half : rank + half + 8] = mine[rank + half :] + theirs[rank + half :]
        merged[rank + half + 8 :] = unfold(other, theirs[rank : rank + half])


def inverse_steps(rank):
    least = 2.0 * (DAMP / rank) / (1.0 + 2.0 * DAMP / rank)
    scales = []
    while (1.0 - least) ** 2 > 1e-7:
        image = least * (2.0 - least)
        scales.append(2.0 / (1.0 + image))
        least = scales[-1] * image
    return scales + [1.0]


def inverses(rank, total):
    mixed = total[:rank, :rank]
    turned = mixed.T
    tail = rank + rank // 2
    diag = total[tail : tail + 1, :rank]
    count = total[tail : tail + 1, rank : rank + 1]
    row = lax.broadcasted_iota(jnp.int32, (rank, rank), 0)
    lane = lax.broadcasted_iota(jnp.int32, (rank, rank), 1)
    eye = row == lane
    sum_out = jnp.where(lane <= row, mixed, turned)
    sum_in = jnp.where(lane > row, mixed, jnp.where(eye, diag, turned))
    factor = 2.0 / (1.0 + 2.0 * DAMP / rank)

    def start(sums):
        trace = jnp.sum(jnp.sum(jnp.where(eye, sums, 0.0), axis=0, keepdims=True), axis=1, keepdims=True)
        return sums * (factor / trace) + jnp.where(eye, factor * DAMP / rank, 0.0), factor * count / trace

    t_out, c_out = start(sum_out)
    t_in, c_in = start(sum_in)
    steps = inverse_steps(rank)
    two_eye = jnp.where(eye, 2.0, 0.0)
    x_out = steps[0] * (two_eye - t_out)
    x_in = steps[0] * (two_eye - t_in)
    t_out = steps[0] * (2.0 * t_out - dot_hi(t_out, t_out))
    t_in = steps[0] * (2.0 * t_in - dot_hi(t_in, t_in))
    for n, scale in enumerate(steps[1:]):
        x_out, x_in, p_out, p_in = (
            scale * (2.0 * x_out - dot_hi(x_out, t_out)),
            scale * (2.0 * x_in - dot_hi(x_in, t_in)),
            t_out,
            t_in,
        )
        if n < len(steps) - 2:
            t_out = scale * (2.0 * p_out - dot_hi(p_out, p_out))
            t_in = scale * (2.0 * p_in - dot_hi(p_in, p_in))
    return x_out, x_in, c_out, c_in


def finish_kernel(seq_len, leads, masks, queries, *refs):
    packs, scores = refs[:-1], refs[-1]
    rank = packs[0].shape[1] // 2
    fixed = rank + rank // 2 + 8

    @pl.when(leads())
    def _():
        total = [ref[:fixed] for ref in packs]
        while len(total) > 1:
            total = [total[n] + total[n + 1] for n in range(0, len(total), 2)]
        inv_out, inv_in, c_out, c_in = inverses(rank, total[0])
        pairs = []
        for ref in packs:
            pairs.append(unfold(ref[:rank], ref[rank : rank + rank // 2]))
            if ref.shape[0] > fixed:
                pairs.append(ref[fixed:])
        left = dot_hi(inv_out, pairs[0]) * c_out
        zero = jnp.zeros((rank, rank), jnp.float32)
        right = jnp.concatenate(
            [jnp.concatenate([inv_in, zero], axis=1), jnp.concatenate([zero, inv_in], axis=1)], axis=0
        )
        straight = dot_hi(left, right) * c_in
        crossed = pltpu.roll(straight, rank, 1)
        count = len(pairs)
        sums = [jnp.sum(pair * straight, axis=0, keepdims=True) for pair in pairs]
        sums += [jnp.sum(pair * crossed, axis=0, keepdims=True) for pair in pairs]
        sums = jnp.concatenate(sums, axis=0)
        num = queries.shape[1]
        index = lax.broadcasted_iota(jnp.int32, (2 * count, num), 0) % count
        mask = sum(jnp.where(index == n, value, 0) for n, value in enumerate(masks))
        device = lax.axis_index("dp") ^ mask
        chosen = queries[...]
        second = jnp.where(chosen == 2 * device + 1, jnp.sum(sums[:, :rank], axis=1, keepdims=True), 0.0)
        first = jnp.where(chosen == 2 * device, jnp.sum(sums[:, rank:], axis=1, keepdims=True), 0.0)
        scale = 1.0 / (rank * seq_len)
        scores[0:1, :] = scale * jnp.sum(
            jnp.concatenate([first[:count], second[count:]], axis=0), axis=0, keepdims=True
        )
        scores[1:2, :] = scale * jnp.sum(
            jnp.concatenate([second[:count], first[count:]], axis=0), axis=0, keepdims=True
        )


def shape(*dims):
    return pltpu.VMEM(dims, jnp.float32)


def call(kernel, name, out_shape, *operands):
    return pl.pallas_call(
        kernel,
        out_shape=out_shape,
        in_specs=[VMEM] * len(operands),
        out_specs=VMEM,
        compiler_params=pltpu.CompilerParams(vmem_limit_bytes=4 * 2**20),
        name=name,
    )(*[pltpu.with_memory_space_constraint(operand, pltpu.VMEM) for operand in operands])


def project(activations, out_grads, proj_in, proj_out, lengths):
    examples, seq_len, hidden = activations.shape
    chunks = 7 if hidden % (7 * 128) == 0 else 1
    width = 2 * proj_in.shape[0]
    operands = [lengths, activations, out_grads, proj_in, proj_out]
    return pl.pallas_call(
        project_kernel,
        out_shape=[shape(examples * seq_len, width), shape(8, width)],
        in_specs=[HBM] * 5,
        out_specs=[VMEM] * 2,
        scratch_shapes=[pltpu.SMEM(lengths.shape, jnp.int32)]
        + [pltpu.VMEM(operand.shape, jnp.bfloat16) for operand in operands[1:]]
        + [pltpu.SemaphoreType.DMA((chunks + 2, 2))],
        compiler_params=pltpu.CompilerParams(vmem_limit_bytes=24 * 2**20),
        name="project",
    )(*[pltpu.with_memory_space_constraint(operand, pltpu.HBM) for operand in operands])


def swap(x, dp, tensor, far, near):
    pairs = []
    for d in range(dp):
        for t in range(tensor):
            masks = far if t % 2 else near
            pairs.append((d * tensor + t, (d ^ masks[0]) * tensor + (t ^ masks[1])))
    return lax.ppermute(x, ("dp", "tensor"), pairs)


def per_device(dp, tensor, activations, out_grads, proj_in, proj_out, lengths, query_ids):
    examples, seq_len, _ = activations.shape
    rank = proj_in.shape[1]
    num = query_ids.shape[0]
    paired = dp == 4 and tensor == 4
    odd = lambda: lax.rem(lax.axis_index("tensor"), 2) == 1
    leads = odd if paired else lambda: True
    sketch, live = project(activations, out_grads, proj_in.T, proj_out.T, lengths)
    sketch = sketch + lax.ppermute(sketch, "tensor", [(t, t ^ 1) for t in range(tensor)])
    if paired:
        other = swap(sketch, dp, tensor, (0, 2), (1, 0))
    else:
        other = jnp.zeros_like(sketch)
        step = 2
        while step < tensor:
            sketch = sketch + lax.ppermute(sketch, "tensor", [(t, t ^ step) for t in range(tensor)])
            step *= 2
    packed = call(
        functools.partial(gram_kernel, seq_len, leads),
        "gram",
        shape(rank + rank // 2 + 8, 2 * rank),
        live,
        sketch,
        other,
    )
    if paired:
        other = swap(packed, dp, tensor, (2, 0), (0, 2))
        rows = 2 * rank + rank // 2 + 8
        merged = call(functools.partial(merge_kernel, leads), "merge", shape(rows, 2 * rank), packed, other)
        packs = [merged, swap(merged, dp, tensor, (1, 0), (0, 2))]
        masks = [0, 2, 1, 3]
    else:
        masks = list(range(dp))
        order = lax.axis_index("dp") ^ jnp.arange(dp, dtype=jnp.int32)
        gathered = lax.all_gather(packed, "dp", axis=0)[order]
        packs = [gathered[n] for n in range(dp)]
    scores = call(
        functools.partial(finish_kernel, seq_len, leads, masks),
        "finish",
        shape(examples, num),
        query_ids.reshape(1, num),
        *packs,
    )
    if paired:
        other = lax.ppermute(scores, "tensor", [(t, t ^ 1) for t in range(tensor)])
        scores = jnp.where(odd(), scores, other)
    return scores.T


def solution(mesh):
    placed = (
        P(("groups", "dp"), None, "tensor"),
        P(("groups", "dp"), None, "tensor"),
        P("tensor", None),
        P("tensor", None),
        P(("groups", "dp")),
        P("groups"),
    )
    return jax.shard_map(
        functools.partial(per_device, mesh.shape["dp"], mesh.shape["tensor"]),
        mesh=mesh,
        in_specs=placed,
        out_specs=P(None, ("groups", "dp")),
        check_vma=False,
    )
```

time: 25.4 us -> 23.4 us (0.921)
  Pallas kernels: 7.54 us -> 4.39 us
  waiting for transfers between devices: 8.4 us -> 9.51 us
  other arithmetic: 0.01 us -> 0.58 us
  local copies, waits for them, and re-layouts: 0.57 us -> 0.01 us
    pallas_call x4 -> x3, Pallas kernels: 3.14 us -> 0.01 us  [call(): pl.pallas_call(kernel, out_shape=out_shape, in_specs=[VMEM] * len(operand...]
    ppermute x7 -> x5, waiting for transfers between devices: 8.4 us -> 9.51 us  [the longest x3 7.7 us: swap(): return lax.ppermute(x, ('dp', 'tensor'), pairs)]
    unnamed x3 -> x2, local copies, waits for them, and re-layouts: 0.57 us -> 0.01 us
    transpose x0 -> x1, other arithmetic: none -> 0.56 us  [per_device(): return scores.T]
    ppermute x7 -> x5, starting transfers between devices: 8.66 us -> 8.77 us  [the longest x3 6.86 us: swap(): return lax.ppermute(x, ('dp', 'tensor'), pairs)]
  transfers between devices with their start and end apart: 7 -> 5, of which waited for: 5 -> 5; matrix products, arithmetic and copies ran while one was open for 0% -> 0% of each run, Pallas kernels for 9% -> 0%
where the time goes in v3:
time: 23.4 us; the launch traced here: 23.3 us
  waiting for transfers between devices  9.51 us (41%)
  starting transfers between devices  8.77 us (37%)
  Pallas kernels  4.39 us (19%)
  other arithmetic  0.58 us (2%)
    ppermute x3, waiting for transfers between devices, swap(): return lax.ppermute(x, ('dp', 'tensor'), pairs)  7.7 us
    ppermute x3, starting transfers between devices, swap(): return lax.ppermute(x, ('dp', 'tensor'), pairs)  6.86 us
    pallas_call x1, Pallas kernels, project(): pl.pallas_call(project_kernel, out_shape=[shape(examples * seq_len, width...  4.39 us
    ppermute x1, starting transfers between devices, per_device(): other = lax.ppermute(scores, 'tensor', [(t, t ^ 1) for t in range(tensor)])  1.39 us
    ppermute x1, waiting for transfers between devices, per_device(): lax.ppermute(sketch, 'tensor', [(t, t ^ 1) for t in range(tensor)])  0.99 us
    ppermute x1, waiting for transfers between devices, per_device(): other = lax.ppermute(scores, 'tensor', [(t, t ^ 1) for t in range(tensor)])  0.82 us
    transpose x1, other arithmetic, per_device(): return scores.T  0.56 us
    ppermute x1, starting transfers between devices, per_device(): lax.ppermute(sketch, 'tensor', [(t, t ^ 1) for t in range(tensor)])  0.52 us
  transfers between devices with their start and end apart: 5, of which 5 were waited for; matrix products, arithmetic and copies ran while one was open for 0% of the time, Pallas kernels for 0%

profile of v3, /device:TPU:0, one launch (start us, length us, event | category | flops | bytes accessed | tf_op | source)
XLA Modules:
  0.0 23.3 jit_solution(10316887612099647623)
XLA Ops:
  0.0 0.0 copy-start
  0.0 4.4 %project.1 = (f32[256,128]{1,0:T(8,128)S(1)}, f32[8,128]{1,0:T(8,128)S(1)}) custom-call(s32[2]{0:T(128)} %lengths.1, bf16[2,128,7168]{2,1,0:T(8,128)(2,1)} %act.1, bf16[2,128,2048]{2,1,0:T(8,128)(2,1)} %grad.1, bf16[64,7168]{1,0:T(8,128)(2,1)} %bitcast.6, bf16[64,2048]{1,0:T(8,128)(2,1)} %bitcast.7), custom_call_target="tpu_custom_call" | custom-call | tf_op jit(solution)/shard_map/project/pallas_call | solution.py:222
  4.4 0.5 %collective-permute-start = (f32[256,128]{1,0:T(8,128)S(1)}, f32[256,128]{1,0:T(8,128)S(1)}, u32[]{:S(2)}, u32[]{:S(2)}) collective-permute-start(f32[256,128]{1,0:T(8,128)S(1)} %get-tuple-element.8), channel_id=1, source_target_pairs={{0,1},{1,0},{2,3},{3,2},{4,5},{5,4},{6,7},{7,6},{8,9},{9,8},{10,11... | collective-permute-start | bytes 393224 | tf_op jit(solution)/shard_map/ppermute | solution.py:252
  4.9 1.0 %collective-permute-done = f32[256,128]{1,0:T(8,128)S(1)} collective-permute-done((f32[256,128]{1,0:T(8,128)S(1)}, f32[256,128]{1,0:T(8,128)S(1)}, u32[]{:S(2)}, u32[]{:S(2)}) %collective-permute-start) | collective-permute-done | bytes 131104 | tf_op jit(solution)/shard_map/ppermute | solution.py:252
  5.9 3.0 %collective-permute-start.1 = (f32[256,128]{1,0:T(8,128)S(1)}, f32[256,128]{1,0:T(8,128)S(1)}, u32[]{:S(2)}, u32[]{:S(2)}) collective-permute-start(f32[256,128]{1,0:T(8,128)S(1)} %add.3.mine), channel_id=1, source_target_pairs={{0,4},{1,3},{2,6},{3,1},{4,0},{5,7},{6,2},{7,5},{8,12},{9,11},{10,... | collective-permute-start | bytes 393224 | tf_op jit(solution)/shard_map/ppermute | solution.py:241
  8.9 2.9 %collective-permute-done.1.theirs = f32[256,128]{1,0:T(8,128)S(1)} collective-permute-done((f32[256,128]{1,0:T(8,128)S(1)}, f32[256,128]{1,0:T(8,128)S(1)}, u32[]{:S(2)}, u32[]{:S(2)}) %collective-permute-start.1) | collective-permute-done | bytes 131104 | tf_op jit(solution)/shard_map/ppermute | solution.py:241
  11.9 1.9 %collective-permute-start.2 = (f32[104,128]{1,0:T(8,128)S(1)}, f32[104,128]{1,0:T(8,128)S(1)}, u32[]{:S(2)}, u32[]{:S(2)}) collective-permute-start(f32[104,128]{1,0:T(8,128)S(1)} %gram.1.mine), channel_id=1, source_target_pairs={{0,2},{1,9},{2,0},{3,11},{4,6},{5,13},{6,4},{7,15},{8,10},{9,1},{1... | collective-permute-start | bytes 159752 | tf_op jit(solution)/shard_map/ppermute | solution.py:241
  13.8 2.2 %collective-permute-done.2.theirs = f32[104,128]{1,0:T(8,128)S(1)} collective-permute-done((f32[104,128]{1,0:T(8,128)S(1)}, f32[104,128]{1,0:T(8,128)S(1)}, u32[]{:S(2)}, u32[]{:S(2)}) %collective-permute-start.2) | collective-permute-done | bytes 53280 | tf_op jit(solution)/shard_map/ppermute | solution.py:241
  16.0 1.9 %collective-permute-start.3 = (f32[168,128]{1,0:T(8,128)S(1)}, f32[168,128]{1,0:T(8,128)S(1)}, u32[]{:S(2)}, u32[]{:S(2)}) collective-permute-start(f32[168,128]{1,0:T(8,128)S(1)} %merge.1.refs_0_), channel_id=1, source_target_pairs={{0,2},{1,5},{2,0},{3,7},{4,6},{5,1},{6,4},{7,3},{8,10},{9,13},{10,... | collective-permute-start | bytes 258056 | tf_op jit(solution)/shard_map/ppermute | solution.py:241
  17.9 2.6 %collective-permute-done.3.refs_1_ = f32[168,128]{1,0:T(8,128)S(1)} collective-permute-done((f32[168,128]{1,0:T(8,128)S(1)}, f32[168,128]{1,0:T(8,128)S(1)}, u32[]{:S(2)}, u32[]{:S(2)}) %collective-permute-start.3) | collective-permute-done | bytes 86048 | tf_op jit(solution)/shard_map/ppermute | solution.py:241
  20.5 0.0 copy-done
  20.5 1.4 %collective-permute-start.4 = (f32[2,64]{1,0:T(2,128)S(1)}, f32[2,64]{1,0:T(2,128)S(1)}, u32[]{:S(2)}, u32[]{:S(2)}) collective-permute-start(f32[2,64]{1,0:T(2,128)S(1)} %finish.1), channel_id=1, source_target_pairs={{0,1},{1,0},{2,3},{3,2},{4,5},{5,4},{6,7},{7,6},{8,9},{9,8},{10,11... | collective-permute-start | bytes 1544 | tf_op jit(solution)/shard_map/ppermute | solution.py:288
  21.9 0.8 %collective-permute-done.4 = f32[2,64]{1,0:T(2,128)S(1)} collective-permute-done((f32[2,64]{1,0:T(2,128)S(1)}, f32[2,64]{1,0:T(2,128)S(1)}, u32[]{:S(2)}, u32[]{:S(2)}) %collective-permute-start.4) | collective-permute-done | bytes 544 | tf_op jit(solution)/shard_map/ppermute | solution.py:288
  22.7 0.6 %select_bitcast_fusion = f32[64,2]{0,1:T(2,128)} fusion(f32[2,64]{1,0:T(2,128)S(1)} %finish.1, f32[2,64]{1,0:T(2,128)S(1)} %collective-permute-done.4, pred[]{:T(512)S(6)} %eq.3), kind=kLoop, calls=%fused_computation | loop fusion | flops 128 | bytes 1537 | tf_op jit(solution)/shard_map/transpose | solution.py:290
  (4 shorter events, 0.0 us)
Async XLA Ops:
  0.0 20.5 %copy-start = (s32[64]{0:T(128)S(1)}, s32[64]{0:T(128)}, u32[]{:S(2)}) copy-start(s32[64]{0:T(128)} %param.11) | copy-start | bytes 772
  4.4 1.5 %collective-permute-start = (f32[256,128]{1,0:T(8,128)S(1)}, f32[256,128]{1,0:T(8,128)S(1)}, u32[]{:S(2)}, u32[]{:S(2)}) collective-permute-start(f32[256,128]{1,0:T(8,128)S(1)} %get-tuple-element.8), channel_id=1, source_target_pairs={{0,1},{1,0},{2,3},{3,2},{4,5},{5,4},{6,7},{7,6},{8,9},{9,8},{10,11... | collective-permute-start | bytes 393224 | tf_op jit(solution)/shard_map/ppermute | solution.py:252
  5.9 5.9 %collective-permute-start.1 = (f32[256,128]{1,0:T(8,128)S(1)}, f32[256,128]{1,0:T(8,128)S(1)}, u32[]{:S(2)}, u32[]{:S(2)}) collective-permute-start(f32[256,128]{1,0:T(8,128)S(1)} %add.3.mine), channel_id=1, source_target_pairs={{0,4},{1,3},{2,6},{3,1},{4,0},{5,7},{6,2},{7,5},{8,12},{9,11},{10,... | collective-permute-start | bytes 393224 | tf_op jit(solution)/shard_map/ppermute | solution.py:241
  11.9 4.1 %collective-permute-start.2 = (f32[104,128]{1,0:T(8,128)S(1)}, f32[104,128]{1,0:T(8,128)S(1)}, u32[]{:S(2)}, u32[]{:S(2)}) collective-permute-start(f32[104,128]{1,0:T(8,128)S(1)} %gram.1.mine), channel_id=1, source_target_pairs={{0,2},{1,9},{2,0},{3,11},{4,6},{5,13},{6,4},{7,15},{8,10},{9,1},{1... | collective-permute-start | bytes 159752 | tf_op jit(solution)/shard_map/ppermute | solution.py:241
  16.0 4.5 %collective-permute-start.3 = (f32[168,128]{1,0:T(8,128)S(1)}, f32[168,128]{1,0:T(8,128)S(1)}, u32[]{:S(2)}, u32[]{:S(2)}) collective-permute-start(f32[168,128]{1,0:T(8,128)S(1)} %merge.1.refs_0_), channel_id=1, source_target_pairs={{0,2},{1,5},{2,0},{3,7},{4,6},{5,1},{6,4},{7,3},{8,10},{9,13},{10,... | collective-permute-start | bytes 258056 | tf_op jit(solution)/shard_map/ppermute | solution.py:241
  20.5 2.2 %collective-permute-start.4 = (f32[2,64]{1,0:T(2,128)S(1)}, f32[2,64]{1,0:T(2,128)S(1)}, u32[]{:S(2)}, u32[]{:S(2)}) collective-permute-start(f32[2,64]{1,0:T(2,128)S(1)} %finish.1), channel_id=1, source_target_pairs={{0,1},{1,0},{2,3},{3,2},{4,5},{5,4},{6,7},{7,6},{8,9},{9,8},{10,11... | collective-permute-start | bytes 1544 | tf_op jit(solution)/shard_map/ppermute | solution.py:288

commit v4 on v3

--- a/solution.py
+++ b/solution.py
@@ -21,43 +21,54 @@
     return jnp.dot(a, b, precision=HIGH, preferred_element_type=jnp.float32)
 
 
-def project_kernel(lengths, act, grad, proj_in, proj_out, sketch, live, len_s, act_v, grad_v, pin_v, pout_v, sems):
-    chunks = sems.shape[0] - 2
-    width = act.shape[2] // chunks
+def project_kernel(lengths, act, grad, proj_in, proj_out, sketch, live, len_s, act_v, grad_v, pin_v, pout_v, out_v, in_v, sems):
+    examples, seq_len, hidden = act.shape
+    rank = proj_in.shape[0]
+    tokens = examples * seq_len
+    stages = sems.shape[0] // 2 - 1
+    width = hidden // (stages - 1)
     copies = []
 
-    def begin(src, dst, slot):
-        copy = pltpu.make_async_copy(src, dst, sems.at[slot, len(copies) % 2])
+    def begin(src, dst):
+        copy = pltpu.make_async_copy(src, dst, sems.at[len(copies)])
         copy.start()
         copies.append(copy)
 
-    begin(proj_out, pout_v, 0)
-    begin(grad, grad_v, 0)
-    begin(lengths, len_s, chunks + 1)
-    for n in range(chunks):
+    begin(proj_out, pout_v)
+    begin(grad, grad_v)
+    for n in range(stages - 1):
         span = pl.ds(n * width, width)
-        begin(proj_in.at[:, span], pin_v.at[:, span], n + 1)
-        begin(act.at[:, :, span], act_v.at[:, :, span], n + 1)
-    examples, seq_len, _ = act.shape
-    rank = proj_in.shape[0]
-    copies[0].wait()
-    copies[1].wait()
-    out_part = dot_nt(grad_v[...].reshape(examples * seq_len, -1), pout_v[...])
-    in_part = jnp.zeros((examples * seq_len, rank), jnp.float32)
-    for n in range(chunks):
-        copies[2 * n + 3].wait()
-        copies[2 * n + 4].wait()
-        span = pl.ds(n * width, width)
-        in_part += dot_nt(act_v[:, :, span].reshape(examples * seq_len, width), pin_v[:, span])
-    both = jnp.concatenate([out_part, in_part], axis=1)
-    token = lax.broadcasted_iota(jnp.int32, (seq_len, 2 * rank), 0)
-    copies[2].wait()
-    count = jnp.int32(0)
-    for e in range(examples):
-        rows = pl.ds(e * seq_len, seq_len)
-        sketch[rows] = jnp.where(token < len_s[e], both[e * seq_len : (e + 1) * seq_len], 0.0)
-        count += len_s[e]
-    live[...] = jnp.full(live.shape, count.astype(jnp.float32))
+        begin(proj_in.at[:, span], pin_v.at[:, span])
+        begin(act.at[:, :, span], act_v.at[:, :, span])
+    begin(lengths, len_s)
+
+    def stage(n):
+        copies[2 * n].wait()
+        copies[2 * n + 1].wait()
+        if n == 0:
+            out_v[...] = dot_nt(grad_v[...].reshape(tokens, -1), pout_v[...])
+            return
+        span = pl.ds((n - 1) * width, width)
+        in_part = dot_nt(act_v[:, :, span].reshape(tokens, width), pin_v[:, span])
+        if n > 1:
+            in_part += in_v[...]
+        if n < stages - 1:
+            in_v[...] = in_part
+            return
+        both = jnp.concatenate([out_v[...], in_part], axis=1)
+        token = lax.broadcasted_iota(jnp.int32, (seq_len, 2 * rank), 0)
+        copies[-1].wait()
+        count = jnp.int32(0)
+        for e in range(examples):
+            rows = pl.ds(e * seq_len, seq_len)
+            sketch[rows] = jnp.where(token < len_s[e], both[e * seq_len : (e + 1) * seq_len], 0.0)
+            count += len_s[e]
+        live[...] = jnp.full(live.shape, count.astype(jnp.float32))
+
+    @pl.loop(0, stages)
+    def _(turn):
+        for n in range(stages):
+            pl.when(turn == n)(functools.partial(stage, n))
 
 
 def gram_kernel(seq_len, leads, live, mine, theirs, packed):
@@ -216,17 +227,18 @@
 
 def project(activations, out_grads, proj_in, proj_out, lengths):
     examples, seq_len, hidden = activations.shape
-    chunks = 7 if hidden % (7 * 128) == 0 else 1
-    width = 2 * proj_in.shape[0]
+    rank = proj_in.shape[0]
+    stages = 3 if hidden % 256 == 0 else 2
     operands = [lengths, activations, out_grads, proj_in, proj_out]
     return pl.pallas_call(
         project_kernel,
-        out_shape=[shape(examples * seq_len, width), shape(8, width)],
+        out_shape=[shape(examples * seq_len, 2 * rank), shape(8, 2 * rank)],
         in_specs=[HBM] * 5,
         out_specs=[VMEM] * 2,
         scratch_shapes=[pltpu.SMEM(lengths.shape, jnp.int32)]
         + [pltpu.VMEM(operand.shape, jnp.bfloat16) for operand in operands[1:]]
-        + [pltpu.SemaphoreType.DMA((chunks + 2, 2))],
+        + [pltpu.VMEM((examples * seq_len, rank), jnp.float32)] * 2
+        + [pltpu.SemaphoreType.DMA((2 * stages + 2,))],
         compiler_params=pltpu.CompilerParams(vmem_limit_bytes=24 * 2**20),
         name="project",
     )(*[pltpu.with_memory_space_constraint(operand, pltpu.HBM) for operand in operands])

time: 23.4 us -> 22.6 us (0.966)
  Pallas kernels: 4.39 us -> 3.54 us
    pallas_call x1, Pallas kernels: 4.39 us -> 3.54 us  [project(): pl.pallas_call(project_kernel, out_shape=[shape(examples * seq_len, 2 * r...]
where the time goes in v4:
time: 22.6 us; the launch traced here: 22.4 us
  waiting for transfers between devices  9.5 us (42%)
  starting transfers between devices  8.77 us (39%)
  Pallas kernels  3.54 us (16%)
  other arithmetic  0.58 us (3%)
    ppermute x3, waiting for transfers between devices, swap(): return lax.ppermute(x, ('dp', 'tensor'), pairs)  7.69 us
    ppermute x3, starting transfers between devices, swap(): return lax.ppermute(x, ('dp', 'tensor'), pairs)  6.87 us
    pallas_call x1, Pallas kernels, project(): pl.pallas_call(project_kernel, out_shape=[shape(examples * seq_len, 2 * r...  3.54 us
    ppermute x1, starting transfers between devices, per_device(): other = lax.ppermute(scores, 'tensor', [(t, t ^ 1) for t in range(tensor)])  1.39 us
    ppermute x1, waiting for transfers between devices, per_device(): lax.ppermute(sketch, 'tensor', [(t, t ^ 1) for t in range(tensor)])  0.99 us
    ppermute x1, waiting for transfers between devices, per_device(): other = lax.ppermute(scores, 'tensor', [(t, t ^ 1) for t in range(tensor)])  0.82 us
    transpose x1, other arithmetic, per_device(): return scores.T  0.56 us
    ppermute x1, starting transfers between devices, per_device(): lax.ppermute(sketch, 'tensor', [(t, t ^ 1) for t in range(tensor)])  0.51 us
  transfers between devices with their start and end apart: 5, of which 5 were waited for; matrix products, arithmetic and copies ran while one was open for 0% of the time, Pallas kernels for 0%

profile of v4, /device:TPU:0, one launch (start us, length us, event | category | flops | bytes accessed | tf_op | source)
XLA Modules:
  0.0 22.4 jit_solution(9016275867474796005)
XLA Ops:
  0.0 0.0 copy-start
  0.0 3.5 %project.1 = (f32[256,128]{1,0:T(8,128)S(1)}, f32[8,128]{1,0:T(8,128)S(1)}) custom-call(s32[2]{0:T(128)} %lengths.1, bf16[2,128,7168]{2,1,0:T(8,128)(2,1)} %act.1, bf16[2,128,2048]{2,1,0:T(8,128)(2,1)} %grad.1, bf16[64,7168]{1,0:T(8,128)(2,1)} %bitcast.6, bf16[64,2048]{1,0:T(8,128)(2,1)} %bitcast.7), custom_call_target="tpu_custom_call" | custom-call | tf_op jit(solution)/shard_map/project/pallas_call | solution.py:233
  3.6 0.5 %collective-permute-start = (f32[256,128]{1,0:T(8,128)S(1)}, f32[256,128]{1,0:T(8,128)S(1)}, u32[]{:S(2)}, u32[]{:S(2)}) collective-permute-start(f32[256,128]{1,0:T(8,128)S(1)} %get-tuple-element.8), channel_id=1, source_target_pairs={{0,1},{1,0},{2,3},{3,2},{4,5},{5,4},{6,7},{7,6},{8,9},{9,8},{10,11... | collective-permute-start | bytes 393224 | tf_op jit(solution)/shard_map/ppermute | solution.py:264
  4.1 1.0 %collective-permute-done = f32[256,128]{1,0:T(8,128)S(1)} collective-permute-done((f32[256,128]{1,0:T(8,128)S(1)}, f32[256,128]{1,0:T(8,128)S(1)}, u32[]{:S(2)}, u32[]{:S(2)}) %collective-permute-start) | collective-permute-done | bytes 131104 | tf_op jit(solution)/shard_map/ppermute | solution.py:264
  5.1 3.0 %collective-permute-start.1 = (f32[256,128]{1,0:T(8,128)S(1)}, f32[256,128]{1,0:T(8,128)S(1)}, u32[]{:S(2)}, u32[]{:S(2)}) collective-permute-start(f32[256,128]{1,0:T(8,128)S(1)} %add.3.mine), channel_id=1, source_target_pairs={{0,4},{1,3},{2,6},{3,1},{4,0},{5,7},{6,2},{7,5},{8,12},{9,11},{10,... | collective-permute-start | bytes 393224 | tf_op jit(solution)/shard_map/ppermute | solution.py:253
  8.1 2.9 %collective-permute-done.1.theirs = f32[256,128]{1,0:T(8,128)S(1)} collective-permute-done((f32[256,128]{1,0:T(8,128)S(1)}, f32[256,128]{1,0:T(8,128)S(1)}, u32[]{:S(2)}, u32[]{:S(2)}) %collective-permute-start.1) | collective-permute-done | bytes 131104 | tf_op jit(solution)/shard_map/ppermute | solution.py:253
  11.0 1.9 %collective-permute-start.2 = (f32[104,128]{1,0:T(8,128)S(1)}, f32[104,128]{1,0:T(8,128)S(1)}, u32[]{:S(2)}, u32[]{:S(2)}) collective-permute-start(f32[104,128]{1,0:T(8,128)S(1)} %gram.1.mine), channel_id=1, source_target_pairs={{0,2},{1,9},{2,0},{3,11},{4,6},{5,13},{6,4},{7,15},{8,10},{9,1},{1... | collective-permute-start | bytes 159752 | tf_op jit(solution)/shard_map/ppermute | solution.py:253
  13.0 2.2 %collective-permute-done.2.theirs = f32[104,128]{1,0:T(8,128)S(1)} collective-permute-done((f32[104,128]{1,0:T(8,128)S(1)}, f32[104,128]{1,0:T(8,128)S(1)}, u32[]{:S(2)}, u32[]{:S(2)}) %collective-permute-start.2) | collective-permute-done | bytes 53280 | tf_op jit(solution)/shard_map/ppermute | solution.py:253
  15.2 1.9 %collective-permute-start.3 = (f32[168,128]{1,0:T(8,128)S(1)}, f32[168,128]{1,0:T(8,128)S(1)}, u32[]{:S(2)}, u32[]{:S(2)}) collective-permute-start(f32[168,128]{1,0:T(8,128)S(1)} %merge.1.refs_0_), channel_id=1, source_target_pairs={{0,2},{1,5},{2,0},{3,7},{4,6},{5,1},{6,4},{7,3},{8,10},{9,13},{10,... | collective-permute-start | bytes 258056 | tf_op jit(solution)/shard_map/ppermute | solution.py:253
  17.1 2.5 %collective-permute-done.3.refs_1_ = f32[168,128]{1,0:T(8,128)S(1)} collective-permute-done((f32[168,128]{1,0:T(8,128)S(1)}, f32[168,128]{1,0:T(8,128)S(1)}, u32[]{:S(2)}, u32[]{:S(2)}) %collective-permute-start.3) | collective-permute-done | bytes 86048 | tf_op jit(solution)/shard_map/ppermute | solution.py:253
  19.6 0.0 copy-done
  19.6 1.4 %collective-permute-start.4 = (f32[2,64]{1,0:T(2,128)S(1)}, f32[2,64]{1,0:T(2,128)S(1)}, u32[]{:S(2)}, u32[]{:S(2)}) collective-permute-start(f32[2,64]{1,0:T(2,128)S(1)} %finish.1), channel_id=1, source_target_pairs={{0,1},{1,0},{2,3},{3,2},{4,5},{5,4},{6,7},{7,6},{8,9},{9,8},{10,11... | collective-permute-start | bytes 1544 | tf_op jit(solution)/shard_map/ppermute | solution.py:300
  21.0 0.8 %collective-permute-done.4 = f32[2,64]{1,0:T(2,128)S(1)} collective-permute-done((f32[2,64]{1,0:T(2,128)S(1)}, f32[2,64]{1,0:T(2,128)S(1)}, u32[]{:S(2)}, u32[]{:S(2)}) %collective-permute-start.4) | collective-permute-done | bytes 544 | tf_op jit(solution)/shard_map/ppermute | solution.py:300
  21.9 0.6 %select_bitcast_fusion = f32[64,2]{0,1:T(2,128)} fusion(f32[2,64]{1,0:T(2,128)S(1)} %finish.1, f32[2,64]{1,0:T(2,128)S(1)} %collective-permute-done.4, pred[]{:T(512)S(6)} %eq.3), kind=kLoop, calls=%fused_computation | loop fusion | flops 128 | bytes 1537 | tf_op jit(solution)/shard_map/transpose | solution.py:302
  (4 shorter events, 0.0 us)
Async XLA Ops:
  0.0 19.6 %copy-start = (s32[64]{0:T(128)S(1)}, s32[64]{0:T(128)}, u32[]{:S(2)}) copy-start(s32[64]{0:T(128)} %param.11) | copy-start | bytes 772
  3.6 1.5 %collective-permute-start = (f32[256,128]{1,0:T(8,128)S(1)}, f32[256,128]{1,0:T(8,128)S(1)}, u32[]{:S(2)}, u32[]{:S(2)}) collective-permute-start(f32[256,128]{1,0:T(8,128)S(1)} %get-tuple-element.8), channel_id=1, source_target_pairs={{0,1},{1,0},{2,3},{3,2},{4,5},{5,4},{6,7},{7,6},{8,9},{9,8},{10,11... | collective-permute-start | bytes 393224 | tf_op jit(solution)/shard_map/ppermute | solution.py:264
  5.1 5.9 %collective-permute-start.1 = (f32[256,128]{1,0:T(8,128)S(1)}, f32[256,128]{1,0:T(8,128)S(1)}, u32[]{:S(2)}, u32[]{:S(2)}) collective-permute-start(f32[256,128]{1,0:T(8,128)S(1)} %add.3.mine), channel_id=1, source_target_pairs={{0,4},{1,3},{2,6},{3,1},{4,0},{5,7},{6,2},{7,5},{8,12},{9,11},{10,... | collective-permute-start | bytes 393224 | tf_op jit(solution)/shard_map/ppermute | solution.py:253
  11.0 4.1 %collective-permute-start.2 = (f32[104,128]{1,0:T(8,128)S(1)}, f32[104,128]{1,0:T(8,128)S(1)}, u32[]{:S(2)}, u32[]{:S(2)}) collective-permute-start(f32[104,128]{1,0:T(8,128)S(1)} %gram.1.mine), channel_id=1, source_target_pairs={{0,2},{1,9},{2,0},{3,11},{4,6},{5,13},{6,4},{7,15},{8,10},{9,1},{1... | collective-permute-start | bytes 159752 | tf_op jit(solution)/shard_map/ppermute | solution.py:253
  15.2 4.5 %collective-permute-start.3 = (f32[168,128]{1,0:T(8,128)S(1)}, f32[168,128]{1,0:T(8,128)S(1)}, u32[]{:S(2)}, u32[]{:S(2)}) collective-permute-start(f32[168,128]{1,0:T(8,128)S(1)} %merge.1.refs_0_), channel_id=1, source_target_pairs={{0,2},{1,5},{2,0},{3,7},{4,6},{5,1},{6,4},{7,3},{8,10},{9,13},{10,... | collective-permute-start | bytes 258056 | tf_op jit(solution)/shard_map/ppermute | solution.py:253
  19.6 2.2 %collective-permute-start.4 = (f32[2,64]{1,0:T(2,128)S(1)}, f32[2,64]{1,0:T(2,128)S(1)}, u32[]{:S(2)}, u32[]{:S(2)}) collective-permute-start(f32[2,64]{1,0:T(2,128)S(1)} %finish.1), channel_id=1, source_target_pairs={{0,1},{1,0},{2,3},{3,2},{4,5},{5,4},{6,7},{7,6},{8,9},{9,8},{10,11... | collective-permute-start | bytes 1544 | tf_op jit(solution)/shard_map/ppermute | solution.py:300

commit v5 on v4

--- a/solution.py
+++ b/solution.py
@@ -129,7 +129,7 @@
     return scales + [1.0]
 
 
-def inverses(rank, total):
+def scaled(rank, total):
     mixed = total[:rank, :rank]
     turned = mixed.T
     tail = rank + rank // 2
@@ -142,29 +142,28 @@
     sum_in = jnp.where(lane > row, mixed, jnp.where(eye, diag, turned))
     factor = 2.0 / (1.0 + 2.0 * DAMP / rank)
 
-    def start(sums):
+    def scale(sums):
         trace = jnp.sum(jnp.sum(jnp.where(eye, sums, 0.0), axis=0, keepdims=True), axis=1, keepdims=True)
         return sums * (factor / trace) + jnp.where(eye, factor * DAMP / rank, 0.0), factor * count / trace
 
-    t_out, c_out = start(sum_out)
-    t_in, c_in = start(sum_in)
+    return *scale(sum_out), *scale(sum_in), jnp.where(eye, 2.0, 0.0)
+
+
+def solve(rank, total, right):
+    t_out, c_out, t_in, c_in, two_eye = scaled(rank, total)
     steps = inverse_steps(rank)
-    two_eye = jnp.where(eye, 2.0, 0.0)
-    x_out = steps[0] * (two_eye - t_out)
     x_in = steps[0] * (two_eye - t_in)
-    t_out = steps[0] * (2.0 * t_out - dot_hi(t_out, t_out))
-    t_in = steps[0] * (2.0 * t_in - dot_hi(t_in, t_in))
-    for n, scale in enumerate(steps[1:]):
-        x_out, x_in, p_out, p_in = (
-            scale * (2.0 * x_out - dot_hi(x_out, t_out)),
-            scale * (2.0 * x_in - dot_hi(x_in, t_in)),
-            t_out,
-            t_in,
-        )
-        if n < len(steps) - 2:
+    for n, scale in enumerate(steps):
+        last = n == len(steps) - 1
+        p_out, p_in = t_out, t_in
+        right = scale * (2.0 * right - dot_hi(p_out, right))
+        if not last:
             t_out = scale * (2.0 * p_out - dot_hi(p_out, p_out))
+        if n > 0:
+            x_in = scale * (2.0 * x_in - dot_hi(x_in, p_in))
+        if not last:
             t_in = scale * (2.0 * p_in - dot_hi(p_in, p_in))
-    return x_out, x_in, c_out, c_in
+    return right, x_in, c_out, c_in
 
 
 def finish_kernel(seq_len, leads, masks, queries, *refs):
@@ -177,13 +176,13 @@
         total = [ref[:fixed] for ref in packs]
         while len(total) > 1:
             total = [total[n] + total[n + 1] for n in range(0, len(total), 2)]
-        inv_out, inv_in, c_out, c_in = inverses(rank, total[0])
         pairs = []
         for ref in packs:
             pairs.append(unfold(ref[:rank], ref[rank : rank + rank // 2]))
             if ref.shape[0] > fixed:
                 pairs.append(ref[fixed:])
-        left = dot_hi(inv_out, pairs[0]) * c_out
+        left, inv_in, c_out, c_in = solve(rank, total[0], pairs[0])
+        left = left * c_out
         zero = jnp.zeros((rank, rank), jnp.float32)
         right = jnp.concatenate(
             [jnp.concatenate([inv_in, zero], axis=1), jnp.concatenate([zero, inv_in], axis=1)], axis=0
@@ -210,6 +209,20 @@
         )
 
 
+def publish_kernel(scores, out, sem):
+    copy = pltpu.make_async_copy(scores, out, sem)
+    copy.start()
+    copy.wait()
+
+
+def replace_kernel(leads, theirs, mine, out, sem):
+    @pl.when(jnp.logical_not(leads()))
+    def _():
+        copy = pltpu.make_async_copy(theirs, out, sem)
+        copy.start()
+        copy.wait()
+
+
 def shape(*dims):
     return pltpu.VMEM(dims, jnp.float32)
 
@@ -253,6 +266,36 @@
     return lax.ppermute(x, ("dp", "tensor"), pairs)
 
 
+def across(x, tensor):
+    return lax.ppermute(x, "tensor", [(t, t ^ 1) for t in range(tensor)])
+
+
+def publish(scores):
+    return pl.pallas_call(
+        publish_kernel,
+        out_shape=jax.ShapeDtypeStruct(scores.shape, scores.dtype),
+        in_specs=[VMEM],
+        out_specs=HBM,
+        scratch_shapes=[pltpu.SemaphoreType.DMA],
+        compiler_params=pltpu.CompilerParams(vmem_limit_bytes=2**20),
+        cost_estimate=pl.CostEstimate(flops=10**9, bytes_accessed=0, transcendentals=0),
+        name="publish",
+    )(pltpu.with_memory_space_constraint(scores, pltpu.VMEM))
+
+
+def replace(theirs, mine, leads):
+    return pl.pallas_call(
+        functools.partial(replace_kernel, leads),
+        out_shape=jax.ShapeDtypeStruct(mine.shape, mine.dtype),
+        in_specs=[VMEM, HBM],
+        out_specs=HBM,
+        scratch_shapes=[pltpu.SemaphoreType.DMA],
+        input_output_aliases={1: 0},
+        compiler_params=pltpu.CompilerParams(vmem_limit_bytes=2**20),
+        name="replace",
+    )(pltpu.with_memory_space_constraint(theirs, pltpu.VMEM), mine)
+
+
 def per_device(dp, tensor, activations, out_grads, proj_in, proj_out, lengths, query_ids):
     examples, seq_len, _ = activations.shape
     rank = proj_in.shape[1]
@@ -261,7 +304,7 @@
     odd = lambda: lax.rem(lax.axis_index("tensor"), 2) == 1
     leads = odd if paired else lambda: True
     sketch, live = project(activations, out_grads, proj_in.T, proj_out.T, lengths)
-    sketch = sketch + lax.ppermute(sketch, "tensor", [(t, t ^ 1) for t in range(tensor)])
+    sketch = sketch + across(sketch, tensor)
     if paired:
         other = swap(sketch, dp, tensor, (0, 2), (1, 0))
     else:
@@ -297,8 +340,8 @@
         *packs,
     )
     if paired:
-        other = lax.ppermute(scores, "tensor", [(t, t ^ 1) for t in range(tensor)])
-        scores = jnp.where(odd(), scores, other)
+        other = across(scores, tensor)
+        scores = replace(other, publish(scores), leads)
     return scores.T
 
 

time: 22.6 us -> 22.3 us (0.987)
  Pallas kernels: 3.54 us -> 4.68 us
  waiting for transfers between devices: 9.5 us -> 8.92 us
  other arithmetic: 0.58 us -> 0.02 us
  starting transfers between devices: 8.77 us -> 8.47 us
    pallas_call x0 -> x2, Pallas kernels: none -> 1.14 us  [the longest x1 0.57 us: publish(): pl.pallas_call(publish_kernel, out_shape=jax.ShapeDtypeStruct(scores.shap...]
    ppermute x2, waiting for transfers between devices: 1.81 us -> 1.23 us  [across(): return lax.ppermute(x, 'tensor', [(t, t ^ 1) for t in range(tensor)])]
    transpose x1 -> x0, other arithmetic: 0.56 us -> none  [per_device(): return scores.T]
    ppermute x2, starting transfers between devices: 1.9 us -> 1.6 us  [across(): return lax.ppermute(x, 'tensor', [(t, t ^ 1) for t in range(tensor)])]
  transfers between devices with their start and end apart: 5 -> 5, of which waited for: 5 -> 5; matrix products, arithmetic and copies ran while one was open for 0% -> 0% of each run, Pallas kernels for 0% -> 3%
where the time goes in v5:
time: 22.3 us; the launch traced here: 22.1 us
  waiting for transfers between devices  8.92 us (40%)
  starting transfers between devices  8.47 us (38%)
  Pallas kernels  4.68 us (21%)
    ppermute x3, waiting for transfers between devices, swap(): return lax.ppermute(x, ('dp', 'tensor'), pairs)  7.69 us
    ppermute x3, starting transfers between devices, swap(): return lax.ppermute(x, ('dp', 'tensor'), pairs)  6.87 us
    pallas_call x1, Pallas kernels, project(): pl.pallas_call(project_kernel, out_shape=[shape(examples * seq_len, 2 * r...  3.54 us
    ppermute x2, starting transfers between devices, across(): return lax.ppermute(x, 'tensor', [(t, t ^ 1) for t in range(tensor)])  1.6 us
    ppermute x2, waiting for transfers between devices, across(): return lax.ppermute(x, 'tensor', [(t, t ^ 1) for t in range(tensor)])  1.23 us
    pallas_call x1, Pallas kernels, publish(): pl.pallas_call(publish_kernel, out_shape=jax.ShapeDtypeStruct(scores.shap...  0.57 us
    pallas_call x1, Pallas kernels, replace(): pl.pallas_call(functools.partial(replace_kernel, leads), out_shape=jax.Sh...  0.57 us
  transfers between devices with their start and end apart: 5, of which 5 were waited for; matrix products, arithmetic and copies ran while one was open for 0% of the time, Pallas kernels for 3%

profile of v5, /device:TPU:0, one launch (start us, length us, event | category | flops | bytes accessed | tf_op | source)
XLA Modules:
  0.0 22.1 jit_solution(4404309662148924248)
XLA Ops:
  0.0 0.0 copy-start
  0.0 3.5 %project.1 = (f32[256,128]{1,0:T(8,128)S(1)}, f32[8,128]{1,0:T(8,128)S(1)}) custom-call(s32[2]{0:T(128)} %lengths.1, bf16[2,128,7168]{2,1,0:T(8,128)(2,1)} %act.1, bf16[2,128,2048]{2,1,0:T(8,128)(2,1)} %grad.1, bf16[64,7168]{1,0:T(8,128)(2,1)} %bitcast.5, bf16[64,2048]{1,0:T(8,128)(2,1)} %bitcast.6), custom_call_target="tpu_custom_call" | custom-call | tf_op jit(solution)/shard_map/project/pallas_call | solution.py:246
  3.6 0.5 %collective-permute-start = (f32[256,128]{1,0:T(8,128)S(1)}, f32[256,128]{1,0:T(8,128)S(1)}, u32[]{:S(2)}, u32[]{:S(2)}) collective-permute-start(f32[256,128]{1,0:T(8,128)S(1)} %get-tuple-element.8), channel_id=1, source_target_pairs={{0,1},{1,0},{2,3},{3,2},{4,5},{5,4},{6,7},{7,6},{8,9},{9,8},{10,11... | collective-permute-start | bytes 393224 | tf_op jit(solution)/shard_map/ppermute | solution.py:270
  4.1 1.0 %collective-permute-done = f32[256,128]{1,0:T(8,128)S(1)} collective-permute-done((f32[256,128]{1,0:T(8,128)S(1)}, f32[256,128]{1,0:T(8,128)S(1)}, u32[]{:S(2)}, u32[]{:S(2)}) %collective-permute-start) | collective-permute-done | bytes 131104 | tf_op jit(solution)/shard_map/ppermute | solution.py:270
  5.1 3.0 %collective-permute-start.1 = (f32[256,128]{1,0:T(8,128)S(1)}, f32[256,128]{1,0:T(8,128)S(1)}, u32[]{:S(2)}, u32[]{:S(2)}) collective-permute-start(f32[256,128]{1,0:T(8,128)S(1)} %add.3.mine), channel_id=1, source_target_pairs={{0,4},{1,3},{2,6},{3,1},{4,0},{5,7},{6,2},{7,5},{8,12},{9,11},{10,... | collective-permute-start | bytes 393224 | tf_op jit(solution)/shard_map/ppermute | solution.py:266
  8.1 2.9 %collective-permute-done.1.theirs = f32[256,128]{1,0:T(8,128)S(1)} collective-permute-done((f32[256,128]{1,0:T(8,128)S(1)}, f32[256,128]{1,0:T(8,128)S(1)}, u32[]{:S(2)}, u32[]{:S(2)}) %collective-permute-start.1) | collective-permute-done | bytes 131104 | tf_op jit(solution)/shard_map/ppermute | solution.py:266
  11.0 1.9 %collective-permute-start.2 = (f32[104,128]{1,0:T(8,128)S(1)}, f32[104,128]{1,0:T(8,128)S(1)}, u32[]{:S(2)}, u32[]{:S(2)}) collective-permute-start(f32[104,128]{1,0:T(8,128)S(1)} %gram.1.mine), channel_id=1, source_target_pairs={{0,2},{1,9},{2,0},{3,11},{4,6},{5,13},{6,4},{7,15},{8,10},{9,1},{1... | collective-permute-start | bytes 159752 | tf_op jit(solution)/shard_map/ppermute | solution.py:266
  13.0 2.2 %collective-permute-done.2.theirs = f32[104,128]{1,0:T(8,128)S(1)} collective-permute-done((f32[104,128]{1,0:T(8,128)S(1)}, f32[104,128]{1,0:T(8,128)S(1)}, u32[]{:S(2)}, u32[]{:S(2)}) %collective-permute-start.2) | collective-permute-done | bytes 53280 | tf_op jit(solution)/shard_map/ppermute | solution.py:266
  15.2 1.9 %collective-permute-start.3 = (f32[168,128]{1,0:T(8,128)S(1)}, f32[168,128]{1,0:T(8,128)S(1)}, u32[]{:S(2)}, u32[]{:S(2)}) collective-permute-start(f32[168,128]{1,0:T(8,128)S(1)} %merge.1.refs_0_), channel_id=1, source_target_pairs={{0,2},{1,5},{2,0},{3,7},{4,6},{5,1},{6,4},{7,3},{8,10},{9,13},{10,... | collective-permute-start | bytes 258056 | tf_op jit(solution)/shard_map/ppermute | solution.py:266
  17.1 2.5 %collective-permute-done.3.refs_1_ = f32[168,128]{1,0:T(8,128)S(1)} collective-permute-done((f32[168,128]{1,0:T(8,128)S(1)}, f32[168,128]{1,0:T(8,128)S(1)}, u32[]{:S(2)}, u32[]{:S(2)}) %collective-permute-start.3) | collective-permute-done | bytes 86048 | tf_op jit(solution)/shard_map/ppermute | solution.py:266
  19.6 0.0 copy-done
  19.6 1.1 %collective-permute-start.4 = (f32[2,64]{1,0:T(2,128)S(1)}, f32[2,64]{1,0:T(2,128)S(1)}, u32[]{:S(2)}, u32[]{:S(2)}) collective-permute-start(f32[2,64]{1,0:T(2,128)S(1)} %finish.1.scores), channel_id=1, source_target_pairs={{0,1},{1,0},{2,3},{3,2},{4,5},{5,4},{6,7},{7,6},{8,9},{9,8},{10,11... | collective-permute-start | bytes 1544 | tf_op jit(solution)/shard_map/ppermute | solution.py:270
  20.7 0.6 %publish.1.mine = f32[2,64]{1,0:T(2,128)} custom-call(f32[2,64]{1,0:T(2,128)S(1)} %finish.1.scores), custom_call_target="tpu_custom_call" | custom-call | flops 1000000000 | tf_op jit(solution)/shard_map/publish/pallas_call | solution.py:274
  21.3 0.2 %collective-permute-done.4.theirs = f32[2,64]{1,0:T(2,128)S(1)} collective-permute-done((f32[2,64]{1,0:T(2,128)S(1)}, f32[2,64]{1,0:T(2,128)S(1)}, u32[]{:S(2)}, u32[]{:S(2)}) %collective-permute-start.4) | collective-permute-done | bytes 544 | tf_op jit(solution)/shard_map/ppermute | solution.py:270
  21.6 0.6 %replace.1 = f32[2,64]{1,0:T(2,128)} custom-call(f32[2,64]{1,0:T(2,128)S(1)} %collective-permute-done.4.theirs, f32[2,64]{1,0:T(2,128)} %publish.1.mine), custom_call_target="tpu_custom_call", output_to_operand_aliasing={{}: (1, {})} | custom-call | tf_op jit(solution)/shard_map/replace/pallas_call | solution.py:287
  (4 shorter events, 0.0 us)
Async XLA Ops:
  0.0 19.6 %copy-start = (s32[64]{0:T(128)S(1)}, s32[64]{0:T(128)}, u32[]{:S(2)}) copy-start(s32[64]{0:T(128)} %param.11) | copy-start | bytes 772
  3.6 1.5 %collective-permute-start = (f32[256,128]{1,0:T(8,128)S(1)}, f32[256,128]{1,0:T(8,128)S(1)}, u32[]{:S(2)}, u32[]{:S(2)}) collective-permute-start(f32[256,128]{1,0:T(8,128)S(1)} %get-tuple-element.8), channel_id=1, source_target_pairs={{0,1},{1,0},{2,3},{3,2},{4,5},{5,4},{6,7},{7,6},{8,9},{9,8},{10,11... | collective-permute-start | bytes 393224 | tf_op jit(solution)/shard_map/ppermute | solution.py:270
  5.1 5.9 %collective-permute-start.1 = (f32[256,128]{1,0:T(8,128)S(1)}, f32[256,128]{1,0:T(8,128)S(1)}, u32[]{:S(2)}, u32[]{:S(2)}) collective-permute-start(f32[256,128]{1,0:T(8,128)S(1)} %add.3.mine), channel_id=1, source_target_pairs={{0,4},{1,3},{2,6},{3,1},{4,0},{5,7},{6,2},{7,5},{8,12},{9,11},{10,... | collective-permute-start | bytes 393224 | tf_op jit(solution)/shard_map/ppermute | solution.py:266
  11.0 4.1 %collective-permute-start.2 = (f32[104,128]{1,0:T(8,128)S(1)}, f32[104,128]{1,0:T(8,128)S(1)}, u32[]{:S(2)}, u32[]{:S(2)}) collective-permute-start(f32[104,128]{1,0:T(8,128)S(1)} %gram.1.mine), channel_id=1, source_target_pairs={{0,2},{1,9},{2,0},{3,11},{4,6},{5,13},{6,4},{7,15},{8,10},{9,1},{1... | collective-permute-start | bytes 159752 | tf_op jit(solution)/shard_map/ppermute | solution.py:266
  15.2 4.5 %collective-permute-start.3 = (f32[168,128]{1,0:T(8,128)S(1)}, f32[168,128]{1,0:T(8,128)S(1)}, u32[]{:S(2)}, u32[]{:S(2)}) collective-permute-start(f32[168,128]{1,0:T(8,128)S(1)} %merge.1.refs_0_), channel_id=1, source_target_pairs={{0,2},{1,5},{2,0},{3,7},{4,6},{5,1},{6,4},{7,3},{8,10},{9,13},{10,... | collective-permute-start | bytes 258056 | tf_op jit(solution)/shard_map/ppermute | solution.py:266
  19.6 1.9 %collective-permute-start.4 = (f32[2,64]{1,0:T(2,128)S(1)}, f32[2,64]{1,0:T(2,128)S(1)}, u32[]{:S(2)}, u32[]{:S(2)}) collective-permute-start(f32[2,64]{1,0:T(2,128)S(1)} %finish.1.scores), channel_id=1, source_target_pairs={{0,1},{1,0},{2,3},{3,2},{4,5},{5,4},{6,7},{7,6},{8,9},{9,8},{10,11... | collective-permute-start | bytes 1544 | tf_op jit(solution)/shard_map/ppermute | solution.py:270

commit v6 on v5

--- a/solution.py
+++ b/solution.py
@@ -73,6 +73,7 @@
 
 def gram_kernel(seq_len, leads, live, mine, theirs, packed):
     rank = mine.shape[1] // 2
+    half = rank // 2
 
     @pl.when(leads())
     def _():
@@ -86,37 +87,28 @@
                 )
             )
         total = grams[0] + grams[1]
-        low = total[rank:]
+        high, low = total[:rank], total[rank:]
+        row = lax.broadcasted_iota(jnp.int32, (half, 2 * rank), 0)
+        lane = lax.broadcasted_iota(jnp.int32, (half, 2 * rank), 1)
+        packed[rank : rank + half] = jnp.where(
+            lane < rank,
+            jnp.where(lane <= row, high[:half], pltpu.roll(low[:half], rank, 1)),
+            jnp.where(lane - rank <= row + half, pltpu.roll(high[half:], rank, 1), low[half:]),
+        )
         row = lax.broadcasted_iota(jnp.int32, (rank, 2 * rank), 0)
         lane = lax.broadcasted_iota(jnp.int32, (rank, 2 * rank), 1)
-        mixed = jnp.where(lane <= row, total[:rank], pltpu.roll(low, rank, 1))
-        packed[:rank] = jnp.where(lane < rank, mixed, grams[0][:rank])
-        half = rank // 2
-        folded = pltpu.roll(grams[1][half:rank], rank, 1)
-        packed[rank : rank + half] = jnp.where(lane[:half] < rank, folded, grams[1][:half])
         diag = jnp.sum(jnp.where(lane == rank + row, low, 0.0), axis=0, keepdims=True)
-        diag = pltpu.roll(jnp.broadcast_to(diag, (8, 2 * rank)), rank, 1)
-        packed[rank + half :] = jnp.where(lane[:8] < rank, diag, live[...])
-
-
-def unfold(top, folded):
-    rank = top.shape[0]
-    lane = lax.broadcasted_iota(jnp.int32, top.shape, 1)
-    return jnp.where(lane < rank, jnp.concatenate([pltpu.roll(folded, rank, 1), folded], axis=0), top)
+        packed[rank + half :] = jnp.where(lane[:8] < rank, live[...], diag)
+        packed[:rank] = jnp.where(lane < rank, pltpu.roll(grams[1][:rank], rank, 1), grams[0][:rank])
 
 
 def merge_kernel(leads, mine, theirs, merged):
     rank = mine.shape[1] // 2
-    half = rank // 2
 
     @pl.when(leads())
     def _():
-        top, other = mine[:rank], theirs[:rank]
-        lane = lax.broadcasted_iota(jnp.int32, top.shape, 1)
-        merged[:rank] = jnp.where(lane < rank, top + other, top)
-        merged[rank : rank + half] = mine[rank : rank + half]
-        merged[rank + half : rank + half + 8] = mine[rank + half :] + theirs[rank + half :]
-        merged[rank + half + 8 :] = unfold(other, theirs[rank : rank + half])
+        merged[:rank] = theirs[:rank]
+        merged[rank:] = mine[rank:] + theirs[rank:]
 
 
 def inverse_steps(rank):
@@ -130,11 +122,11 @@
 
 
 def scaled(rank, total):
-    mixed = total[:rank, :rank]
+    half = rank // 2
+    mixed = jnp.concatenate([total[:half, :rank], total[:half, rank:]], axis=0)
     turned = mixed.T
-    tail = rank + rank // 2
-    diag = total[tail : tail + 1, :rank]
-    count = total[tail : tail + 1, rank : rank + 1]
+    diag = total[half : half + 1, rank:]
+    count = total[half : half + 1, :1]
     row = lax.broadcasted_iota(jnp.int32, (rank, rank), 0)
     lane = lax.broadcasted_iota(jnp.int32, (rank, rank), 1)
     eye = row == lane
@@ -166,22 +158,17 @@
     return right, x_in, c_out, c_in
 
 
-def finish_kernel(seq_len, leads, masks, queries, *refs):
-    packs, scores = refs[:-1], refs[-1]
-    rank = packs[0].shape[1] // 2
-    fixed = rank + rank // 2 + 8
+def finish_kernel(seq_len, leads, masks, count, queries, *refs):
+    blocks, scores = refs[:-1], refs[-1]
+    rank = blocks[0].shape[1] // 2
 
     @pl.when(leads())
     def _():
-        total = [ref[:fixed] for ref in packs]
+        pairs = [ref[:rank] for ref in blocks]
+        total = [ref[rank:] for ref in blocks[:count]]
         while len(total) > 1:
             total = [total[n] + total[n + 1] for n in range(0, len(total), 2)]
-        pairs = []
-        for ref in packs:
-            pairs.append(unfold(ref[:rank], ref[rank : rank + rank // 2]))
-            if ref.shape[0] > fixed:
-                pairs.append(ref[fixed:])
-        left, inv_in, c_out, c_in = solve(rank, total[0], pairs[0])
+        left, inv_in, c_out, c_in = solve(rank, total[0], pairs[masks.index(0)])
         left = left * c_out
         zero = jnp.zeros((rank, rank), jnp.float32)
         right = jnp.concatenate(
@@ -189,12 +176,12 @@
         )
         straight = dot_hi(left, right) * c_in
         crossed = pltpu.roll(straight, rank, 1)
-        count = len(pairs)
+        size = len(pairs)
         sums = [jnp.sum(pair * straight, axis=0, keepdims=True) for pair in pairs]
         sums += [jnp.sum(pair * crossed, axis=0, keepdims=True) for pair in pairs]
         sums = jnp.concatenate(sums, axis=0)
         num = queries.shape[1]
-        index = lax.broadcasted_iota(jnp.int32, (2 * count, num), 0) % count
+        index = lax.broadcasted_iota(jnp.int32, (2 * size, num), 0) % size
         mask = sum(jnp.where(index == n, value, 0) for n, value in enumerate(masks))
         device = lax.axis_index("dp") ^ mask
         chosen = queries[...]
@@ -202,10 +189,10 @@
         first = jnp.where(chosen == 2 * device, jnp.sum(sums[:, rank:], axis=1, keepdims=True), 0.0)
         scale = 1.0 / (rank * seq_len)
         scores[0:1, :] = scale * jnp.sum(
-            jnp.concatenate([first[:count], second[count:]], axis=0), axis=0, keepdims=True
+            jnp.concatenate([first[:size], second[size:]], axis=0), axis=0, keepdims=True
         )
         scores[1:2, :] = scale * jnp.sum(
-            jnp.concatenate([second[:count], first[count:]], axis=0), axis=0, keepdims=True
+            jnp.concatenate([second[:size], first[size:]], axis=0), axis=0, keepdims=True
         )
 
 
@@ -322,22 +309,27 @@
         other,
     )
     if paired:
+        own = packed
+        near = swap(packed, dp, tensor, (1, 0), (0, 2))
         other = swap(packed, dp, tensor, (2, 0), (0, 2))
-        rows = 2 * rank + rank // 2 + 8
-        merged = call(functools.partial(merge_kernel, leads), "merge", shape(rows, 2 * rank), packed, other)
-        packs = [merged, swap(merged, dp, tensor, (1, 0), (0, 2))]
-        masks = [0, 2, 1, 3]
+        merged = call(
+            functools.partial(merge_kernel, leads), "merge", shape(rank + rank // 2 + 8, 2 * rank), packed, other
+        )
+        blocks = [merged, swap(merged, dp, tensor, (1, 0), (0, 2)), own, near]
+        masks = [2, 3, 0, 1]
+        count = 2
     else:
         masks = list(range(dp))
+        count = dp
         order = lax.axis_index("dp") ^ jnp.arange(dp, dtype=jnp.int32)
         gathered = lax.all_gather(packed, "dp", axis=0)[order]
-        packs = [gathered[n] for n in range(dp)]
+        blocks = [gathered[n] for n in range(dp)]
     scores = call(
-        functools.partial(finish_kernel, seq_len, leads, masks),
+        functools.partial(finish_kernel, seq_len, leads, masks, count),
         "finish",
         shape(examples, num),
         query_ids.reshape(1, num),
-        *packs,
+        *blocks,
     )
     if paired:
         other = across(scores, tensor)

time: 22.3 us -> 21.9 us (0.982)
  waiting for transfers between devices: 8.92 us -> 8.48 us
    ppermute x3 -> x4, waiting for transfers between devices: 7.69 us -> 7.25 us  [swap(): return lax.ppermute(x, ('dp', 'tensor'), pairs)]
    ppermute x3 -> x4, starting transfers between devices: 6.87 us -> 6.96 us  [swap(): return lax.ppermute(x, ('dp', 'tensor'), pairs)]
  transfers between devices with their start and end apart: 5 -> 6, of which waited for: 5 -> 5; matrix products, arithmetic and copies ran while one was open for 0% -> 0% of each run, Pallas kernels for 3% -> 3%
where the time goes in v6:
time: 21.9 us; the launch traced here: 21.8 us
  starting transfers between devices  8.59 us (39%)
  waiting for transfers between devices  8.48 us (39%)
  Pallas kernels  4.68 us (21%)
    ppermute x4, waiting for transfers between devices, swap(): return lax.ppermute(x, ('dp', 'tensor'), pairs)  7.25 us
    ppermute x4, starting transfers between devices, swap(): return lax.ppermute(x, ('dp', 'tensor'), pairs)  6.96 us
    pallas_call x1, Pallas kernels, project(): pl.pallas_call(project_kernel, out_shape=[shape(examples * seq_len, 2 * r...  3.54 us
    ppermute x2, starting transfers between devices, across(): return lax.ppermute(x, 'tensor', [(t, t ^ 1) for t in range(tensor)])  1.63 us
    ppermute x2, waiting for transfers between devices, across(): return lax.ppermute(x, 'tensor', [(t, t ^ 1) for t in range(tensor)])  1.23 us
    pallas_call x1, Pallas kernels, publish(): pl.pallas_call(publish_kernel, out_shape=jax.ShapeDtypeStruct(scores.shap...  0.57 us
    pallas_call x1, Pallas kernels, replace(): pl.pallas_call(functools.partial(replace_kernel, leads), out_shape=jax.Sh...  0.57 us
  transfers between devices with their start and end apart: 6, of which 5 were waited for; matrix products, arithmetic and copies ran while one was open for 0% of the time, Pallas kernels for 3%

profile of v6, /device:TPU:0, one launch (start us, length us, event | category | flops | bytes accessed | tf_op | source)
XLA Modules:
  0.0 21.8 jit_solution(9758900700148139536)
XLA Ops:
  0.0 0.0 copy-start
  0.0 3.5 %project.1 = (f32[256,128]{1,0:T(8,128)S(1)}, f32[8,128]{1,0:T(8,128)S(1)}) custom-call(s32[2]{0:T(128)} %lengths.1, bf16[2,128,7168]{2,1,0:T(8,128)(2,1)} %act.1, bf16[2,128,2048]{2,1,0:T(8,128)(2,1)} %grad.1, bf16[64,7168]{1,0:T(8,128)(2,1)} %bitcast.5, bf16[64,2048]{1,0:T(8,128)(2,1)} %bitcast.6), custom_call_target="tpu_custom_call" | custom-call | tf_op jit(solution)/shard_map/project/pallas_call | solution.py:233
  3.6 0.5 %collective-permute-start = (f32[256,128]{1,0:T(8,128)S(1)}, f32[256,128]{1,0:T(8,128)S(1)}, u32[]{:S(2)}, u32[]{:S(2)}) collective-permute-start(f32[256,128]{1,0:T(8,128)S(1)} %get-tuple-element.8), channel_id=1, source_target_pairs={{0,1},{1,0},{2,3},{3,2},{4,5},{5,4},{6,7},{7,6},{8,9},{9,8},{10,11... | collective-permute-start | bytes 393224 | tf_op jit(solution)/shard_map/ppermute | solution.py:257
  4.1 1.0 %collective-permute-done = f32[256,128]{1,0:T(8,128)S(1)} collective-permute-done((f32[256,128]{1,0:T(8,128)S(1)}, f32[256,128]{1,0:T(8,128)S(1)}, u32[]{:S(2)}, u32[]{:S(2)}) %collective-permute-start) | collective-permute-done | bytes 131104 | tf_op jit(solution)/shard_map/ppermute | solution.py:257
  5.1 3.0 %collective-permute-start.1 = (f32[256,128]{1,0:T(8,128)S(1)}, f32[256,128]{1,0:T(8,128)S(1)}, u32[]{:S(2)}, u32[]{:S(2)}) collective-permute-start(f32[256,128]{1,0:T(8,128)S(1)} %add.3.mine), channel_id=1, source_target_pairs={{0,4},{1,3},{2,6},{3,1},{4,0},{5,7},{6,2},{7,5},{8,12},{9,11},{10,... | collective-permute-start | bytes 393224 | tf_op jit(solution)/shard_map/ppermute | solution.py:253
  8.1 2.9 %collective-permute-done.1.theirs = f32[256,128]{1,0:T(8,128)S(1)} collective-permute-done((f32[256,128]{1,0:T(8,128)S(1)}, f32[256,128]{1,0:T(8,128)S(1)}, u32[]{:S(2)}, u32[]{:S(2)}) %collective-permute-start.1) | collective-permute-done | bytes 131104 | tf_op jit(solution)/shard_map/ppermute | solution.py:253
  11.0 1.9 %collective-permute-start.2 = (f32[104,128]{1,0:T(8,128)S(1)}, f32[104,128]{1,0:T(8,128)S(1)}, u32[]{:S(2)}, u32[]{:S(2)}) collective-permute-start(f32[104,128]{1,0:T(8,128)S(1)} %gram.1.mine.refs_2_), channel_id=1, source_target_pairs={{0,2},{1,9},{2,0},{3,11},{4,6},{5,13},{6,4},{7,15},{8,10},{9,1},{1... | collective-permute-start | bytes 159752 | tf_op jit(solution)/shard_map/ppermute | solution.py:253
  13.0 0.1 collective-permute-start.4
  13.0 2.1 %collective-permute-done.2.theirs = f32[104,128]{1,0:T(8,128)S(1)} collective-permute-done((f32[104,128]{1,0:T(8,128)S(1)}, f32[104,128]{1,0:T(8,128)S(1)}, u32[]{:S(2)}, u32[]{:S(2)}) %collective-permute-start.2) | collective-permute-done | bytes 53280 | tf_op jit(solution)/shard_map/ppermute | solution.py:253
  15.2 1.9 %collective-permute-start.3 = (f32[104,128]{1,0:T(8,128)S(1)}, f32[104,128]{1,0:T(8,128)S(1)}, u32[]{:S(2)}, u32[]{:S(2)}) collective-permute-start(f32[104,128]{1,0:T(8,128)S(1)} %merge.1.refs_0_), channel_id=1, source_target_pairs={{0,2},{1,5},{2,0},{3,7},{4,6},{5,1},{6,4},{7,3},{8,10},{9,13},{10,... | collective-permute-start | bytes 159752 | tf_op jit(solution)/shard_map/ppermute | solution.py:253
  17.1 0.0 collective-permute-done.4.refs_3_
  17.1 2.2 %collective-permute-done.3.refs_1_ = f32[104,128]{1,0:T(8,128)S(1)} collective-permute-done((f32[104,128]{1,0:T(8,128)S(1)}, f32[104,128]{1,0:T(8,128)S(1)}, u32[]{:S(2)}, u32[]{:S(2)}) %collective-permute-start.3) | collective-permute-done | bytes 53280 | tf_op jit(solution)/shard_map/ppermute | solution.py:253
  19.3 0.0 copy-done
  19.3 1.1 %collective-permute-start.5 = (f32[2,64]{1,0:T(2,128)S(1)}, f32[2,64]{1,0:T(2,128)S(1)}, u32[]{:S(2)}, u32[]{:S(2)}) collective-permute-start(f32[2,64]{1,0:T(2,128)S(1)} %finish.1.scores), channel_id=1, source_target_pairs={{0,1},{1,0},{2,3},{3,2},{4,5},{5,4},{6,7},{7,6},{8,9},{9,8},{10,11... | collective-permute-start | bytes 1544 | tf_op jit(solution)/shard_map/ppermute | solution.py:257
  20.4 0.6 %publish.1.mine = f32[2,64]{1,0:T(2,128)} custom-call(f32[2,64]{1,0:T(2,128)S(1)} %finish.1.scores), custom_call_target="tpu_custom_call" | custom-call | flops 1000000000 | tf_op jit(solution)/shard_map/publish/pallas_call | solution.py:261
  21.0 0.2 %collective-permute-done.5.theirs = f32[2,64]{1,0:T(2,128)S(1)} collective-permute-done((f32[2,64]{1,0:T(2,128)S(1)}, f32[2,64]{1,0:T(2,128)S(1)}, u32[]{:S(2)}, u32[]{:S(2)}) %collective-permute-start.5) | collective-permute-done | bytes 544 | tf_op jit(solution)/shard_map/ppermute | solution.py:257
  21.2 0.6 %replace.1 = f32[2,64]{1,0:T(2,128)} custom-call(f32[2,64]{1,0:T(2,128)S(1)} %collective-permute-done.5.theirs, f32[2,64]{1,0:T(2,128)} %publish.1.mine), custom_call_target="tpu_custom_call", output_to_operand_aliasing={{}: (1, {})} | custom-call | tf_op jit(solution)/shard_map/replace/pallas_call | solution.py:274
  (4 shorter events, 0.0 us)
Async XLA Ops:
  0.0 19.3 %copy-start = (s32[64]{0:T(128)S(1)}, s32[64]{0:T(128)}, u32[]{:S(2)}) copy-start(s32[64]{0:T(128)} %param.11) | copy-start | bytes 772
  3.6 1.5 %collective-permute-start = (f32[256,128]{1,0:T(8,128)S(1)}, f32[256,128]{1,0:T(8,128)S(1)}, u32[]{:S(2)}, u32[]{:S(2)}) collective-permute-start(f32[256,128]{1,0:T(8,128)S(1)} %get-tuple-element.8), channel_id=1, source_target_pairs={{0,1},{1,0},{2,3},{3,2},{4,5},{5,4},{6,7},{7,6},{8,9},{9,8},{10,11... | collective-permute-start | bytes 393224 | tf_op jit(solution)/shard_map/ppermute | solution.py:257
  5.1 5.9 %collective-permute-start.1 = (f32[256,128]{1,0:T(8,128)S(1)}, f32[256,128]{1,0:T(8,128)S(1)}, u32[]{:S(2)}, u32[]{:S(2)}) collective-permute-start(f32[256,128]{1,0:T(8,128)S(1)} %add.3.mine), channel_id=1, source_target_pairs={{0,4},{1,3},{2,6},{3,1},{4,0},{5,7},{6,2},{7,5},{8,12},{9,11},{10,... | collective-permute-start | bytes 393224 | tf_op jit(solution)/shard_map/ppermute | solution.py:253
  11.0 4.1 %collective-permute-start.2 = (f32[104,128]{1,0:T(8,128)S(1)}, f32[104,128]{1,0:T(8,128)S(1)}, u32[]{:S(2)}, u32[]{:S(2)}) collective-permute-start(f32[104,128]{1,0:T(8,128)S(1)} %gram.1.mine.refs_2_), channel_id=1, source_target_pairs={{0,2},{1,9},{2,0},{3,11},{4,6},{5,13},{6,4},{7,15},{8,10},{9,1},{1... | collective-permute-start | bytes 159752 | tf_op jit(solution)/shard_map/ppermute | solution.py:253
  13.0 4.1 %collective-permute-start.4 = (f32[104,128]{1,0:T(8,128)S(1)}, f32[104,128]{1,0:T(8,128)S(1)}, u32[]{:S(2)}, u32[]{:S(2)}) collective-permute-start(f32[104,128]{1,0:T(8,128)S(1)} %gram.1.mine.refs_2_), channel_id=1, source_target_pairs={{0,2},{1,5},{2,0},{3,7},{4,6},{5,1},{6,4},{7,3},{8,10},{9,13},{10,... | collective-permute-start | bytes 159752 | tf_op jit(solution)/shard_map/ppermute | solution.py:253
  15.2 4.1 %collective-permute-start.3 = (f32[104,128]{1,0:T(8,128)S(1)}, f32[104,128]{1,0:T(8,128)S(1)}, u32[]{:S(2)}, u32[]{:S(2)}) collective-permute-start(f32[104,128]{1,0:T(8,128)S(1)} %merge.1.refs_0_), channel_id=1, source_target_pairs={{0,2},{1,5},{2,0},{3,7},{4,6},{5,1},{6,4},{7,3},{8,10},{9,13},{10,... | collective-permute-start | bytes 159752 | tf_op jit(solution)/shard_map/ppermute | solution.py:253
  19.3 1.9 %collective-permute-start.5 = (f32[2,64]{1,0:T(2,128)S(1)}, f32[2,64]{1,0:T(2,128)S(1)}, u32[]{:S(2)}, u32[]{:S(2)}) collective-permute-start(f32[2,64]{1,0:T(2,128)S(1)} %finish.1.scores), channel_id=1, source_target_pairs={{0,1},{1,0},{2,3},{3,2},{4,5},{5,4},{6,7},{7,6},{8,9},{9,8},{10,11... | collective-permute-start | bytes 1544 | tf_op jit(solution)/shard_map/ppermute | solution.py:257

commit v7 on v6

--- a/solution.py
+++ b/solution.py
@@ -11,6 +11,7 @@
 VMEM = pl.BlockSpec(memory_space=pltpu.VMEM)
 HBM = pl.BlockSpec(memory_space=pltpu.HBM)
 DAMP = 0.1
+STEPS = 5
 
 
 def dot_nt(a, b):
@@ -111,17 +112,7 @@
         merged[rank:] = mine[rank:] + theirs[rank:]
 
 
-def inverse_steps(rank):
-    least = 2.0 * (DAMP / rank) / (1.0 + 2.0 * DAMP / rank)
-    scales = []
-    while (1.0 - least) ** 2 > 1e-7:
-        image = least * (2.0 - least)
-        scales.append(2.0 / (1.0 + image))
-        least = scales[-1] * image
-    return scales + [1.0]
-
-
-def scaled(rank, total):
+def normalised(rank, total):
     half = rank // 2
     mixed = jnp.concatenate([total[:half, :rank], total[:half, rank:]], axis=0)
     turned = mixed.T
@@ -132,30 +123,58 @@
     eye = row == lane
     sum_out = jnp.where(lane <= row, mixed, turned)
     sum_in = jnp.where(lane > row, mixed, jnp.where(eye, diag, turned))
-    factor = 2.0 / (1.0 + 2.0 * DAMP / rank)
-
-    def scale(sums):
+
+    def divide(sums):
         trace = jnp.sum(jnp.sum(jnp.where(eye, sums, 0.0), axis=0, keepdims=True), axis=1, keepdims=True)
-        return sums * (factor / trace) + jnp.where(eye, factor * DAMP / rank, 0.0), factor * count / trace
-
-    return *scale(sum_out), *scale(sum_in), jnp.where(eye, 2.0, 0.0)
+        return sums / trace + jnp.where(eye, DAMP / rank, 0.0), count / trace
+
+    return *divide(sum_out), *divide(sum_in), jnp.where(eye, 1.0, 0.0)
+
+
+def total_square(matrix):
+    return jnp.sum(jnp.sum(matrix * matrix, axis=0, keepdims=True), axis=1, keepdims=True)
 
 
 def solve(rank, total, right):
-    t_out, c_out, t_in, c_in, two_eye = scaled(rank, total)
-    steps = inverse_steps(rank)
-    x_in = steps[0] * (two_eye - t_in)
-    for n, scale in enumerate(steps):
-        last = n == len(steps) - 1
-        p_out, p_in = t_out, t_in
-        right = scale * (2.0 * right - dot_hi(p_out, right))
-        if not last:
-            t_out = scale * (2.0 * p_out - dot_hi(p_out, p_out))
-        if n > 0:
-            x_in = scale * (2.0 * x_in - dot_hi(x_in, p_in))
-        if not last:
-            t_in = scale * (2.0 * p_in - dot_hi(p_in, p_in))
-    return right, x_in, c_out, c_in
+    d_out, c_out, d_in, c_in, eye = normalised(rank, total)
+
+    def scale(matrix):
+        mean = (1.0 + DAMP) / rank
+        spread = jnp.sqrt(jnp.maximum(total_square(matrix) / rank - mean * mean, 0.0))
+        return 2.0 / (mean + spread * (rank - 1) ** 0.5 + DAMP / rank)
+
+    s_out, s_in = scale(d_out), scale(d_in)
+    t_out = s_out * (2.0 * d_out - s_out * dot_hi(d_out, d_out))
+    t_in = s_in * (2.0 * d_in - s_in * dot_hi(d_in, d_in))
+    right = 2.0 * right - s_out * dot_hi(d_out, right)
+    x_in = 2.0 * eye - s_in * d_in
+
+    def square(t_out, t_in):
+        return 2.0 * t_out - dot_hi(t_out, t_out), 2.0 * t_in - dot_hi(t_in, t_in)
+
+    def update(t_out, t_in, right, x_in):
+        return 2.0 * right - dot_hi(t_out, right), 2.0 * x_in - dot_hi(x_in, t_in)
+
+    def residual(t_out, t_in):
+        return jnp.sum(total_square(eye - t_out) + total_square(eye - t_in))
+
+    for n in range(STEPS - 1):
+        right, x_in = update(t_out, t_in, right, x_in)
+        if n < STEPS - 2:
+            t_out, t_in = square(t_out, t_in)
+
+    def unfinished(state):
+        return jnp.logical_and(state[0] > 1e-5, state[1] < 40)
+
+    def more(state):
+        _, n, t_out, t_in, right, x_in = state
+        t_out, t_in = square(t_out, t_in)
+        right, x_in = update(t_out, t_in, right, x_in)
+        return residual(t_out, t_in), n + 1, t_out, t_in, right, x_in
+
+    state = (residual(t_out, t_in), jnp.int32(0), t_out, t_in, right, x_in)
+    _, _, _, _, right, x_in = lax.while_loop(unfinished, more, state)
+    return right, x_in, c_out * s_out, c_in * s_in
 
 
 def finish_kernel(seq_len, leads, masks, count, queries, *refs):

time: 21.9 us -> 22.6 us (1.032)
  starting transfers between devices: 8.59 us -> 9.29 us
    ppermute x2, starting transfers between devices: 1.63 us -> 2.33 us  [across(): return lax.ppermute(x, 'tensor', [(t, t ^ 1) for t in range(tensor)])]
where the time goes in v7:
time: 22.6 us; the launch traced here: 22.5 us
  starting transfers between devices  9.29 us (41%)
  waiting for transfers between devices  8.48 us (38%)
  Pallas kernels  4.68 us (21%)
    ppermute x4, waiting for transfers between devices, swap(): return lax.ppermute(x, ('dp', 'tensor'), pairs)  7.25 us
    ppermute x4, starting transfers between devices, swap(): return lax.ppermute(x, ('dp', 'tensor'), pairs)  6.96 us
    pallas_call x1, Pallas kernels, project(): pl.pallas_call(project_kernel, out_shape=[shape(examples * seq_len, 2 * r...  3.54 us
    ppermute x2, starting transfers between devices, across(): return lax.ppermute(x, 'tensor', [(t, t ^ 1) for t in range(tensor)])  2.33 us
    ppermute x2, waiting for transfers between devices, across(): return lax.ppermute(x, 'tensor', [(t, t ^ 1) for t in range(tensor)])  1.23 us
    pallas_call x1, Pallas kernels, publish(): pl.pallas_call(publish_kernel, out_shape=jax.ShapeDtypeStruct(scores.shap...  0.57 us
    pallas_call x1, Pallas kernels, replace(): pl.pallas_call(functools.partial(replace_kernel, leads), out_shape=jax.Sh...  0.57 us
  transfers between devices with their start and end apart: 6, of which 5 were waited for; matrix products, arithmetic and copies ran while one was open for 0% of the time, Pallas kernels for 3%

profile of v7, /device:TPU:0, one launch (start us, length us, event | category | flops | bytes accessed | tf_op | source)
XLA Modules:
  0.0 22.5 jit_solution(5093150559019857347)
XLA Ops:
  0.0 0.0 copy-start
  0.0 3.5 %project.1 = (f32[256,128]{1,0:T(8,128)S(1)}, f32[8,128]{1,0:T(8,128)S(1)}) custom-call(s32[2]{0:T(128)} %lengths.1, bf16[2,128,7168]{2,1,0:T(8,128)(2,1)} %act.1, bf16[2,128,2048]{2,1,0:T(8,128)(2,1)} %grad.1, bf16[64,7168]{1,0:T(8,128)(2,1)} %bitcast.5, bf16[64,2048]{1,0:T(8,128)(2,1)} %bitcast.6), custom_call_target="tpu_custom_call" | custom-call | tf_op jit(solution)/shard_map/project/pallas_call | solution.py:252
  3.6 0.5 %collective-permute-start = (f32[256,128]{1,0:T(8,128)S(1)}, f32[256,128]{1,0:T(8,128)S(1)}, u32[]{:S(2)}, u32[]{:S(2)}) collective-permute-start(f32[256,128]{1,0:T(8,128)S(1)} %get-tuple-element.8), channel_id=1, source_target_pairs={{0,1},{1,0},{2,3},{3,2},{4,5},{5,4},{6,7},{7,6},{8,9},{9,8},{10,11... | collective-permute-start | bytes 393224 | tf_op jit(solution)/shard_map/ppermute | solution.py:276
  4.1 1.0 %collective-permute-done = f32[256,128]{1,0:T(8,128)S(1)} collective-permute-done((f32[256,128]{1,0:T(8,128)S(1)}, f32[256,128]{1,0:T(8,128)S(1)}, u32[]{:S(2)}, u32[]{:S(2)}) %collective-permute-start) | collective-permute-done | bytes 131104 | tf_op jit(solution)/shard_map/ppermute | solution.py:276
  5.1 3.0 %collective-permute-start.1 = (f32[256,128]{1,0:T(8,128)S(1)}, f32[256,128]{1,0:T(8,128)S(1)}, u32[]{:S(2)}, u32[]{:S(2)}) collective-permute-start(f32[256,128]{1,0:T(8,128)S(1)} %add.3.mine), channel_id=1, source_target_pairs={{0,4},{1,3},{2,6},{3,1},{4,0},{5,7},{6,2},{7,5},{8,12},{9,11},{10,... | collective-permute-start | bytes 393224 | tf_op jit(solution)/shard_map/ppermute | solution.py:272
  8.1 2.9 %collective-permute-done.1.theirs = f32[256,128]{1,0:T(8,128)S(1)} collective-permute-done((f32[256,128]{1,0:T(8,128)S(1)}, f32[256,128]{1,0:T(8,128)S(1)}, u32[]{:S(2)}, u32[]{:S(2)}) %collective-permute-start.1) | collective-permute-done | bytes 131104 | tf_op jit(solution)/shard_map/ppermute | solution.py:272
  11.0 1.9 %collective-permute-start.2 = (f32[104,128]{1,0:T(8,128)S(1)}, f32[104,128]{1,0:T(8,128)S(1)}, u32[]{:S(2)}, u32[]{:S(2)}) collective-permute-start(f32[104,128]{1,0:T(8,128)S(1)} %gram.1.mine.refs_2_), channel_id=1, source_target_pairs={{0,2},{1,9},{2,0},{3,11},{4,6},{5,13},{6,4},{7,15},{8,10},{9,1},{1... | collective-permute-start | bytes 159752 | tf_op jit(solution)/shard_map/ppermute | solution.py:272
  13.0 0.1 collective-permute-start.4
  13.0 2.1 %collective-permute-done.2.theirs = f32[104,128]{1,0:T(8,128)S(1)} collective-permute-done((f32[104,128]{1,0:T(8,128)S(1)}, f32[104,128]{1,0:T(8,128)S(1)}, u32[]{:S(2)}, u32[]{:S(2)}) %collective-permute-start.2) | collective-permute-done | bytes 53280 | tf_op jit(solution)/shard_map/ppermute | solution.py:272
  15.2 1.9 %collective-permute-start.3 = (f32[104,128]{1,0:T(8,128)S(1)}, f32[104,128]{1,0:T(8,128)S(1)}, u32[]{:S(2)}, u32[]{:S(2)}) collective-permute-start(f32[104,128]{1,0:T(8,128)S(1)} %merge.1.refs_0_), channel_id=1, source_target_pairs={{0,2},{1,5},{2,0},{3,7},{4,6},{5,1},{6,4},{7,3},{8,10},{9,13},{10,... | collective-permute-start | bytes 159752 | tf_op jit(solution)/shard_map/ppermute | solution.py:272
  17.1 0.0 collective-permute-done.4.refs_3_
  17.1 2.2 %collective-permute-done.3.refs_1_ = f32[104,128]{1,0:T(8,128)S(1)} collective-permute-done((f32[104,128]{1,0:T(8,128)S(1)}, f32[104,128]{1,0:T(8,128)S(1)}, u32[]{:S(2)}, u32[]{:S(2)}) %collective-permute-start.3) | collective-permute-done | bytes 53280 | tf_op jit(solution)/shard_map/ppermute | solution.py:272
  19.3 0.0 copy-done
  19.3 1.8 %collective-permute-start.5 = (f32[2,64]{1,0:T(2,128)S(1)}, f32[2,64]{1,0:T(2,128)S(1)}, u32[]{:S(2)}, u32[]{:S(2)}) collective-permute-start(f32[2,64]{1,0:T(2,128)S(1)} %finish.1.scores), channel_id=1, source_target_pairs={{0,1},{1,0},{2,3},{3,2},{4,5},{5,4},{6,7},{7,6},{8,9},{9,8},{10,11... | collective-permute-start | bytes 1544 | tf_op jit(solution)/shard_map/ppermute | solution.py:276
  21.1 0.6 %publish.1.mine = f32[2,64]{1,0:T(2,128)} custom-call(f32[2,64]{1,0:T(2,128)S(1)} %finish.1.scores), custom_call_target="tpu_custom_call" | custom-call | flops 1000000000 | tf_op jit(solution)/shard_map/publish/pallas_call | solution.py:280
  21.7 0.2 %collective-permute-done.5.theirs = f32[2,64]{1,0:T(2,128)S(1)} collective-permute-done((f32[2,64]{1,0:T(2,128)S(1)}, f32[2,64]{1,0:T(2,128)S(1)}, u32[]{:S(2)}, u32[]{:S(2)}) %collective-permute-start.5) | collective-permute-done | bytes 544 | tf_op jit(solution)/shard_map/ppermute | solution.py:276
  21.9 0.6 %replace.1 = f32[2,64]{1,0:T(2,128)} custom-call(f32[2,64]{1,0:T(2,128)S(1)} %collective-permute-done.5.theirs, f32[2,64]{1,0:T(2,128)} %publish.1.mine), custom_call_target="tpu_custom_call", output_to_operand_aliasing={{}: (1, {})} | custom-call | tf_op jit(solution)/shard_map/replace/pallas_call | solution.py:293
  (4 shorter events, 0.0 us)
Async XLA Ops:
  0.0 19.3 %copy-start = (s32[64]{0:T(128)S(1)}, s32[64]{0:T(128)}, u32[]{:S(2)}) copy-start(s32[64]{0:T(128)} %param.11) | copy-start | bytes 772
  3.6 1.5 %collective-permute-start = (f32[256,128]{1,0:T(8,128)S(1)}, f32[256,128]{1,0:T(8,128)S(1)}, u32[]{:S(2)}, u32[]{:S(2)}) collective-permute-start(f32[256,128]{1,0:T(8,128)S(1)} %get-tuple-element.8), channel_id=1, source_target_pairs={{0,1},{1,0},{2,3},{3,2},{4,5},{5,4},{6,7},{7,6},{8,9},{9,8},{10,11... | collective-permute-start | bytes 393224 | tf_op jit(solution)/shard_map/ppermute | solution.py:276
  5.1 5.9 %collective-permute-start.1 = (f32[256,128]{1,0:T(8,128)S(1)}, f32[256,128]{1,0:T(8,128)S(1)}, u32[]{:S(2)}, u32[]{:S(2)}) collective-permute-start(f32[256,128]{1,0:T(8,128)S(1)} %add.3.mine), channel_id=1, source_target_pairs={{0,4},{1,3},{2,6},{3,1},{4,0},{5,7},{6,2},{7,5},{8,12},{9,11},{10,... | collective-permute-start | bytes 393224 | tf_op jit(solution)/shard_map/ppermute | solution.py:272
  11.0 4.1 %collective-permute-start.2 = (f32[104,128]{1,0:T(8,128)S(1)}, f32[104,128]{1,0:T(8,128)S(1)}, u32[]{:S(2)}, u32[]{:S(2)}) collective-permute-start(f32[104,128]{1,0:T(8,128)S(1)} %gram.1.mine.refs_2_), channel_id=1, source_target_pairs={{0,2},{1,9},{2,0},{3,11},{4,6},{5,13},{6,4},{7,15},{8,10},{9,1},{1... | collective-permute-start | bytes 159752 | tf_op jit(solution)/shard_map/ppermute | solution.py:272
  13.0 4.1 %collective-permute-start.4 = (f32[104,128]{1,0:T(8,128)S(1)}, f32[104,128]{1,0:T(8,128)S(1)}, u32[]{:S(2)}, u32[]{:S(2)}) collective-permute-start(f32[104,128]{1,0:T(8,128)S(1)} %gram.1.mine.refs_2_), channel_id=1, source_target_pairs={{0,2},{1,5},{2,0},{3,7},{4,6},{5,1},{6,4},{7,3},{8,10},{9,13},{10,... | collective-permute-start | bytes 159752 | tf_op jit(solution)/shard_map/ppermute | solution.py:272
  15.2 4.1 %collective-permute-start.3 = (f32[104,128]{1,0:T(8,128)S(1)}, f32[104,128]{1,0:T(8,128)S(1)}, u32[]{:S(2)}, u32[]{:S(2)}) collective-permute-start(f32[104,128]{1,0:T(8,128)S(1)} %merge.1.refs_0_), channel_id=1, source_target_pairs={{0,2},{1,5},{2,0},{3,7},{4,6},{5,1},{6,4},{7,3},{8,10},{9,13},{10,... | collective-permute-start | bytes 159752 | tf_op jit(solution)/shard_map/ppermute | solution.py:272
  19.3 2.6 %collective-permute-start.5 = (f32[2,64]{1,0:T(2,128)S(1)}, f32[2,64]{1,0:T(2,128)S(1)}, u32[]{:S(2)}, u32[]{:S(2)}) collective-permute-start(f32[2,64]{1,0:T(2,128)S(1)} %finish.1.scores), channel_id=1, source_target_pairs={{0,1},{1,0},{2,3},{3,2},{4,5},{5,4},{6,7},{7,6},{8,9},{9,8},{10,11... | collective-permute-start | bytes 1544 | tf_op jit(solution)/shard_map/ppermute | solution.py:276

commit v8 on v7

--- a/solution.py
+++ b/solution.py
@@ -98,8 +98,10 @@
         )
         row = lax.broadcasted_iota(jnp.int32, (rank, 2 * rank), 0)
         lane = lax.broadcasted_iota(jnp.int32, (rank, 2 * rank), 1)
-        diag = jnp.sum(jnp.where(lane == rank + row, low, 0.0), axis=0, keepdims=True)
-        packed[rank + half :] = jnp.where(lane[:8] < rank, live[...], diag)
+        diag_in = jnp.sum(jnp.where(lane == rank + row, low, 0.0), axis=0, keepdims=True)
+        diag_out = jnp.sum(jnp.where(lane == row, high, 0.0), axis=0, keepdims=True)
+        tail = jnp.where(row[:8] == 1, live[...], diag_in + diag_out)
+        packed[rank + half :] = tail
         packed[:rank] = jnp.where(lane < rank, pltpu.roll(grams[1][:rank], rank, 1), grams[0][:rank])
 
 
@@ -117,18 +119,19 @@
     mixed = jnp.concatenate([total[:half, :rank], total[:half, rank:]], axis=0)
     turned = mixed.T
     diag = total[half : half + 1, rank:]
-    count = total[half : half + 1, :1]
+    diags = total[half : half + 1]
+    count = total[half + 1 : half + 2, :1]
     row = lax.broadcasted_iota(jnp.int32, (rank, rank), 0)
     lane = lax.broadcasted_iota(jnp.int32, (rank, rank), 1)
     eye = row == lane
     sum_out = jnp.where(lane <= row, mixed, turned)
     sum_in = jnp.where(lane > row, mixed, jnp.where(eye, diag, turned))
 
-    def divide(sums):
-        trace = jnp.sum(jnp.sum(jnp.where(eye, sums, 0.0), axis=0, keepdims=True), axis=1, keepdims=True)
-        return sums / trace + jnp.where(eye, DAMP / rank, 0.0), count / trace
-
-    return *divide(sum_out), *divide(sum_in), jnp.where(eye, 1.0, 0.0)
+    def divide(sums, diag):
+        inverse = 1.0 / jnp.sum(diag, axis=1, keepdims=True)
+        return sums * inverse + jnp.where(eye, DAMP / rank, 0.0), count * inverse
+
+    return *divide(sum_out, diags[:, :rank]), *divide(sum_in, diags[:, rank:]), jnp.where(eye, 1.0, 0.0)
 
 
 def total_square(matrix):
@@ -156,7 +159,7 @@
         return 2.0 * right - dot_hi(t_out, right), 2.0 * x_in - dot_hi(x_in, t_in)
 
     def residual(t_out, t_in):
-        return jnp.sum(total_square(eye - t_out) + total_square(eye - t_in))
+        return jnp.sum(jnp.maximum(total_square(eye - t_out), total_square(eye - t_in)))
 
     for n in range(STEPS - 1):
         right, x_in = update(t_out, t_in, right, x_in)
@@ -164,7 +167,7 @@
             t_out, t_in = square(t_out, t_in)
 
     def unfinished(state):
-        return jnp.logical_and(state[0] > 1e-5, state[1] < 40)
+        return jnp.logical_and(state[0] > 3e-5, state[1] < 40)
 
     def more(state):
         _, n, t_out, t_in, right, x_in = state

time: 22.6 us -> 22.5 us (level)
  no operation moved by 1% of the time
where the time goes in v8:
time: 22.5 us; the launch traced here: 22.4 us
  starting transfers between devices  9.19 us (41%)
  waiting for transfers between devices  8.48 us (38%)
  Pallas kernels  4.68 us (21%)
    ppermute x4, waiting for transfers between devices, swap(): return lax.ppermute(x, ('dp', 'tensor'), pairs)  7.25 us
    ppermute x4, starting transfers between devices, swap(): return lax.ppermute(x, ('dp', 'tensor'), pairs)  6.96 us
    pallas_call x1, Pallas kernels, project(): pl.pallas_call(project_kernel, out_shape=[shape(examples * seq_len, 2 * r...  3.54 us
    ppermute x2, starting transfers between devices, across(): return lax.ppermute(x, 'tensor', [(t, t ^ 1) for t in range(tensor)])  2.23 us
    ppermute x2, waiting for transfers between devices, across(): return lax.ppermute(x, 'tensor', [(t, t ^ 1) for t in range(tensor)])  1.23 us
    pallas_call x1, Pallas kernels, publish(): pl.pallas_call(publish_kernel, out_shape=jax.ShapeDtypeStruct(scores.shap...  0.57 us
    pallas_call x1, Pallas kernels, replace(): pl.pallas_call(functools.partial(replace_kernel, leads), out_shape=jax.Sh...  0.57 us
  transfers between devices with their start and end apart: 6, of which 5 were waited for; matrix products, arithmetic and copies ran while one was open for 0% of the time, Pallas kernels for 3%

profile of v8, /device:TPU:0, one launch (start us, length us, event | category | flops | bytes accessed | tf_op | source)
XLA Modules:
  0.0 22.4 jit_solution(9365161705633133026)
XLA Ops:
  0.0 0.0 copy-start
  0.0 3.5 %project.1 = (f32[256,128]{1,0:T(8,128)S(1)}, f32[8,128]{1,0:T(8,128)S(1)}) custom-call(s32[2]{0:T(128)} %lengths.1, bf16[2,128,7168]{2,1,0:T(8,128)(2,1)} %act.1, bf16[2,128,2048]{2,1,0:T(8,128)(2,1)} %grad.1, bf16[64,7168]{1,0:T(8,128)(2,1)} %bitcast.5, bf16[64,2048]{1,0:T(8,128)(2,1)} %bitcast.6), custom_call_target="tpu_custom_call" | custom-call | tf_op jit(solution)/shard_map/project/pallas_call | solution.py:255
  3.6 0.5 %collective-permute-start = (f32[256,128]{1,0:T(8,128)S(1)}, f32[256,128]{1,0:T(8,128)S(1)}, u32[]{:S(2)}, u32[]{:S(2)}) collective-permute-start(f32[256,128]{1,0:T(8,128)S(1)} %get-tuple-element.8), channel_id=1, source_target_pairs={{0,1},{1,0},{2,3},{3,2},{4,5},{5,4},{6,7},{7,6},{8,9},{9,8},{10,11... | collective-permute-start | bytes 393224 | tf_op jit(solution)/shard_map/ppermute | solution.py:279
  4.1 1.0 %collective-permute-done = f32[256,128]{1,0:T(8,128)S(1)} collective-permute-done((f32[256,128]{1,0:T(8,128)S(1)}, f32[256,128]{1,0:T(8,128)S(1)}, u32[]{:S(2)}, u32[]{:S(2)}) %collective-permute-start) | collective-permute-done | bytes 131104 | tf_op jit(solution)/shard_map/ppermute | solution.py:279
  5.1 3.0 %collective-permute-start.1 = (f32[256,128]{1,0:T(8,128)S(1)}, f32[256,128]{1,0:T(8,128)S(1)}, u32[]{:S(2)}, u32[]{:S(2)}) collective-permute-start(f32[256,128]{1,0:T(8,128)S(1)} %add.3.mine), channel_id=1, source_target_pairs={{0,4},{1,3},{2,6},{3,1},{4,0},{5,7},{6,2},{7,5},{8,12},{9,11},{10,... | collective-permute-start | bytes 393224 | tf_op jit(solution)/shard_map/ppermute | solution.py:275
  8.1 2.9 %collective-permute-done.1.theirs = f32[256,128]{1,0:T(8,128)S(1)} collective-permute-done((f32[256,128]{1,0:T(8,128)S(1)}, f32[256,128]{1,0:T(8,128)S(1)}, u32[]{:S(2)}, u32[]{:S(2)}) %collective-permute-start.1) | collective-permute-done | bytes 131104 | tf_op jit(solution)/shard_map/ppermute | solution.py:275
  11.0 1.9 %collective-permute-start.2 = (f32[104,128]{1,0:T(8,128)S(1)}, f32[104,128]{1,0:T(8,128)S(1)}, u32[]{:S(2)}, u32[]{:S(2)}) collective-permute-start(f32[104,128]{1,0:T(8,128)S(1)} %gram.1.mine.refs_2_), channel_id=1, source_target_pairs={{0,2},{1,9},{2,0},{3,11},{4,6},{5,13},{6,4},{7,15},{8,10},{9,1},{1... | collective-permute-start | bytes 159752 | tf_op jit(solution)/shard_map/ppermute | solution.py:275
  13.0 0.1 collective-permute-start.4
  13.0 2.1 %collective-permute-done.2.theirs = f32[104,128]{1,0:T(8,128)S(1)} collective-permute-done((f32[104,128]{1,0:T(8,128)S(1)}, f32[104,128]{1,0:T(8,128)S(1)}, u32[]{:S(2)}, u32[]{:S(2)}) %collective-permute-start.2) | collective-permute-done | bytes 53280 | tf_op jit(solution)/shard_map/ppermute | solution.py:275
  15.2 1.9 %collective-permute-start.3 = (f32[104,128]{1,0:T(8,128)S(1)}, f32[104,128]{1,0:T(8,128)S(1)}, u32[]{:S(2)}, u32[]{:S(2)}) collective-permute-start(f32[104,128]{1,0:T(8,128)S(1)} %merge.1.refs_0_), channel_id=1, source_target_pairs={{0,2},{1,5},{2,0},{3,7},{4,6},{5,1},{6,4},{7,3},{8,10},{9,13},{10,... | collective-permute-start | bytes 159752 | tf_op jit(solution)/shard_map/ppermute | solution.py:275
  17.1 0.0 collective-permute-done.4.refs_3_
  17.1 2.2 %collective-permute-done.3.refs_1_ = f32[104,128]{1,0:T(8,128)S(1)} collective-permute-done((f32[104,128]{1,0:T(8,128)S(1)}, f32[104,128]{1,0:T(8,128)S(1)}, u32[]{:S(2)}, u32[]{:S(2)}) %collective-permute-start.3) | collective-permute-done | bytes 53280 | tf_op jit(solution)/shard_map/ppermute | solution.py:275
  19.3 0.0 copy-done
  19.3 1.7 %collective-permute-start.5 = (f32[2,64]{1,0:T(2,128)S(1)}, f32[2,64]{1,0:T(2,128)S(1)}, u32[]{:S(2)}, u32[]{:S(2)}) collective-permute-start(f32[2,64]{1,0:T(2,128)S(1)} %finish.1.scores), channel_id=1, source_target_pairs={{0,1},{1,0},{2,3},{3,2},{4,5},{5,4},{6,7},{7,6},{8,9},{9,8},{10,11... | collective-permute-start | bytes 1544 | tf_op jit(solution)/shard_map/ppermute | solution.py:279
  21.0 0.6 %publish.1.mine = f32[2,64]{1,0:T(2,128)} custom-call(f32[2,64]{1,0:T(2,128)S(1)} %finish.1.scores), custom_call_target="tpu_custom_call" | custom-call | flops 1000000000 | tf_op jit(solution)/shard_map/publish/pallas_call | solution.py:283
  21.6 0.2 %collective-permute-done.5.theirs = f32[2,64]{1,0:T(2,128)S(1)} collective-permute-done((f32[2,64]{1,0:T(2,128)S(1)}, f32[2,64]{1,0:T(2,128)S(1)}, u32[]{:S(2)}, u32[]{:S(2)}) %collective-permute-start.5) | collective-permute-done | bytes 544 | tf_op jit(solution)/shard_map/ppermute | solution.py:279
  21.8 0.6 %replace.1 = f32[2,64]{1,0:T(2,128)} custom-call(f32[2,64]{1,0:T(2,128)S(1)} %collective-permute-done.5.theirs, f32[2,64]{1,0:T(2,128)} %publish.1.mine), custom_call_target="tpu_custom_call", output_to_operand_aliasing={{}: (1, {})} | custom-call | tf_op jit(solution)/shard_map/replace/pallas_call | solution.py:296
  (4 shorter events, 0.0 us)
Async XLA Ops:
  0.0 19.3 %copy-start = (s32[64]{0:T(128)S(1)}, s32[64]{0:T(128)}, u32[]{:S(2)}) copy-start(s32[64]{0:T(128)} %param.11) | copy-start | bytes 772
  3.6 1.5 %collective-permute-start = (f32[256,128]{1,0:T(8,128)S(1)}, f32[256,128]{1,0:T(8,128)S(1)}, u32[]{:S(2)}, u32[]{:S(2)}) collective-permute-start(f32[256,128]{1,0:T(8,128)S(1)} %get-tuple-element.8), channel_id=1, source_target_pairs={{0,1},{1,0},{2,3},{3,2},{4,5},{5,4},{6,7},{7,6},{8,9},{9,8},{10,11... | collective-permute-start | bytes 393224 | tf_op jit(solution)/shard_map/ppermute | solution.py:279
  5.1 5.9 %collective-permute-start.1 = (f32[256,128]{1,0:T(8,128)S(1)}, f32[256,128]{1,0:T(8,128)S(1)}, u32[]{:S(2)}, u32[]{:S(2)}) collective-permute-start(f32[256,128]{1,0:T(8,128)S(1)} %add.3.mine), channel_id=1, source_target_pairs={{0,4},{1,3},{2,6},{3,1},{4,0},{5,7},{6,2},{7,5},{8,12},{9,11},{10,... | collective-permute-start | bytes 393224 | tf_op jit(solution)/shard_map/ppermute | solution.py:275
  11.0 4.1 %collective-permute-start.2 = (f32[104,128]{1,0:T(8,128)S(1)}, f32[104,128]{1,0:T(8,128)S(1)}, u32[]{:S(2)}, u32[]{:S(2)}) collective-permute-start(f32[104,128]{1,0:T(8,128)S(1)} %gram.1.mine.refs_2_), channel_id=1, source_target_pairs={{0,2},{1,9},{2,0},{3,11},{4,6},{5,13},{6,4},{7,15},{8,10},{9,1},{1... | collective-permute-start | bytes 159752 | tf_op jit(solution)/shard_map/ppermute | solution.py:275
  13.0 4.1 %collective-permute-start.4 = (f32[104,128]{1,0:T(8,128)S(1)}, f32[104,128]{1,0:T(8,128)S(1)}, u32[]{:S(2)}, u32[]{:S(2)}) collective-permute-start(f32[104,128]{1,0:T(8,128)S(1)} %gram.1.mine.refs_2_), channel_id=1, source_target_pairs={{0,2},{1,5},{2,0},{3,7},{4,6},{5,1},{6,4},{7,3},{8,10},{9,13},{10,... | collective-permute-start | bytes 159752 | tf_op jit(solution)/shard_map/ppermute | solution.py:275
  15.2 4.1 %collective-permute-start.3 = (f32[104,128]{1,0:T(8,128)S(1)}, f32[104,128]{1,0:T(8,128)S(1)}, u32[]{:S(2)}, u32[]{:S(2)}) collective-permute-start(f32[104,128]{1,0:T(8,128)S(1)} %merge.1.refs_0_), channel_id=1, source_target_pairs={{0,2},{1,5},{2,0},{3,7},{4,6},{5,1},{6,4},{7,3},{8,10},{9,13},{10,... | collective-permute-start | bytes 159752 | tf_op jit(solution)/shard_map/ppermute | solution.py:275
  19.3 2.5 %collective-permute-start.5 = (f32[2,64]{1,0:T(2,128)S(1)}, f32[2,64]{1,0:T(2,128)S(1)}, u32[]{:S(2)}, u32[]{:S(2)}) collective-permute-start(f32[2,64]{1,0:T(2,128)S(1)} %finish.1.scores), channel_id=1, source_target_pairs={{0,1},{1,0},{2,3},{3,2},{4,5},{5,4},{6,7},{7,6},{8,9},{9,8},{10,11... | collective-permute-start | bytes 1544 | tf_op jit(solution)/shard_map/ppermute | solution.py:279

commit v9 on v8

--- a/solution.py
+++ b/solution.py
@@ -193,29 +193,27 @@
         left, inv_in, c_out, c_in = solve(rank, total[0], pairs[masks.index(0)])
         left = left * c_out
         zero = jnp.zeros((rank, rank), jnp.float32)
-        right = jnp.concatenate(
-            [jnp.concatenate([inv_in, zero], axis=1), jnp.concatenate([zero, inv_in], axis=1)], axis=0
-        )
-        straight = dot_hi(left, right) * c_in
-        crossed = pltpu.roll(straight, rank, 1)
+        beside = jnp.concatenate([inv_in, zero, zero, inv_in], axis=1)
+        before = jnp.concatenate([zero, inv_in, inv_in, zero], axis=1)
+        both = dot_hi(left, jnp.concatenate([beside, before], axis=0)) * c_in
+        straight, crossed = both[:, : 2 * rank], both[:, 2 * rank :]
         size = len(pairs)
         sums = [jnp.sum(pair * straight, axis=0, keepdims=True) for pair in pairs]
         sums += [jnp.sum(pair * crossed, axis=0, keepdims=True) for pair in pairs]
         sums = jnp.concatenate(sums, axis=0)
-        num = queries.shape[1]
-        index = lax.broadcasted_iota(jnp.int32, (2 * size, num), 0) % size
-        mask = sum(jnp.where(index == n, value, 0) for n, value in enumerate(masks))
-        device = lax.axis_index("dp") ^ mask
+        inner = lax.broadcasted_iota(jnp.int32, sums.shape, 1) < rank
+        second = jnp.sum(jnp.where(inner, sums, 0.0), axis=1, keepdims=True)
+        first = jnp.sum(jnp.where(inner, 0.0, sums), axis=1, keepdims=True)
+        row = lax.broadcasted_iota(jnp.int32, (2 * size, queries.shape[1]), 0)
+        mask = sum(jnp.where(row % size == n, value, 0) for n, value in enumerate(masks))
+        example = 2 * (lax.axis_index("dp") ^ mask)
         chosen = queries[...]
-        second = jnp.where(chosen == 2 * device + 1, jnp.sum(sums[:, :rank], axis=1, keepdims=True), 0.0)
-        first = jnp.where(chosen == 2 * device, jnp.sum(sums[:, rank:], axis=1, keepdims=True), 0.0)
         scale = 1.0 / (rank * seq_len)
-        scores[0:1, :] = scale * jnp.sum(
-            jnp.concatenate([first[:size], second[size:]], axis=0), axis=0, keepdims=True
-        )
-        scores[1:2, :] = scale * jnp.sum(
-            jnp.concatenate([second[:size], first[size:]], axis=0), axis=0, keepdims=True
-        )
+        second = jnp.where(chosen == example + 1, scale * second, 0.0)
+        first = jnp.where(chosen == example, scale * first, 0.0)
+        same = row < size
+        scores[0:1, :] = jnp.sum(jnp.where(same, first, second), axis=0, keepdims=True)
+        scores[1:2, :] = jnp.sum(jnp.where(same, second, first), axis=0, keepdims=True)
 
 
 def publish_kernel(scores, out, sem):

time: 22.5 us -> 22.2 us (0.987)
  no operation moved by 1% of the time
where the time goes in v9:
time: 22.2 us; the launch traced here: 22.3 us
  starting transfers between devices  9.08 us (41%)
  waiting for transfers between devices  8.48 us (38%)
  Pallas kernels  4.68 us (21%)
    ppermute x4, waiting for transfers between devices, swap(): return lax.ppermute(x, ('dp', 'tensor'), pairs)  7.25 us
    ppermute x4, starting transfers between devices, swap(): return lax.ppermute(x, ('dp', 'tensor'), pairs)  6.96 us
    pallas_call x1, Pallas kernels, project(): pl.pallas_call(project_kernel, out_shape=[shape(examples * seq_len, 2 * r...  3.54 us
    ppermute x2, starting transfers between devices, across(): return lax.ppermute(x, 'tensor', [(t, t ^ 1) for t in range(tensor)])  2.12 us
    ppermute x2, waiting for transfers between devices, across(): return lax.ppermute(x, 'tensor', [(t, t ^ 1) for t in range(tensor)])  1.23 us
    pallas_call x1, Pallas kernels, publish(): pl.pallas_call(publish_kernel, out_shape=jax.ShapeDtypeStruct(scores.shap...  0.57 us
    pallas_call x1, Pallas kernels, replace(): pl.pallas_call(functools.partial(replace_kernel, leads), out_shape=jax.Sh...  0.57 us
  transfers between devices with their start and end apart: 6, of which 5 were waited for; matrix products, arithmetic and copies ran while one was open for 0% of the time, Pallas kernels for 3%

profile of v9, /device:TPU:0, one launch (start us, length us, event | category | flops | bytes accessed | tf_op | source)
XLA Modules:
  0.0 22.3 jit_solution(11626732801119635233)
XLA Ops:
  0.0 0.0 copy-start
  0.0 3.5 %project.1 = (f32[256,128]{1,0:T(8,128)S(1)}, f32[8,128]{1,0:T(8,128)S(1)}) custom-call(s32[2]{0:T(128)} %lengths.1, bf16[2,128,7168]{2,1,0:T(8,128)(2,1)} %act.1, bf16[2,128,2048]{2,1,0:T(8,128)(2,1)} %grad.1, bf16[64,7168]{1,0:T(8,128)(2,1)} %bitcast.5, bf16[64,2048]{1,0:T(8,128)(2,1)} %bitcast.6), custom_call_target="tpu_custom_call" | custom-call | tf_op jit(solution)/shard_map/project/pallas_call | solution.py:253
  3.6 0.5 %collective-permute-start = (f32[256,128]{1,0:T(8,128)S(1)}, f32[256,128]{1,0:T(8,128)S(1)}, u32[]{:S(2)}, u32[]{:S(2)}) collective-permute-start(f32[256,128]{1,0:T(8,128)S(1)} %get-tuple-element.8), channel_id=1, source_target_pairs={{0,1},{1,0},{2,3},{3,2},{4,5},{5,4},{6,7},{7,6},{8,9},{9,8},{10,11... | collective-permute-start | bytes 393224 | tf_op jit(solution)/shard_map/ppermute | solution.py:277
  4.1 1.0 %collective-permute-done = f32[256,128]{1,0:T(8,128)S(1)} collective-permute-done((f32[256,128]{1,0:T(8,128)S(1)}, f32[256,128]{1,0:T(8,128)S(1)}, u32[]{:S(2)}, u32[]{:S(2)}) %collective-permute-start) | collective-permute-done | bytes 131104 | tf_op jit(solution)/shard_map/ppermute | solution.py:277
  5.1 3.0 %collective-permute-start.1 = (f32[256,128]{1,0:T(8,128)S(1)}, f32[256,128]{1,0:T(8,128)S(1)}, u32[]{:S(2)}, u32[]{:S(2)}) collective-permute-start(f32[256,128]{1,0:T(8,128)S(1)} %add.3.mine), channel_id=1, source_target_pairs={{0,4},{1,3},{2,6},{3,1},{4,0},{5,7},{6,2},{7,5},{8,12},{9,11},{10,... | collective-permute-start | bytes 393224 | tf_op jit(solution)/shard_map/ppermute | solution.py:273
  8.1 2.9 %collective-permute-done.1.theirs = f32[256,128]{1,0:T(8,128)S(1)} collective-permute-done((f32[256,128]{1,0:T(8,128)S(1)}, f32[256,128]{1,0:T(8,128)S(1)}, u32[]{:S(2)}, u32[]{:S(2)}) %collective-permute-start.1) | collective-permute-done | bytes 131104 | tf_op jit(solution)/shard_map/ppermute | solution.py:273
  11.0 1.9 %collective-permute-start.2 = (f32[104,128]{1,0:T(8,128)S(1)}, f32[104,128]{1,0:T(8,128)S(1)}, u32[]{:S(2)}, u32[]{:S(2)}) collective-permute-start(f32[104,128]{1,0:T(8,128)S(1)} %gram.1.mine.refs_2_), channel_id=1, source_target_pairs={{0,2},{1,9},{2,0},{3,11},{4,6},{5,13},{6,4},{7,15},{8,10},{9,1},{1... | collective-permute-start | bytes 159752 | tf_op jit(solution)/shard_map/ppermute | solution.py:273
  13.0 0.1 collective-permute-start.4
  13.0 2.1 %collective-permute-done.2.theirs = f32[104,128]{1,0:T(8,128)S(1)} collective-permute-done((f32[104,128]{1,0:T(8,128)S(1)}, f32[104,128]{1,0:T(8,128)S(1)}, u32[]{:S(2)}, u32[]{:S(2)}) %collective-permute-start.2) | collective-permute-done | bytes 53280 | tf_op jit(solution)/shard_map/ppermute | solution.py:273
  15.2 1.9 %collective-permute-start.3 = (f32[104,128]{1,0:T(8,128)S(1)}, f32[104,128]{1,0:T(8,128)S(1)}, u32[]{:S(2)}, u32[]{:S(2)}) collective-permute-start(f32[104,128]{1,0:T(8,128)S(1)} %merge.1.refs_0_), channel_id=1, source_target_pairs={{0,2},{1,5},{2,0},{3,7},{4,6},{5,1},{6,4},{7,3},{8,10},{9,13},{10,... | collective-permute-start | bytes 159752 | tf_op jit(solution)/shard_map/ppermute | solution.py:273
  17.1 0.0 collective-permute-done.4.refs_3_
  17.1 2.2 %collective-permute-done.3.refs_1_ = f32[104,128]{1,0:T(8,128)S(1)} collective-permute-done((f32[104,128]{1,0:T(8,128)S(1)}, f32[104,128]{1,0:T(8,128)S(1)}, u32[]{:S(2)}, u32[]{:S(2)}) %collective-permute-start.3) | collective-permute-done | bytes 53280 | tf_op jit(solution)/shard_map/ppermute | solution.py:273
  19.3 0.0 copy-done
  19.3 1.6 %collective-permute-start.5 = (f32[2,64]{1,0:T(2,128)S(1)}, f32[2,64]{1,0:T(2,128)S(1)}, u32[]{:S(2)}, u32[]{:S(2)}) collective-permute-start(f32[2,64]{1,0:T(2,128)S(1)} %finish.1.scores), channel_id=1, source_target_pairs={{0,1},{1,0},{2,3},{3,2},{4,5},{5,4},{6,7},{7,6},{8,9},{9,8},{10,11... | collective-permute-start | bytes 1544 | tf_op jit(solution)/shard_map/ppermute | solution.py:277
  20.9 0.6 %publish.1.mine = f32[2,64]{1,0:T(2,128)} custom-call(f32[2,64]{1,0:T(2,128)S(1)} %finish.1.scores), custom_call_target="tpu_custom_call" | custom-call | flops 1000000000 | tf_op jit(solution)/shard_map/publish/pallas_call | solution.py:281
  21.5 0.2 %collective-permute-done.5.theirs = f32[2,64]{1,0:T(2,128)S(1)} collective-permute-done((f32[2,64]{1,0:T(2,128)S(1)}, f32[2,64]{1,0:T(2,128)S(1)}, u32[]{:S(2)}, u32[]{:S(2)}) %collective-permute-start.5) | collective-permute-done | bytes 544 | tf_op jit(solution)/shard_map/ppermute | solution.py:277
  21.7 0.6 %replace.1 = f32[2,64]{1,0:T(2,128)} custom-call(f32[2,64]{1,0:T(2,128)S(1)} %collective-permute-done.5.theirs, f32[2,64]{1,0:T(2,128)} %publish.1.mine), custom_call_target="tpu_custom_call", output_to_operand_aliasing={{}: (1, {})} | custom-call | tf_op jit(solution)/shard_map/replace/pallas_call | solution.py:294
  (4 shorter events, 0.0 us)
Async XLA Ops:
  0.0 19.3 %copy-start = (s32[64]{0:T(128)S(1)}, s32[64]{0:T(128)}, u32[]{:S(2)}) copy-start(s32[64]{0:T(128)} %param.11) | copy-start | bytes 772
  3.6 1.5 %collective-permute-start = (f32[256,128]{1,0:T(8,128)S(1)}, f32[256,128]{1,0:T(8,128)S(1)}, u32[]{:S(2)}, u32[]{:S(2)}) collective-permute-start(f32[256,128]{1,0:T(8,128)S(1)} %get-tuple-element.8), channel_id=1, source_target_pairs={{0,1},{1,0},{2,3},{3,2},{4,5},{5,4},{6,7},{7,6},{8,9},{9,8},{10,11... | collective-permute-start | bytes 393224 | tf_op jit(solution)/shard_map/ppermute | solution.py:277
  5.1 5.9 %collective-permute-start.1 = (f32[256,128]{1,0:T(8,128)S(1)}, f32[256,128]{1,0:T(8,128)S(1)}, u32[]{:S(2)}, u32[]{:S(2)}) collective-permute-start(f32[256,128]{1,0:T(8,128)S(1)} %add.3.mine), channel_id=1, source_target_pairs={{0,4},{1,3},{2,6},{3,1},{4,0},{5,7},{6,2},{7,5},{8,12},{9,11},{10,... | collective-permute-start | bytes 393224 | tf_op jit(solution)/shard_map/ppermute | solution.py:273
  11.0 4.1 %collective-permute-start.2 = (f32[104,128]{1,0:T(8,128)S(1)}, f32[104,128]{1,0:T(8,128)S(1)}, u32[]{:S(2)}, u32[]{:S(2)}) collective-permute-start(f32[104,128]{1,0:T(8,128)S(1)} %gram.1.mine.refs_2_), channel_id=1, source_target_pairs={{0,2},{1,9},{2,0},{3,11},{4,6},{5,13},{6,4},{7,15},{8,10},{9,1},{1... | collective-permute-start | bytes 159752 | tf_op jit(solution)/shard_map/ppermute | solution.py:273
  13.0 4.1 %collective-permute-start.4 = (f32[104,128]{1,0:T(8,128)S(1)}, f32[104,128]{1,0:T(8,128)S(1)}, u32[]{:S(2)}, u32[]{:S(2)}) collective-permute-start(f32[104,128]{1,0:T(8,128)S(1)} %gram.1.mine.refs_2_), channel_id=1, source_target_pairs={{0,2},{1,5},{2,0},{3,7},{4,6},{5,1},{6,4},{7,3},{8,10},{9,13},{10,... | collective-permute-start | bytes 159752 | tf_op jit(solution)/shard_map/ppermute | solution.py:273
  15.2 4.1 %collective-permute-start.3 = (f32[104,128]{1,0:T(8,128)S(1)}, f32[104,128]{1,0:T(8,128)S(1)}, u32[]{:S(2)}, u32[]{:S(2)}) collective-permute-start(f32[104,128]{1,0:T(8,128)S(1)} %merge.1.refs_0_), channel_id=1, source_target_pairs={{0,2},{1,5},{2,0},{3,7},{4,6},{5,1},{6,4},{7,3},{8,10},{9,13},{10,... | collective-permute-start | bytes 159752 | tf_op jit(solution)/shard_map/ppermute | solution.py:273
  19.3 2.4 %collective-permute-start.5 = (f32[2,64]{1,0:T(2,128)S(1)}, f32[2,64]{1,0:T(2,128)S(1)}, u32[]{:S(2)}, u32[]{:S(2)}) collective-permute-start(f32[2,64]{1,0:T(2,128)S(1)} %finish.1.scores), channel_id=1, source_target_pairs={{0,1},{1,0},{2,3},{3,2},{4,5},{5,4},{6,7},{7,6},{8,9},{9,8},{10,11... | collective-permute-start | bytes 1544 | tf_op jit(solution)/shard_map/ppermute | solution.py:277

commit v10 on v9

--- a/solution.py
+++ b/solution.py
@@ -12,6 +12,7 @@
 HBM = pl.BlockSpec(memory_space=pltpu.HBM)
 DAMP = 0.1
 STEPS = 5
+LEAST = 3e-5
 
 
 def dot_nt(a, b):
@@ -138,7 +139,7 @@
     return jnp.sum(jnp.sum(matrix * matrix, axis=0, keepdims=True), axis=1, keepdims=True)
 
 
-def solve(rank, total, right):
+def solve(rank, total, right, held):
     d_out, c_out, d_in, c_in, eye = normalised(rank, total)
 
     def scale(matrix):
@@ -163,25 +164,36 @@
 
     for n in range(STEPS - 1):
         right, x_in = update(t_out, t_in, right, x_in)
+        if n == STEPS - 3:
+            early = residual(t_out, t_in)
         if n < STEPS - 2:
             t_out, t_in = square(t_out, t_in)
 
-    def unfinished(state):
-        return jnp.logical_and(state[0] > 3e-5, state[1] < 40)
-
-    def more(state):
-        _, n, t_out, t_in, right, x_in = state
-        t_out, t_in = square(t_out, t_in)
-        right, x_in = update(t_out, t_in, right, x_in)
-        return residual(t_out, t_in), n + 1, t_out, t_in, right, x_in
-
-    state = (residual(t_out, t_in), jnp.int32(0), t_out, t_in, right, x_in)
-    _, _, _, _, right, x_in = lax.while_loop(unfinished, more, state)
+    for ref, value in zip(held, (t_out, t_in, right, x_in)):
+        ref[...] = value
+
+    @pl.when(early * early > 5e-5)
+    def _():
+        def unfinished(state):
+            return jnp.logical_and(state[0] > LEAST, state[1] < 40)
+
+        def more(state):
+            _, n, t_out, t_in, right, x_in = state
+            t_out, t_in = square(t_out, t_in)
+            right, x_in = update(t_out, t_in, right, x_in)
+            return residual(t_out, t_in), n + 1, t_out, t_in, right, x_in
+
+        state = (residual(held[0][...], held[1][...]), jnp.int32(0), *[ref[...] for ref in held])
+        state = lax.while_loop(unfinished, more, state)
+        held[2][...] = state[4]
+        held[3][...] = state[5]
+
+    right, x_in = held[2][...], held[3][...]
     return right, x_in, c_out * s_out, c_in * s_in
 
 
 def finish_kernel(seq_len, leads, masks, count, queries, *refs):
-    blocks, scores = refs[:-1], refs[-1]
+    blocks, scores, held = refs[:-5], refs[-5], refs[-4:]
     rank = blocks[0].shape[1] // 2
 
     @pl.when(leads())
@@ -190,7 +202,7 @@
         total = [ref[rank:] for ref in blocks[:count]]
         while len(total) > 1:
             total = [total[n] + total[n + 1] for n in range(0, len(total), 2)]
-        left, inv_in, c_out, c_in = solve(rank, total[0], pairs[masks.index(0)])
+        left, inv_in, c_out, c_in = solve(rank, total[0], pairs[masks.index(0)], held)
         left = left * c_out
         zero = jnp.zeros((rank, rank), jnp.float32)
         beside = jnp.concatenate([inv_in, zero, zero, inv_in], axis=1)
@@ -234,12 +246,13 @@
     return pltpu.VMEM(dims, jnp.float32)
 
 
-def call(kernel, name, out_shape, *operands):
+def call(kernel, name, out_shape, *operands, scratch=()):
     return pl.pallas_call(
         kernel,
         out_shape=out_shape,
         in_specs=[VMEM] * len(operands),
         out_specs=VMEM,
+        scratch_shapes=list(scratch),
         compiler_params=pltpu.CompilerParams(vmem_limit_bytes=4 * 2**20),
         name=name,
     )(*[pltpu.with_memory_space_constraint(operand, pltpu.VMEM) for operand in operands])
@@ -350,6 +363,7 @@
         shape(examples, num),
         query_ids.reshape(1, num),
         *blocks,
+        scratch=[shape(rank, rank), shape(rank, rank), shape(rank, 2 * rank), shape(rank, rank)],
     )
     if paired:
         other = across(scores, tensor)

time: 22.2 us -> 22.6 us (1.018); the launches traced: 22.3 us -> 22.4 us
  no operation moved by 1% of the time
where the time goes in v10:
time: 22.6 us; the launch traced here: 22.4 us
  starting transfers between devices  9.21 us (41%)
  waiting for transfers between devices  8.48 us (38%)
  Pallas kernels  4.68 us (21%)
    ppermute x4, waiting for transfers between devices, swap(): return lax.ppermute(x, ('dp', 'tensor'), pairs)  7.25 us
    ppermute x4, starting transfers between devices, swap(): return lax.ppermute(x, ('dp', 'tensor'), pairs)  6.96 us
    pallas_call x1, Pallas kernels, project(): pl.pallas_call(project_kernel, out_shape=[shape(examples * seq_len, 2 * r...  3.54 us
    ppermute x2, starting transfers between devices, across(): return lax.ppermute(x, 'tensor', [(t, t ^ 1) for t in range(tensor)])  2.25 us
    ppermute x2, waiting for transfers between devices, across(): return lax.ppermute(x, 'tensor', [(t, t ^ 1) for t in range(tensor)])  1.23 us
    pallas_call x1, Pallas kernels, publish(): pl.pallas_call(publish_kernel, out_shape=jax.ShapeDtypeStruct(scores.shap...  0.57 us
    pallas_call x1, Pallas kernels, replace(): pl.pallas_call(functools.partial(replace_kernel, leads), out_shape=jax.Sh...  0.57 us
  transfers between devices with their start and end apart: 6, of which 5 were waited for; matrix products, arithmetic and copies ran while one was open for 0% of the time, Pallas kernels for 3%

profile of v10, /device:TPU:0, one launch (start us, length us, event | category | flops | bytes accessed | tf_op | source)
XLA Modules:
  0.0 22.4 jit_solution(2389757642673981028)
XLA Ops:
  0.0 0.0 copy-start
  0.0 3.5 %project.1 = (f32[256,128]{1,0:T(8,128)S(1)}, f32[8,128]{1,0:T(8,128)S(1)}) custom-call(s32[2]{0:T(128)} %lengths.1, bf16[2,128,7168]{2,1,0:T(8,128)(2,1)} %act.1, bf16[2,128,2048]{2,1,0:T(8,128)(2,1)} %grad.1, bf16[64,7168]{1,0:T(8,128)(2,1)} %bitcast.5, bf16[64,2048]{1,0:T(8,128)(2,1)} %bitcast.6), custom_call_target="tpu_custom_call" | custom-call | tf_op jit(solution)/shard_map/project/pallas_call | solution.py:266
  3.6 0.5 %collective-permute-start = (f32[256,128]{1,0:T(8,128)S(1)}, f32[256,128]{1,0:T(8,128)S(1)}, u32[]{:S(2)}, u32[]{:S(2)}) collective-permute-start(f32[256,128]{1,0:T(8,128)S(1)} %get-tuple-element.8), channel_id=1, source_target_pairs={{0,1},{1,0},{2,3},{3,2},{4,5},{5,4},{6,7},{7,6},{8,9},{9,8},{10,11... | collective-permute-start | bytes 393224 | tf_op jit(solution)/shard_map/ppermute | solution.py:290
  4.1 1.0 %collective-permute-done = f32[256,128]{1,0:T(8,128)S(1)} collective-permute-done((f32[256,128]{1,0:T(8,128)S(1)}, f32[256,128]{1,0:T(8,128)S(1)}, u32[]{:S(2)}, u32[]{:S(2)}) %collective-permute-start) | collective-permute-done | bytes 131104 | tf_op jit(solution)/shard_map/ppermute | solution.py:290
  5.1 3.0 %collective-permute-start.1 = (f32[256,128]{1,0:T(8,128)S(1)}, f32[256,128]{1,0:T(8,128)S(1)}, u32[]{:S(2)}, u32[]{:S(2)}) collective-permute-start(f32[256,128]{1,0:T(8,128)S(1)} %add.3.mine), channel_id=1, source_target_pairs={{0,4},{1,3},{2,6},{3,1},{4,0},{5,7},{6,2},{7,5},{8,12},{9,11},{10,... | collective-permute-start | bytes 393224 | tf_op jit(solution)/shard_map/ppermute | solution.py:286
  8.1 2.9 %collective-permute-done.1.theirs = f32[256,128]{1,0:T(8,128)S(1)} collective-permute-done((f32[256,128]{1,0:T(8,128)S(1)}, f32[256,128]{1,0:T(8,128)S(1)}, u32[]{:S(2)}, u32[]{:S(2)}) %collective-permute-start.1) | collective-permute-done | bytes 131104 | tf_op jit(solution)/shard_map/ppermute | solution.py:286
  11.0 1.9 %collective-permute-start.2 = (f32[104,128]{1,0:T(8,128)S(1)}, f32[104,128]{1,0:T(8,128)S(1)}, u32[]{:S(2)}, u32[]{:S(2)}) collective-permute-start(f32[104,128]{1,0:T(8,128)S(1)} %gram.1.mine.refs_2_), channel_id=1, source_target_pairs={{0,2},{1,9},{2,0},{3,11},{4,6},{5,13},{6,4},{7,15},{8,10},{9,1},{1... | collective-permute-start | bytes 159752 | tf_op jit(solution)/shard_map/ppermute | solution.py:286
  13.0 0.1 collective-permute-start.4
  13.0 2.1 %collective-permute-done.2.theirs = f32[104,128]{1,0:T(8,128)S(1)} collective-permute-done((f32[104,128]{1,0:T(8,128)S(1)}, f32[104,128]{1,0:T(8,128)S(1)}, u32[]{:S(2)}, u32[]{:S(2)}) %collective-permute-start.2) | collective-permute-done | bytes 53280 | tf_op jit(solution)/shard_map/ppermute | solution.py:286
  15.2 1.9 %collective-permute-start.3 = (f32[104,128]{1,0:T(8,128)S(1)}, f32[104,128]{1,0:T(8,128)S(1)}, u32[]{:S(2)}, u32[]{:S(2)}) collective-permute-start(f32[104,128]{1,0:T(8,128)S(1)} %merge.1.refs_0_), channel_id=1, source_target_pairs={{0,2},{1,5},{2,0},{3,7},{4,6},{5,1},{6,4},{7,3},{8,10},{9,13},{10,... | collective-permute-start | bytes 159752 | tf_op jit(solution)/shard_map/ppermute | solution.py:286
  17.1 0.0 collective-permute-done.4.refs_3_
  17.1 2.2 %collective-permute-done.3.refs_1_ = f32[104,128]{1,0:T(8,128)S(1)} collective-permute-done((f32[104,128]{1,0:T(8,128)S(1)}, f32[104,128]{1,0:T(8,128)S(1)}, u32[]{:S(2)}, u32[]{:S(2)}) %collective-permute-start.3) | collective-permute-done | bytes 53280 | tf_op jit(solution)/shard_map/ppermute | solution.py:286
  19.3 0.0 copy-done
  19.3 1.7 %collective-permute-start.5 = (f32[2,64]{1,0:T(2,128)S(1)}, f32[2,64]{1,0:T(2,128)S(1)}, u32[]{:S(2)}, u32[]{:S(2)}) collective-permute-start(f32[2,64]{1,0:T(2,128)S(1)} %finish.1.scores), channel_id=1, source_target_pairs={{0,1},{1,0},{2,3},{3,2},{4,5},{5,4},{6,7},{7,6},{8,9},{9,8},{10,11... | collective-permute-start | bytes 1544 | tf_op jit(solution)/shard_map/ppermute | solution.py:290
  21.0 0.6 %publish.1.mine = f32[2,64]{1,0:T(2,128)} custom-call(f32[2,64]{1,0:T(2,128)S(1)} %finish.1.scores), custom_call_target="tpu_custom_call" | custom-call | flops 1000000000 | tf_op jit(solution)/shard_map/publish/pallas_call | solution.py:294
  21.6 0.2 %collective-permute-done.5.theirs = f32[2,64]{1,0:T(2,128)S(1)} collective-permute-done((f32[2,64]{1,0:T(2,128)S(1)}, f32[2,64]{1,0:T(2,128)S(1)}, u32[]{:S(2)}, u32[]{:S(2)}) %collective-permute-start.5) | collective-permute-done | bytes 544 | tf_op jit(solution)/shard_map/ppermute | solution.py:290
  21.8 0.6 %replace.1 = f32[2,64]{1,0:T(2,128)} custom-call(f32[2,64]{1,0:T(2,128)S(1)} %collective-permute-done.5.theirs, f32[2,64]{1,0:T(2,128)} %publish.1.mine), custom_call_target="tpu_custom_call", output_to_operand_aliasing={{}: (1, {})} | custom-call | tf_op jit(solution)/shard_map/replace/pallas_call | solution.py:307
  (4 shorter events, 0.0 us)
Async XLA Ops:
  0.0 19.3 %copy-start = (s32[64]{0:T(128)S(1)}, s32[64]{0:T(128)}, u32[]{:S(2)}) copy-start(s32[64]{0:T(128)} %param.11) | copy-start | bytes 772
  3.6 1.5 %collective-permute-start = (f32[256,128]{1,0:T(8,128)S(1)}, f32[256,128]{1,0:T(8,128)S(1)}, u32[]{:S(2)}, u32[]{:S(2)}) collective-permute-start(f32[256,128]{1,0:T(8,128)S(1)} %get-tuple-element.8), channel_id=1, source_target_pairs={{0,1},{1,0},{2,3},{3,2},{4,5},{5,4},{6,7},{7,6},{8,9},{9,8},{10,11... | collective-permute-start | bytes 393224 | tf_op jit(solution)/shard_map/ppermute | solution.py:290
  5.1 5.9 %collective-permute-start.1 = (f32[256,128]{1,0:T(8,128)S(1)}, f32[256,128]{1,0:T(8,128)S(1)}, u32[]{:S(2)}, u32[]{:S(2)}) collective-permute-start(f32[256,128]{1,0:T(8,128)S(1)} %add.3.mine), channel_id=1, source_target_pairs={{0,4},{1,3},{2,6},{3,1},{4,0},{5,7},{6,2},{7,5},{8,12},{9,11},{10,... | collective-permute-start | bytes 393224 | tf_op jit(solution)/shard_map/ppermute | solution.py:286
  11.0 4.1 %collective-permute-start.2 = (f32[104,128]{1,0:T(8,128)S(1)}, f32[104,128]{1,0:T(8,128)S(1)}, u32[]{:S(2)}, u32[]{:S(2)}) collective-permute-start(f32[104,128]{1,0:T(8,128)S(1)} %gram.1.mine.refs_2_), channel_id=1, source_target_pairs={{0,2},{1,9},{2,0},{3,11},{4,6},{5,13},{6,4},{7,15},{8,10},{9,1},{1... | collective-permute-start | bytes 159752 | tf_op jit(solution)/shard_map/ppermute | solution.py:286
  13.0 4.1 %collective-permute-start.4 = (f32[104,128]{1,0:T(8,128)S(1)}, f32[104,128]{1,0:T(8,128)S(1)}, u32[]{:S(2)}, u32[]{:S(2)}) collective-permute-start(f32[104,128]{1,0:T(8,128)S(1)} %gram.1.mine.refs_2_), channel_id=1, source_target_pairs={{0,2},{1,5},{2,0},{3,7},{4,6},{5,1},{6,4},{7,3},{8,10},{9,13},{10,... | collective-permute-start | bytes 159752 | tf_op jit(solution)/shard_map/ppermute | solution.py:286
  15.2 4.1 %collective-permute-start.3 = (f32[104,128]{1,0:T(8,128)S(1)}, f32[104,128]{1,0:T(8,128)S(1)}, u32[]{:S(2)}, u32[]{:S(2)}) collective-permute-start(f32[104,128]{1,0:T(8,128)S(1)} %merge.1.refs_0_), channel_id=1, source_target_pairs={{0,2},{1,5},{2,0},{3,7},{4,6},{5,1},{6,4},{7,3},{8,10},{9,13},{10,... | collective-permute-start | bytes 159752 | tf_op jit(solution)/shard_map/ppermute | solution.py:286
  19.3 2.6 %collective-permute-start.5 = (f32[2,64]{1,0:T(2,128)S(1)}, f32[2,64]{1,0:T(2,128)S(1)}, u32[]{:S(2)}, u32[]{:S(2)}) collective-permute-start(f32[2,64]{1,0:T(2,128)S(1)} %finish.1.scores), channel_id=1, source_target_pairs={{0,1},{1,0},{2,3},{3,2},{4,5},{5,4},{6,7},{7,6},{8,9},{9,8},{10,11... | collective-permute-start | bytes 1544 | tf_op jit(solution)/shard_map/ppermute | solution.py:290

commit v11 on v9

--- a/solution.py
+++ b/solution.py
@@ -22,7 +22,7 @@
     return jnp.dot(a, b, precision=HIGH, preferred_element_type=jnp.float32)
 
 
-def project_kernel(lengths, act, grad, proj_in, proj_out, sketch, live, len_s, act_v, grad_v, pin_v, pout_v, out_v, in_v, sems):
+def project_kernel(lengths, act, grad, proj_in, proj_out, sketch, live, len_s, act_v, grad_v, pin_v, pout_v, in_v, sems):
     examples, seq_len, hidden = act.shape
     rank = proj_in.shape[0]
     tokens = examples * seq_len
@@ -35,19 +35,29 @@
         copy.start()
         copies.append(copy)
 
+    begin(lengths, len_s)
     begin(proj_out, pout_v)
     begin(grad, grad_v)
     for n in range(stages - 1):
         span = pl.ds(n * width, width)
         begin(proj_in.at[:, span], pin_v.at[:, span])
         begin(act.at[:, :, span], act_v.at[:, :, span])
-    begin(lengths, len_s)
+
+    def store(part, lanes):
+        token = lax.broadcasted_iota(jnp.int32, (seq_len, rank), 0)
+        for e in range(examples):
+            rows = slice(e * seq_len, (e + 1) * seq_len)
+            sketch[rows, lanes] = jnp.where(token < len_s[e], part[rows], 0.0)
 
     def stage(n):
-        copies[2 * n].wait()
+        if n == 0:
+            copies[0].wait()
+            count = sum(len_s[e] for e in range(examples))
+            live[...] = jnp.full(live.shape, count.astype(jnp.float32))
         copies[2 * n + 1].wait()
+        copies[2 * n + 2].wait()
         if n == 0:
-            out_v[...] = dot_nt(grad_v[...].reshape(tokens, -1), pout_v[...])
+            store(dot_nt(grad_v[...].reshape(tokens, -1), pout_v[...]), slice(0, rank))
             return
         span = pl.ds((n - 1) * width, width)
         in_part = dot_nt(act_v[:, :, span].reshape(tokens, width), pin_v[:, span])
@@ -55,16 +65,8 @@
             in_part += in_v[...]
         if n < stages - 1:
             in_v[...] = in_part
-            return
-        both = jnp.concatenate([out_v[...], in_part], axis=1)
-        token = lax.broadcasted_iota(jnp.int32, (seq_len, 2 * rank), 0)
-        copies[-1].wait()
-        count = jnp.int32(0)
-        for e in range(examples):
-            rows = pl.ds(e * seq_len, seq_len)
-            sketch[rows] = jnp.where(token < len_s[e], both[e * seq_len : (e + 1) * seq_len], 0.0)
-            count += len_s[e]
-        live[...] = jnp.full(live.shape, count.astype(jnp.float32))
+        else:
+            store(in_part, slice(rank, 2 * rank))
 
     @pl.loop(0, stages)
     def _(turn):
@@ -257,7 +259,7 @@
         out_specs=[VMEM] * 2,
         scratch_shapes=[pltpu.SMEM(lengths.shape, jnp.int32)]
         + [pltpu.VMEM(operand.shape, jnp.bfloat16) for operand in operands[1:]]
-        + [pltpu.VMEM((examples * seq_len, rank), jnp.float32)] * 2
+        + [pltpu.VMEM((examples * seq_len, rank), jnp.float32)]
         + [pltpu.SemaphoreType.DMA((2 * stages + 2,))],
         compiler_params=pltpu.CompilerParams(vmem_limit_bytes=24 * 2**20),
         name="project",

time: 22.2 us -> 22.2 us (level); the launches traced: 22.3 us -> 21.9 us
  starting transfers between devices: 9.08 us -> 8.69 us
    ppermute x2, starting transfers between devices: 2.12 us -> 1.73 us  [across(): return lax.ppermute(x, 'tensor', [(t, t ^ 1) for t in range(tensor)])]
where the time goes in v11:
time: 22.2 us; the launch traced here: 21.9 us
  starting transfers between devices  8.69 us (39%)
  waiting for transfers between devices  8.48 us (38%)
  Pallas kernels  4.66 us (21%)
    ppermute x4, waiting for transfers between devices, swap(): return lax.ppermute(x, ('dp', 'tensor'), pairs)  7.25 us
    ppermute x4, starting transfers between devices, swap(): return lax.ppermute(x, ('dp', 'tensor'), pairs)  6.96 us
    pallas_call x1, Pallas kernels, project(): pl.pallas_call(project_kernel, out_shape=[shape(examples * seq_len, 2 * r...  3.52 us
    ppermute x2, starting transfers between devices, across(): return lax.ppermute(x, 'tensor', [(t, t ^ 1) for t in range(tensor)])  1.73 us
    ppermute x2, waiting for transfers between devices, across(): return lax.ppermute(x, 'tensor', [(t, t ^ 1) for t in range(tensor)])  1.23 us
    pallas_call x1, Pallas kernels, publish(): pl.pallas_call(publish_kernel, out_shape=jax.ShapeDtypeStruct(scores.shap...  0.57 us
    pallas_call x1, Pallas kernels, replace(): pl.pallas_call(functools.partial(replace_kernel, leads), out_shape=jax.Sh...  0.57 us
  transfers between devices with their start and end apart: 6, of which 5 were waited for; matrix products, arithmetic and copies ran while one was open for 0% of the time, Pallas kernels for 3%

profile of v11, /device:TPU:0, one launch (start us, length us, event | category | flops | bytes accessed | tf_op | source)
XLA Modules:
  0.0 21.9 jit_solution(1813340627842639038)
XLA Ops:
  0.0 0.0 copy-start
  0.0 3.5 %project.1 = (f32[256,128]{1,0:T(8,128)S(1)}, f32[8,128]{1,0:T(8,128)S(1)}) custom-call(s32[2]{0:T(128)} %lengths.1, bf16[2,128,7168]{2,1,0:T(8,128)(2,1)} %act.1, bf16[2,128,2048]{2,1,0:T(8,128)(2,1)} %grad.1, bf16[64,7168]{1,0:T(8,128)(2,1)} %bitcast.5, bf16[64,2048]{1,0:T(8,128)(2,1)} %bitcast.6), custom_call_target="tpu_custom_call" | custom-call | tf_op jit(solution)/shard_map/project/pallas_call | solution.py:255
  3.5 0.5 %collective-permute-start = (f32[256,128]{1,0:T(8,128)S(1)}, f32[256,128]{1,0:T(8,128)S(1)}, u32[]{:S(2)}, u32[]{:S(2)}) collective-permute-start(f32[256,128]{1,0:T(8,128)S(1)} %get-tuple-element.8), channel_id=1, source_target_pairs={{0,1},{1,0},{2,3},{3,2},{4,5},{5,4},{6,7},{7,6},{8,9},{9,8},{10,11... | collective-permute-start | bytes 393224 | tf_op jit(solution)/shard_map/ppermute | solution.py:279
  4.0 1.0 %collective-permute-done = f32[256,128]{1,0:T(8,128)S(1)} collective-permute-done((f32[256,128]{1,0:T(8,128)S(1)}, f32[256,128]{1,0:T(8,128)S(1)}, u32[]{:S(2)}, u32[]{:S(2)}) %collective-permute-start) | collective-permute-done | bytes 131104 | tf_op jit(solution)/shard_map/ppermute | solution.py:279
  5.0 3.0 %collective-permute-start.1 = (f32[256,128]{1,0:T(8,128)S(1)}, f32[256,128]{1,0:T(8,128)S(1)}, u32[]{:S(2)}, u32[]{:S(2)}) collective-permute-start(f32[256,128]{1,0:T(8,128)S(1)} %add.3.mine), channel_id=1, source_target_pairs={{0,4},{1,3},{2,6},{3,1},{4,0},{5,7},{6,2},{7,5},{8,12},{9,11},{10,... | collective-permute-start | bytes 393224 | tf_op jit(solution)/shard_map/ppermute | solution.py:275
  8.0 2.9 %collective-permute-done.1.theirs = f32[256,128]{1,0:T(8,128)S(1)} collective-permute-done((f32[256,128]{1,0:T(8,128)S(1)}, f32[256,128]{1,0:T(8,128)S(1)}, u32[]{:S(2)}, u32[]{:S(2)}) %collective-permute-start.1) | collective-permute-done | bytes 131104 | tf_op jit(solution)/shard_map/ppermute | solution.py:275
  11.0 1.9 %collective-permute-start.2 = (f32[104,128]{1,0:T(8,128)S(1)}, f32[104,128]{1,0:T(8,128)S(1)}, u32[]{:S(2)}, u32[]{:S(2)}) collective-permute-start(f32[104,128]{1,0:T(8,128)S(1)} %gram.1.mine.refs_2_), channel_id=1, source_target_pairs={{0,2},{1,9},{2,0},{3,11},{4,6},{5,13},{6,4},{7,15},{8,10},{9,1},{1... | collective-permute-start | bytes 159752 | tf_op jit(solution)/shard_map/ppermute | solution.py:275
  12.9 0.1 collective-permute-start.4
  13.0 2.1 %collective-permute-done.2.theirs = f32[104,128]{1,0:T(8,128)S(1)} collective-permute-done((f32[104,128]{1,0:T(8,128)S(1)}, f32[104,128]{1,0:T(8,128)S(1)}, u32[]{:S(2)}, u32[]{:S(2)}) %collective-permute-start.2) | collective-permute-done | bytes 53280 | tf_op jit(solution)/shard_map/ppermute | solution.py:275
  15.1 1.9 %collective-permute-start.3 = (f32[104,128]{1,0:T(8,128)S(1)}, f32[104,128]{1,0:T(8,128)S(1)}, u32[]{:S(2)}, u32[]{:S(2)}) collective-permute-start(f32[104,128]{1,0:T(8,128)S(1)} %merge.1.refs_0_), channel_id=1, source_target_pairs={{0,2},{1,5},{2,0},{3,7},{4,6},{5,1},{6,4},{7,3},{8,10},{9,13},{10,... | collective-permute-start | bytes 159752 | tf_op jit(solution)/shard_map/ppermute | solution.py:275
  17.1 0.0 collective-permute-done.4.refs_3_
  17.1 2.2 %collective-permute-done.3.refs_1_ = f32[104,128]{1,0:T(8,128)S(1)} collective-permute-done((f32[104,128]{1,0:T(8,128)S(1)}, f32[104,128]{1,0:T(8,128)S(1)}, u32[]{:S(2)}, u32[]{:S(2)}) %collective-permute-start.3) | collective-permute-done | bytes 53280 | tf_op jit(solution)/shard_map/ppermute | solution.py:275
  19.3 0.0 copy-done
  19.3 1.2 %collective-permute-start.5 = (f32[2,64]{1,0:T(2,128)S(1)}, f32[2,64]{1,0:T(2,128)S(1)}, u32[]{:S(2)}, u32[]{:S(2)}) collective-permute-start(f32[2,64]{1,0:T(2,128)S(1)} %finish.1.scores), channel_id=1, source_target_pairs={{0,1},{1,0},{2,3},{3,2},{4,5},{5,4},{6,7},{7,6},{8,9},{9,8},{10,11... | collective-permute-start | bytes 1544 | tf_op jit(solution)/shard_map/ppermute | solution.py:279
  20.5 0.6 %publish.1.mine = f32[2,64]{1,0:T(2,128)} custom-call(f32[2,64]{1,0:T(2,128)S(1)} %finish.1.scores), custom_call_target="tpu_custom_call" | custom-call | flops 1000000000 | tf_op jit(solution)/shard_map/publish/pallas_call | solution.py:283
  21.1 0.2 %collective-permute-done.5.theirs = f32[2,64]{1,0:T(2,128)S(1)} collective-permute-done((f32[2,64]{1,0:T(2,128)S(1)}, f32[2,64]{1,0:T(2,128)S(1)}, u32[]{:S(2)}, u32[]{:S(2)}) %collective-permute-start.5) | collective-permute-done | bytes 544 | tf_op jit(solution)/shard_map/ppermute | solution.py:279
  21.3 0.6 %replace.1 = f32[2,64]{1,0:T(2,128)} custom-call(f32[2,64]{1,0:T(2,128)S(1)} %collective-permute-done.5.theirs, f32[2,64]{1,0:T(2,128)} %publish.1.mine), custom_call_target="tpu_custom_call", output_to_operand_aliasing={{}: (1, {})} | custom-call | tf_op jit(solution)/shard_map/replace/pallas_call | solution.py:296
  (4 shorter events, 0.0 us)
Async XLA Ops:
  0.0 19.3 %copy-start = (s32[64]{0:T(128)S(1)}, s32[64]{0:T(128)}, u32[]{:S(2)}) copy-start(s32[64]{0:T(128)} %param.11) | copy-start | bytes 772
  3.5 1.5 %collective-permute-start = (f32[256,128]{1,0:T(8,128)S(1)}, f32[256,128]{1,0:T(8,128)S(1)}, u32[]{:S(2)}, u32[]{:S(2)}) collective-permute-start(f32[256,128]{1,0:T(8,128)S(1)} %get-tuple-element.8), channel_id=1, source_target_pairs={{0,1},{1,0},{2,3},{3,2},{4,5},{5,4},{6,7},{7,6},{8,9},{9,8},{10,11... | collective-permute-start | bytes 393224 | tf_op jit(solution)/shard_map/ppermute | solution.py:279
  5.0 5.9 %collective-permute-start.1 = (f32[256,128]{1,0:T(8,128)S(1)}, f32[256,128]{1,0:T(8,128)S(1)}, u32[]{:S(2)}, u32[]{:S(2)}) collective-permute-start(f32[256,128]{1,0:T(8,128)S(1)} %add.3.mine), channel_id=1, source_target_pairs={{0,4},{1,3},{2,6},{3,1},{4,0},{5,7},{6,2},{7,5},{8,12},{9,11},{10,... | collective-permute-start | bytes 393224 | tf_op jit(solution)/shard_map/ppermute | solution.py:275
  11.0 4.1 %collective-permute-start.2 = (f32[104,128]{1,0:T(8,128)S(1)}, f32[104,128]{1,0:T(8,128)S(1)}, u32[]{:S(2)}, u32[]{:S(2)}) collective-permute-start(f32[104,128]{1,0:T(8,128)S(1)} %gram.1.mine.refs_2_), channel_id=1, source_target_pairs={{0,2},{1,9},{2,0},{3,11},{4,6},{5,13},{6,4},{7,15},{8,10},{9,1},{1... | collective-permute-start | bytes 159752 | tf_op jit(solution)/shard_map/ppermute | solution.py:275
  12.9 4.1 %collective-permute-start.4 = (f32[104,128]{1,0:T(8,128)S(1)}, f32[104,128]{1,0:T(8,128)S(1)}, u32[]{:S(2)}, u32[]{:S(2)}) collective-permute-start(f32[104,128]{1,0:T(8,128)S(1)} %gram.1.mine.refs_2_), channel_id=1, source_target_pairs={{0,2},{1,5},{2,0},{3,7},{4,6},{5,1},{6,4},{7,3},{8,10},{9,13},{10,... | collective-permute-start | bytes 159752 | tf_op jit(solution)/shard_map/ppermute | solution.py:275
  15.1 4.1 %collective-permute-start.3 = (f32[104,128]{1,0:T(8,128)S(1)}, f32[104,128]{1,0:T(8,128)S(1)}, u32[]{:S(2)}, u32[]{:S(2)}) collective-permute-start(f32[104,128]{1,0:T(8,128)S(1)} %merge.1.refs_0_), channel_id=1, source_target_pairs={{0,2},{1,5},{2,0},{3,7},{4,6},{5,1},{6,4},{7,3},{8,10},{9,13},{10,... | collective-permute-start | bytes 159752 | tf_op jit(solution)/shard_map/ppermute | solution.py:275
  19.3 2.0 %collective-permute-start.5 = (f32[2,64]{1,0:T(2,128)S(1)}, f32[2,64]{1,0:T(2,128)S(1)}, u32[]{:S(2)}, u32[]{:S(2)}) collective-permute-start(f32[2,64]{1,0:T(2,128)S(1)} %finish.1.scores), channel_id=1, source_target_pairs={{0,1},{1,0},{2,3},{3,2},{4,5},{5,4},{6,7},{7,6},{8,9},{9,8},{10,11... | collective-permute-start | bytes 1544 | tf_op jit(solution)/shard_map/ppermute | solution.py:279
